TPU v7x, 32 devices: a whole 2x2x4 slice. The times are simulated.
32 devices in a mesh: wide: 8 (over y, x, core), narrow: 4 (over z).
Axes of the slice: x: 2, y: 2, z: 4, core: 2. Of those that a mesh axis runs over, the one named last changes fastest.
Arguments:
- tokens: bfloat16 [98304, 768], P(('wide', 'narrow')), may hold values from -6 to 6
- cotangent: bfloat16 [98304, 768], P(('wide', 'narrow')), may hold values from -6 to 6
- segments: int32 [96, 1024], P(('wide', 'narrow')), may hold values from 0 to 7, never falling along the last dimension, each value on 1 to 512 neighbouring positions
- picks: int32 [96, 128], P(('wide', 'narrow')), may hold values from 0 to 1023, as said below
- w_qkv: float32 [768, 2304], P(('wide', 'narrow')), may hold values from -0.21875 to 0.21875
- w_out: float32 [768, 768], P(('wide', 'narrow')), may hold values from -0.625 to 0.625
- w_up: float32 [768, 3072], P(('wide', 'narrow')), may hold values from -0.21875 to 0.21875
- w_down: float32 [3072, 768], P(('wide', 'narrow')), may hold values from -0.109375 to 0.109375
- vectors: float32 [3, 768], P(None, ('wide', 'narrow')), may hold values from -1 to 2.5
- m_qkv: float32 [768, 2304], P(('wide', 'narrow')), may hold values from -0.75 to 0.75
- m_out: float32 [768, 768], P(('wide', 'narrow')), may hold values from -0.75 to 0.75
- m_up: float32 [768, 3072], P(('wide', 'narrow')), may hold values from -0.75 to 0.75
- m_down: float32 [3072, 768], P(('wide', 'narrow')), may hold values from -0.75 to 0.75
- m_vectors: float32 [3, 768], P(None, ('wide', 'narrow')), may hold values from -0.75 to 0.75
- v_qkv: float32 [768, 2304], P(('wide', 'narrow')), may hold values from 0.0012288 to 0.0049152
- v_out: float32 [768, 768], P(('wide', 'narrow')), may hold values from 0.0012288 to 0.0049152
- v_up: float32 [768, 3072], P(('wide', 'narrow')), may hold values from 0.0012288 to 0.0049152
- v_down: float32 [3072, 768], P(('wide', 'narrow')), may hold values from 0.0012288 to 0.0049152
- v_vectors: float32 [3, 768], P(None, ('wide', 'narrow')), may hold values from 0.24576 to 0.98304
Outputs:
- mixed: bfloat16 [98304, 768], P(('wide', 'narrow'))
- input_grad: bfloat16 [98304, 768], P(('wide', 'narrow'))
- grad_norm: float32 [], replicated
- new_qkv: float32 [768, 2304], P(('wide', 'narrow'))
- new_out: float32 [768, 768], P(('wide', 'narrow'))
- new_up: float32 [768, 3072], P(('wide', 'narrow'))
- new_down: float32 [3072, 768], P(('wide', 'narrow'))
- first_qkv: float32 [768, 2304], P(('wide', 'narrow'))
- first_out: float32 [768, 768], P(('wide', 'narrow'))
- first_up: float32 [768, 3072], P(('wide', 'narrow'))
- first_down: float32 [3072, 768], P(('wide', 'narrow'))
- first_vectors: float32 [3, 768], P(None, ('wide', 'narrow'))
- second_qkv: float32 [768, 2304], P(('wide', 'narrow'))
- second_out: float32 [768, 768], P(('wide', 'narrow'))
- second_up: float32 [768, 3072], P(('wide', 'narrow'))
- second_down: float32 [3072, 768], P(('wide', 'narrow'))
- second_vectors: float32 [3, 768], P(None, ('wide', 'narrow'))
Inputs may be any that keep to these rules, and one draw needn't show every extreme that they name: `picks`: each row holds 128 distinct positions of its sequence in rising order.
All inputs are finite; a program needn't handle non-finite values.
Results may differ from a plain program's by a relative error of at most 0.012.
The roundings to bfloat16 on the way count: a program that leaves them out, or rounds other values in their place, can miss the bound.
Values may be sent and summed in bfloat16 or wider, within the bound.
No kernel may reach another device: no remote copies, remote signals or barrier semaphores. Data moves between devices by JAX's collectives and lax.ppermute only.
A program may use at most 192 MiB of HBM per device.

v0:
```python
import math

import jax
import jax.numpy as jnp
from jax import lax
from jax.sharding import PartitionSpec as P

HEAD_DIM = 64


norm_eps = 1e-06
beta_one = 0.9
beta_two = 0.999
adam_eps = 1e-08
learn_rate = 0.03
decay_rate = 0.1
adam_step = 10
limit_scale = 0.01
masked_out = -1e30


def rms_scale(inputs, gain):
    inverse = lax.rsqrt(jnp.mean(inputs * inputs, axis=-1, keepdims=True) + norm_eps)
    return inputs * inverse * gain


def gelu_tanh(inputs):
    return jax.nn.gelu(inputs, approximate=True)


def contract_rows(left, right):
    return lax.dot_general(
        left, right, (((0,), (0,)), ((), ())), preferred_element_type=jnp.float32
    )


def contract_cols(left, right):
    return lax.dot_general(
        left, right, (((1,), (1,)), ((), ())), preferred_element_type=jnp.float32
    )


def keep_pair(pair):
    return pair


def routed_forward(picked, allowed, weight_set):
    w_qkv, w_out, w_up, w_down, vectors = weight_set
    gain_rows = vectors.astype(jnp.float32)
    row_count, model_width = picked.shape
    head_count = model_width // HEAD_DIM
    normed = rms_scale(picked, gain_rows[0]).astype(jnp.bfloat16)
    projected = jnp.dot(normed, w_qkv, preferred_element_type=jnp.float32).astype(jnp.bfloat16)
    split_heads = projected.reshape(row_count, 3, head_count, HEAD_DIM)
    queries = split_heads[:, 0]
    keys_all = split_heads[:, 1]
    value_rows = split_heads[:, 2]
    scores = jnp.einsum(
        "qhd,khd->hqk", queries, keys_all, preferred_element_type=jnp.float32
    ) * HEAD_DIM ** (-0.5)
    scores = jnp.where(allowed[None], scores, masked_out)
    top_score = jnp.max(scores, axis=-1, keepdims=True)
    log_total = top_score + jnp.log(jnp.sum(jnp.exp(scores - top_score), axis=-1, keepdims=True))
    soft_probs = jnp.exp(scores - log_total)
    probs_low = soft_probs.astype(jnp.bfloat16)
    attended = jnp.einsum("hqk,khd->qhd", probs_low, value_rows, preferred_element_type=jnp.float32)
    attended = attended.reshape(row_count, model_width).astype(jnp.bfloat16)
    attn_out = jnp.dot(attended, w_out, preferred_element_type=jnp.float32)
    middle = picked + attn_out
    normed_two = rms_scale(middle, gain_rows[1]).astype(jnp.bfloat16)
    up_proj = jnp.dot(normed_two, w_up, preferred_element_type=jnp.float32)
    hidden = gelu_tanh(up_proj).astype(jnp.bfloat16)
    mlp_out = jnp.dot(hidden, w_down, preferred_element_type=jnp.float32)
    router_logit = jnp.sum(picked * gain_rows[2], axis=-1)
    gating = jax.nn.sigmoid(router_logit)
    branch_add = gating[:, None] * (attn_out + mlp_out)
    saved = (
        normed,
        split_heads,
        soft_probs,
        probs_low,
        attended,
        attn_out,
        middle,
        normed_two,
        up_proj,
        hidden,
        mlp_out,
        gating,
    )
    return (branch_add, saved)


def routed_backward(picked, weight_set, saved, back_rows, send_mlp):
    w_qkv, w_out, w_up, w_down, vectors = weight_set
    gain_rows = vectors.astype(jnp.float32)
    (
        normed,
        split_heads,
        soft_probs,
        probs_low,
        attended,
        attn_out,
        middle,
        normed_two,
        up_proj,
        hidden,
        mlp_out,
        gating,
    ) = saved
    row_count, model_width = picked.shape
    head_scale = HEAD_DIM ** (-0.5)
    queries = split_heads[:, 0]
    keys_all = split_heads[:, 1]
    value_rows = split_heads[:, 2]
    gate_grad = jnp.sum(back_rows * (attn_out + mlp_out), axis=-1)
    logit_grad = gate_grad * gating * (1.0 - gating)
    branch_grad = gating[:, None] * back_rows
    mlp_low = branch_grad.astype(jnp.bfloat16)
    grad_down = contract_rows(hidden, mlp_low)
    hidden_grad = contract_cols(mlp_low, w_down)
    up_grad = jax.vjp(gelu_tanh, up_proj)[1](hidden_grad)[0].astype(jnp.bfloat16)
    grad_up = contract_rows(normed_two, up_grad)
    mlp_part = send_mlp((grad_up, grad_down))
    normed_two_grad = contract_cols(up_grad, w_up)
    middle_grad, gain_two_grad = jax.vjp(rms_scale, middle, gain_rows[1])[1](normed_two_grad)
    attn_grad = (branch_grad + middle_grad).astype(jnp.bfloat16)
    grad_out = contract_rows(attended, attn_grad)
    attended_grad = (
        contract_cols(attn_grad, w_out).astype(jnp.bfloat16).reshape(row_count, -1, HEAD_DIM)
    )
    value_grad = jnp.einsum(
        "hqk,qhd->khd", probs_low, attended_grad, preferred_element_type=jnp.float32
    )
    probs_grad = jnp.einsum(
        "qhd,khd->hqk", attended_grad, value_rows, preferred_element_type=jnp.float32
    )
    score_grad = soft_probs * (
        probs_grad - jnp.sum(probs_grad * soft_probs, axis=-1, keepdims=True)
    )
    score_low = score_grad.astype(jnp.bfloat16)
    query_grad = (
        jnp.einsum("hqk,khd->qhd", score_low, keys_all, preferred_element_type=jnp.float32)
        * head_scale
    )
    key_grad = (
        jnp.einsum("hqk,qhd->khd", score_low, queries, preferred_element_type=jnp.float32)
        * head_scale
    )
    qkv_grad = (
        jnp.stack([query_grad, key_grad, value_grad], axis=1)
        .reshape(row_count, 3 * model_width)
        .astype(jnp.bfloat16)
    )
    grad_qkv = contract_rows(normed, qkv_grad)
    normed_grad = contract_cols(qkv_grad, w_qkv)
    norm_rows_grad, gain_one_grad = jax.vjp(rms_scale, picked, gain_rows[0])[1](normed_grad)
    router_grad = jnp.sum(logit_grad[:, None] * picked, axis=0)
    picked_grad = back_rows + middle_grad + norm_rows_grad + logit_grad[:, None] * gain_rows[2]
    grad_vectors = jnp.stack([gain_one_grad, gain_two_grad, router_grad], axis=0)
    return (picked_grad, (grad_qkv, grad_out, grad_vectors), mlp_part)


def moment_update(grad_part, first, second):
    first_new = beta_one * first + (1.0 - beta_one) * grad_part
    second_new = beta_two * second + (1.0 - beta_two) * grad_part * grad_part
    return (first_new, second_new)


def adam_update(master, grad_part, first, second):
    first_new, second_new = moment_update(grad_part, first, second)
    first_hat = first_new / (1.0 - beta_one**adam_step)
    second_hat = second_new / (1.0 - beta_two**adam_step)
    master_new = master - learn_rate * (
        first_hat / (jnp.sqrt(second_hat) + adam_eps) + decay_rate * master
    )
    return (master_new, first_new, second_new)


def per_device(
    tokens,
    cotangent,
    segments,
    picks,
    w_qkv,
    w_out,
    w_up,
    w_down,
    vectors,
    m_qkv,
    m_out,
    m_up,
    m_down,
    m_vectors,
    v_qkv,
    v_out,
    v_up,
    v_down,
    v_vectors,
):
    masters = (w_qkv, w_out, w_up, w_down, vectors)
    low_masters = tuple((master.astype(jnp.bfloat16) for master in masters))
    gathered = (
        lax.all_gather(low_masters[0], ("wide", "narrow"), axis=0, tiled=True),
        lax.all_gather(low_masters[1], ("wide", "narrow"), axis=0, tiled=True),
        lax.all_gather(low_masters[2], ("wide", "narrow"), axis=0, tiled=True),
        lax.all_gather(low_masters[3], ("wide", "narrow"), axis=0, tiled=True),
        lax.all_gather(low_masters[4], ("wide", "narrow"), axis=1, tiled=True),
    )
    seq_count, top_count = picks.shape
    seq_len = segments.shape[1]
    model_width = tokens.shape[1]
    seq_index = jnp.arange(seq_count, dtype=jnp.int32)[:, None]
    tok_blocks = tokens.reshape(seq_count, seq_len, model_width)
    picked = tok_blocks[seq_index, picks].reshape(-1, model_width).astype(jnp.float32)
    seg_sel = segments[seq_index, picks].reshape(-1)
    positions = picks.reshape(-1)
    row_seq = jnp.repeat(jnp.arange(seq_count, dtype=jnp.int32), top_count)
    allowed = (
        (row_seq[:, None] == row_seq[None, :])
        & (seg_sel[:, None] == seg_sel[None, :])
        & (positions[None, :] <= positions[:, None])
    )
    branch_add, saved = routed_forward(picked, allowed, gathered)
    new_rows = (picked + branch_add).astype(jnp.bfloat16).reshape(seq_count, top_count, model_width)
    mixed_rows = tok_blocks.at[seq_index, picks].set(new_rows).reshape(tokens.shape)
    back_blocks = cotangent.reshape(seq_count, seq_len, model_width)
    back_rows = back_blocks[seq_index, picks].reshape(-1, model_width).astype(jnp.float32)
    back_weights = (
        lax.all_gather(low_masters[0], ("wide", "narrow"), axis=0, tiled=True),
        lax.all_gather(low_masters[1], ("wide", "narrow"), axis=0, tiled=True),
        lax.all_gather(low_masters[2], ("wide", "narrow"), axis=0, tiled=True),
        lax.all_gather(low_masters[3], ("wide", "narrow"), axis=0, tiled=True),
        lax.all_gather(low_masters[4], ("wide", "narrow"), axis=1, tiled=True),
    )
    recomputed = routed_forward(picked, allowed, back_weights)[1]
    picked_grad, attn_parts, mlp_parts = routed_backward(
        picked, back_weights, recomputed, back_rows, keep_pair
    )
    grad_shards = (
        lax.psum_scatter(attn_parts[0], ("wide", "narrow"), scatter_dimension=0, tiled=True),
        lax.psum_scatter(attn_parts[1], ("wide", "narrow"), scatter_dimension=0, tiled=True),
        lax.psum_scatter(mlp_parts[0], ("wide", "narrow"), scatter_dimension=0, tiled=True),
        lax.psum_scatter(mlp_parts[1], ("wide", "narrow"), scatter_dimension=0, tiled=True),
        lax.psum_scatter(attn_parts[2], ("wide", "narrow"), scatter_dimension=1, tiled=True),
    )
    grad_rows = picked_grad.astype(jnp.bfloat16).reshape(seq_count, top_count, model_width)
    input_grad = back_blocks.at[seq_index, picks].set(grad_rows).reshape(cotangent.shape)
    local_sq = jnp.sum(jnp.stack([jnp.sum(grad_shard * grad_shard) for grad_shard in grad_shards]))
    total_sq = lax.psum(local_sq, ("wide", "narrow"))
    grad_norm = jnp.sqrt(total_sq)
    devices_all = lax.axis_size("wide") * lax.axis_size("narrow")
    ff_width = w_up.shape[1]
    params_all = 4 * model_width * model_width + 2 * model_width * ff_width + 3 * model_width
    selected_all = seq_count * top_count * devices_all
    clip_limit = limit_scale * math.sqrt(params_all * selected_all)
    factor = jnp.minimum(1.0, clip_limit / (grad_norm + 1e-06))
    firsts = (m_qkv, m_out, m_up, m_down)
    seconds = (v_qkv, v_out, v_up, v_down)
    results = [
        adam_update(masters[index], grad_shards[index] * factor, firsts[index], seconds[index])
        for index in range(4)
    ]
    first_vec, second_vec = moment_update(grad_shards[4] * factor, m_vectors, v_vectors)
    return (
        mixed_rows,
        input_grad,
        grad_norm,
        results[0][0],
        results[1][0],
        results[2][0],
        results[3][0],
        results[0][1],
        results[1][1],
        results[2][1],
        results[3][1],
        first_vec,
        results[0][2],
        results[1][2],
        results[2][2],
        results[3][2],
        second_vec,
    )


def solution(mesh):
    placed = (
        P(("wide", "narrow"), None),
        P(("wide", "narrow"), None),
        P(("wide", "narrow"), None),
        P(("wide", "narrow"), None),
        P(("wide", "narrow"), None),
        P(("wide", "narrow"), None),
        P(("wide", "narrow"), None),
        P(("wide", "narrow"), None),
        P(None, ("wide", "narrow")),
        P(("wide", "narrow"), None),
        P(("wide", "narrow"), None),
        P(("wide", "narrow"), None),
        P(("wide", "narrow"), None),
        P(None, ("wide", "narrow")),
        P(("wide", "narrow"), None),
        P(("wide", "narrow"), None),
        P(("wide", "narrow"), None),
        P(("wide", "narrow"), None),
        P(None, ("wide", "narrow")),
    )
    return jax.shard_map(
        per_device,
        mesh=mesh,
        in_specs=placed,
        out_specs=(
            P(("wide", "narrow"), None),
            P(("wide", "narrow"), None),
            P(),
            P(("wide", "narrow"), None),
            P(("wide", "narrow"), None),
            P(("wide", "narrow"), None),
            P(("wide", "narrow"), None),
            P(("wide", "narrow"), None),
            P(("wide", "narrow"), None),
            P(("wide", "narrow"), None),
            P(("wide", "narrow"), None),
            P(None, ("wide", "narrow")),
            P(("wide", "narrow"), None),
            P(("wide", "narrow"), None),
            P(("wide", "narrow"), None),
            P(("wide", "narrow"), None),
            P(None, ("wide", "narrow")),
        ),
        check_vma=False,
    )
```

profile of v0, /device:TPU:0, one launch (start us, length us, event | category | flops | bytes accessed | tf_op | source)
XLA Modules:
  0.0 908.1 jit_solution(4113294113755812110)
XLA Ops:
  7.3 5.0 copy.77
  12.3 2.2 copy.78
  17.5 69.9 %all-gather = bf16[32,24,3]{1,2,0:T(4,128)(2,1)S(1)} all-gather(bf16[1,24,3]{1,2,0:T(4,128)(2,1)S(1)} %convert_bitcast_fusion), channel_id=1, replica_groups=mesh['wide'=8,'narrow'=4] {'wide','narrow'}, dimensions={0}, use_global_device_ids=true | all-gather | bytes 4752 | tf_op jit(solution)/shard_map/all_gather | solution.py:208
  87.7 3.7 gather_fusion.1
  91.4 10.1 %gather_fusion = bf16[384,768]{1,0:T(8,128)(2,1)S(1)} fusion(bf16[3,1024,768]{2,1,0:T(8,128)(2,1)} %bitcast.111, s32[384]{0:T(512)S(1)} %get-tuple-element.48), kind=kCustom, calls=%fused_computation | custom fusion | bytes 1182720 | tf_op jit(solution)/shard_map/gather | solution.py:215
  101.5 11.3 %gather_fusion.2 = bf16[384,768]{1,0:T(8,128)(2,1)} fusion(bf16[3,1024,768]{2,1,0:T(8,128)(2,1)} %bitcast.108, s32[384]{0:T(512)S(1)} %get-tuple-element.48), kind=kCustom, calls=%fused_computation.2 | custom fusion | bytes 1182720 | tf_op jit(solution)/shard_map/gather | solution.py:228
  114.4 4.8 convolution_convert_fusion
  119.2 2.9 copy.61
  122.2 1.3 fusion
  123.4 1.5 exponential_reduce_fusion
  124.9 1.4 copy-done.2
  126.3 2.9 convolution_convert_fusion.2
  129.2 5.3 all-gather.8.cloned.1.call-done
  134.5 3.3 multiply_reduce_fusion.4
  137.8 62.6 %all-gather.10.cloned.1.call-done = bf16[768,3072]{1,0:T(8,128)(2,1)} async-done(((bf16[24,3072]{1,0:T(8,128)(2,1)}), bf16[768,3072]{1,0:T(8,128)(2,1)}) %all-gather.10.cloned.1.call-update) | async-done | bytes 4718608 | tf_op jit(solution)/shard_map/all_gather | solution.py:206
  200.5 6.6 fusion.56
  207.1 59.0 %all-gather.12.cloned.1.call-done = bf16[3072,768]{1,0:T(8,128)(2,1)} async-done(((bf16[96,768]{1,0:T(8,128)(2,1)}), bf16[3072,768]{1,0:T(8,128)(2,1)}) %all-gather.12.cloned.1.call-update) | async-done | bytes 4718608 | tf_op jit(solution)/shard_map/all_gather | solution.py:207
  266.1 8.2 fusion.7
  274.3 2.4 multiply_reduce_fusion.2
  276.8 1.8 copy-done.36
  278.6 1.3 copy-done.37
  280.0 4.3 fusion.23
  285.1 2.2 fusion.62
  287.3 2.9 convolution_convert_fusion.1
  290.2 2.1 copy.63
  292.4 5.7 multiply_reduce_fusion
  298.1 2.0 multiply_convert_fusion
  300.1 1.4 fusion.13
  302.6 2.0 convolution_bitcast_fusion
  304.8 1.3 copy-done.8
  306.4 4.9 fusion.61
  311.4 7.2 fusion.55
  319.6 9.0 fusion.31
  329.7 5.3 fusion.17
  335.1 52.5 %scatter_fusion = bf16[3,1024,768]{2,1,0:T(8,128)(2,1)} fusion(bf16[3,1024,768]{2,1,0:T(8,128)(2,1)} %bitcast.112, s32[384]{0:T(512)S(1)} %get-tuple-element.49, bf16[384,768]{1,0:T(8,128)(2,1)S(1)} %copy-done.24), kind=kCustom, calls=%fused_computation.3 | custom fusion | bytes 1772544 | tf_op jit(solution)/shard_map/scatter | solution.py:226
  387.7 39.8 %all-reduce = f32[3,768]{1,0:T(4,128)S(1)} all-reduce(f32[3,768]{1,0:T(4,128)S(1)} %pad_maximum_fusion), channel_id=6, replica_groups=mesh['wide'=8,'narrow'=4] {'wide','narrow'}, use_global_device_ids=true, to_apply=%region_22.23.clone | all-reduce | flops 2304 | bytes 18432
  428.1 2.4 fusion.22
  430.6 1.5 multiply_reduce_fusion.10
  432.1 82.8 %reduce-scatter.6.cloned.1.call-done = f32[24,2304]{1,0:T(8,128)} async-done(((f32[768,2304]{1,0:T(8,128)}), f32[24,2304]{1,0:T(8,128)}) %reduce-scatter.6.cloned.1.call-update) | async-done | bytes 221200 | tf_op jit(solution)/shard_map/reduce_scatter | solution.py:241
  514.9 1.6 multiply_reduce_fusion.9
  517.8 137.9 %reduce-scatter.10.cloned.1.call-done = f32[24,3072]{1,0:T(8,128)} async-done(((f32[768,3072]{1,0:T(8,128)}), f32[24,3072]{1,0:T(8,128)}) %reduce-scatter.10.cloned.1.call-update) | async-done | bytes 294928 | tf_op jit(solution)/shard_map/reduce_scatter | solution.py:243
  655.7 1.6 multiply_reduce_fusion.8
  658.0 139.2 %reduce-scatter.12.cloned.1.call-done = f32[96,768]{1,0:T(8,128)} async-done(((f32[3072,768]{1,0:T(8,128)}), f32[96,768]{1,0:T(8,128)}) %reduce-scatter.12.cloned.1.call-update) | async-done | bytes 294928 | tf_op jit(solution)/shard_map/reduce_scatter | solution.py:244
  797.2 1.6 multiply_reduce_fusion.7
  800.2 52.6 %scatter_fusion.1 = bf16[3,1024,768]{2,1,0:T(8,128)(2,1)} fusion(bf16[3,1024,768]{2,1,0:T(8,128)(2,1)} %bitcast.109, s32[384]{0:T(512)S(1)} %get-tuple-element.49, bf16[384,768]{1,0:T(8,128)(2,1)S(1)} %fusion.22), kind=kCustom, calls=%fused_computation.4 | custom fusion | bytes 1772544 | tf_op jit(solution)/shard_map/scatter | solution.py:248
  852.9 39.6 %psum.7 = f32[]{:T(128)} all-reduce(f32[]{:T(128)S(6)} %reduce_sum.222), channel_id=1, replica_groups=mesh['wide'=8,'narrow'=4] {'wide','narrow'}, use_global_device_ids=true, to_apply=%region_24.25 | all-reduce | flops 1 | bytes 8 | tf_op jit(solution)/shard_map/psum | solution.py:250
  893.9 1.7 multiply_subtract_fusion.3
  895.6 2.0 multiply_subtract_fusion.2
  (128 shorter events, 13.0 us)
Async XLA Ops:
  7.2 80.5 %copy-start = (s32[3,1024]{1,0:T(4,128)S(1)}, s32[3,1024]{1,0:T(4,128)}, u32[]{:S(2)}) copy-start(s32[3,1024]{1,0:T(4,128)} %param.21) | copy-start | bytes 36868
  7.2 107.2 %all-gather.6.cloned.1.call-start = ((), (), s32[]{:S(2)}) async-start(), calls=%async_computation.4 | async-start | bytes 3649536 | tf_op jit(solution)/shard_map/all_gather | solution.py:204
  7.3 5.0 copy-start.7
  12.2 2.2 copy-start.22
  12.2 3.0 copy-start.30
  12.2 3.7 copy-start.15
  12.3 4.5 copy-start.14
  12.3 5.2 copy-start.32
  12.3 75.4 %copy-start.31 = (s32[3,128]{1,0:T(4,128)S(1)}, s32[3,128]{1,0:T(4,128)}, u32[]{:S(2)}) copy-start(s32[3,128]{1,0:T(4,128)} %param.22) | copy-start | bytes 4612
  15.2 119.4 %all-gather.8.cloned.1.call-start = ((), (), s32[]{:S(2)}) async-start(), calls=%async_computation.5 | async-start | bytes 1216512 | tf_op jit(solution)/shard_map/all_gather | solution.py:205
  15.9 184.5 %all-gather.10.cloned.1.call-start = ((), (), s32[]{:S(2)}) async-start(), calls=%async_computation.6 | async-start | bytes 4866048 | tf_op jit(solution)/shard_map/all_gather | solution.py:206
  16.7 249.4 %all-gather.12.cloned.1.call-start = ((), (), s32[]{:S(2)}) async-start(), calls=%async_computation.7 | async-start | bytes 4866048 | tf_op jit(solution)/shard_map/all_gather | solution.py:207
  17.4 413.2 %reduce-scatter.8.cloned.1.call-start = ((), (), s32[]{:S(2)}) async-start(), calls=%async_computation.9 | async-start | bytes 2433024 | tf_op jit(solution)/shard_map/reduce_scatter | solution.py:242
  101.5 12.9 %copy-start.3 = (bf16[384,768]{1,0:T(8,128)(2,1)}, bf16[384,768]{1,0:T(8,128)(2,1)S(1)}, u32[]{:S(2)}) copy-start(bf16[384,768]{1,0:T(8,128)(2,1)S(1)} %gather_fusion) | copy-start | bytes 1769476
  123.4 2.9 copy-start.2
  266.1 8.2 copy-start.35
  274.3 2.5 copy-start.10
  274.3 2.5 copy-start.4
  274.3 2.5 copy-start.11
  274.3 2.5 copy-start.20
  274.3 4.3 copy-start.36
  274.3 5.6 copy-start.37
  276.8 7.5 copy-start.19
  280.0 5.1 copy-start.9
  284.3 0.8 copy-start.25
  292.3 222.6 %reduce-scatter.6.cloned.1.call-start = ((), (), s32[]{:S(2)}) async-start(), calls=%async_computation.8 | async-start | bytes 7299072 | tf_op jit(solution)/shard_map/reduce_scatter | solution.py:241
  292.4 5.7 slice-start
  292.4 5.7 slice-start.1
  301.5 1.1 copy-start.13
  304.5 1.6 copy-start.8
  304.8 1.6 copy-start.6
  311.3 344.4 %reduce-scatter.10.cloned.1.call-start = ((), (), s32[]{:S(2)}) async-start(), calls=%async_computation.10 | async-start | bytes 9732096 | tf_op jit(solution)/shard_map/reduce_scatter | solution.py:243
  318.6 1.1 copy-start.12
  318.6 478.6 %reduce-scatter.12.cloned.1.call-start = ((), (), s32[]{:S(2)}) async-start(), calls=%async_computation.11 | async-start | bytes 9732096 | tf_op jit(solution)/shard_map/reduce_scatter | solution.py:244
  328.7 1.1 copy-start.5
  329.7 5.4 copy-start.24
  800.2 93.1 %copy-start.33 = (f32[3,24]{1,0:T(4,128)S(1)}, f32[3,24]{1,0:T(4,128)}, u32[]{:S(2)}) copy-start(f32[3,24]{1,0:T(4,128)} %param.37) | copy-start | bytes 868
  800.2 93.1 %copy-start.34 = (f32[3,24]{1,0:T(4,128)S(1)}, f32[3,24]{1,0:T(4,128)}, u32[]{:S(2)}) copy-start(f32[3,24]{1,0:T(4,128)} %param.32) | copy-start | bytes 868
  800.2 95.4 %copy-start.21 = (f32[24,2304]{1,0:T(8,128)S(1)}, f32[24,2304]{1,0:T(8,128)}, u32[]{:S(2)}) copy-start(f32[24,2304]{1,0:T(8,128)} %reduce-scatter.6.cloned.1.call-done) | copy-start | bytes 663556
  800.2 95.4 %copy-start.23 = (f32[24,2304]{1,0:T(8,128)S(1)}, f32[24,2304]{1,0:T(8,128)}, u32[]{:S(2)}) copy-start(f32[24,2304]{1,0:T(8,128)} %param.23) | copy-start | bytes 663556
  800.2 97.4 %copy-start.18 = (f32[96,768]{1,0:T(8,128)S(1)}, f32[96,768]{1,0:T(8,128)}, u32[]{:S(2)}) copy-start(f32[96,768]{1,0:T(8,128)} %reduce-scatter.12.cloned.1.call-done) | copy-start | bytes 884740
  800.2 97.4 %copy-start.26 = (f32[96,768]{1,0:T(8,128)S(1)}, f32[96,768]{1,0:T(8,128)}, u32[]{:S(2)}) copy-start(f32[96,768]{1,0:T(8,128)} %param.31) | copy-start | bytes 884740
  800.2 97.4 %copy-start.27 = (f32[96,768]{1,0:T(8,128)S(1)}, f32[96,768]{1,0:T(8,128)}, u32[]{:S(2)}) copy-start(f32[96,768]{1,0:T(8,128)} %param.36) | copy-start | bytes 884740
  852.8 45.8 %copy-start.16 = (f32[24,3072]{1,0:T(8,128)S(1)}, f32[24,3072]{1,0:T(8,128)}, u32[]{:S(2)}) copy-start(f32[24,3072]{1,0:T(8,128)} %param.25) | copy-start | bytes 884740
  852.8 45.8 %copy-start.17 = (f32[24,3072]{1,0:T(8,128)S(1)}, f32[24,3072]{1,0:T(8,128)}, u32[]{:S(2)}) copy-start(f32[24,3072]{1,0:T(8,128)} %reduce-scatter.10.cloned.1.call-done) | copy-start | bytes 884740
  852.9 45.8 %copy-start.28 = (f32[24,3072]{1,0:T(8,128)S(1)}, f32[24,3072]{1,0:T(8,128)}, u32[]{:S(2)}) copy-start(f32[24,3072]{1,0:T(8,128)} %param.30) | copy-start | bytes 884740
  852.9 45.8 %copy-start.29 = (f32[24,3072]{1,0:T(8,128)S(1)}, f32[24,3072]{1,0:T(8,128)}, u32[]{:S(2)}) copy-start(f32[24,3072]{1,0:T(8,128)} %param.35) | copy-start | bytes 884740
  895.6 4.1 copy-start.1
Sparse Core Ops, SparseCore 0:
  15.3 62.9 all-gather.5
  81.6 52.8 all-gather.7
  137.9 62.4 all-gather.9
  203.7 62.3 all-gather.11
  292.5 97.8 reduce-scatter.7
  396.8 118.0 reduce-scatter.5
  520.8 134.8 reduce-scatter.9
  662.6 134.5 reduce-scatter.11
where the time goes:
time: 918 us; the launch traced here: 908 us
  waiting for transfers between devices  487 us (53%)
  local copies, waits for them, and re-layouts  152 us (17%)
  blocking collectives  149 us (16%)
  matrix products  75.2 us (8%)
  other arithmetic  24 us (3%)
  between operations  20.3 us (2%)
    reduce_scatter x1, waiting for transfers between devices, per_device(): lax.psum_scatter(mlp_parts[1], ('wide', 'narrow'), scatter_dimension=0, t...  139 us
    reduce_scatter x1, waiting for transfers between devices, per_device(): lax.psum_scatter(mlp_parts[0], ('wide', 'narrow'), scatter_dimension=0, t...  138 us
    reduce_scatter x1, waiting for transfers between devices, per_device(): lax.psum_scatter(attn_parts[0], ('wide', 'narrow'), scatter_dimension=0,...  82.8 us
    all_gather x1, blocking collectives, per_device(): lax.all_gather(low_masters[4], ('wide', 'narrow'), axis=1, tiled=True)  69.9 us
    all_gather x1, waiting for transfers between devices, per_device(): lax.all_gather(low_masters[2], ('wide', 'narrow'), axis=0, tiled=True)  62.6 us
    all_gather x1, waiting for transfers between devices, per_device(): lax.all_gather(low_masters[3], ('wide', 'narrow'), axis=0, tiled=True)  59 us
    scatter x1, local copies, waits for them, and re-layouts, per_device(): back_blocks.at[seq_index, picks].set(grad_rows).reshape(cotangent.shape)  52.6 us
    scatter x1, local copies, waits for them, and re-layouts, per_device(): tok_blocks.at[seq_index, picks].set(new_rows).reshape(tokens.shape)  52.5 us
  transfers between devices with their start and end apart: 8, of which 6 were waited for; matrix products, arithmetic and copies ran while one was open for 17% of the time, Pallas kernels for 0%

commit v1 on v0

v1 whole, which is shorter than its diff:
```python
import functools
import math

import jax
import jax.numpy as jnp
from jax import lax
from jax.experimental import pallas as pl
from jax.experimental.pallas import tpu as pltpu
from jax.sharding import PartitionSpec as P

HEAD_DIM = 64


norm_eps = 1e-06
beta_one = 0.9
beta_two = 0.999
adam_eps = 1e-08
learn_rate = 0.03
decay_rate = 0.1
adam_step = 10
limit_scale = 0.01
masked_out = -1e30
AXES = ("wide", "narrow")


def moment_update(grad_part, first, second):
    first_new = beta_one * first + (1.0 - beta_one) * grad_part
    second_new = beta_two * second + (1.0 - beta_two) * grad_part * grad_part
    return (first_new, second_new)


def adam_update(master, grad_part, first, second):
    first_new, second_new = moment_update(grad_part, first, second)
    first_hat = first_new / (1.0 - beta_one**adam_step)
    second_hat = second_new / (1.0 - beta_two**adam_step)
    master_new = master - learn_rate * (
        first_hat / (jnp.sqrt(second_hat) + adam_eps) + decay_rate * master
    )
    return (master_new, first_new, second_new)


f32, bf16 = jnp.float32, jnp.bfloat16
PAIR = 2 * HEAD_DIM
head_scale = HEAD_DIM ** (-0.5)
KEEP_L = ((0, 0, 0), (0, 1, 0))
KEEP_R = ((0, 0, 1), (1, 0, 1))
FAR_L = ((1, 0, 0), (1, 1, 0))
FAR_R = ((0, 1, 1), (1, 1, 1))
GROUPS = (KEEP_L, KEEP_R, FAR_L, FAR_R)


def kernel(body, name, outs, args, kinds, scratch=(), limit=24, loose=0):
    spaces = {"s": pltpu.SMEM, "v": pltpu.VMEM, "a": pltpu.HBM}
    held = len(outs) - loose
    return pl.pallas_call(
        body,
        out_shape=[
            jax.ShapeDtypeStruct(*out) if place < held else pltpu.HBM(*out)
            for place, out in enumerate(outs)
        ],
        in_specs=[pl.BlockSpec(memory_space=spaces[kind]) for kind in kinds],
        out_specs=[
            pl.BlockSpec(memory_space=pltpu.VMEM if place < held else pltpu.HBM)
            for place in range(len(outs))
        ],
        scratch_shapes=list(scratch),
        compiler_params=pltpu.CompilerParams(vmem_limit_bytes=limit << 20),
        name=name,
    )(
        *(
            pltpu.with_memory_space_constraint(arg, pltpu.HBM) if kind == "a" else arg
            for arg, kind in zip(args, kinds)
        )
    )


def each_block(pieces):
    for core in range(2):
        for group, flips in enumerate(GROUPS):
            for place, flip in enumerate(flips):
                yield flip[0] * 4 + flip[1] * 2 + core, flip[2], pieces[core * 4 + group].at[place]


def start_all(copies):
    for copy in copies:
        copy.start()


def wait_all(copies):
    for copy in copies:
        copy.wait()


def fetch(pieces, me, sem, base, left, right):
    copies = []
    for flip, half, block in each_block(pieces):
        rows = block.shape[0]
        start = pl.multiple_of((me ^ flip) * rows, rows)
        for target, column, out_column, width in (left, right)[half]:
            copies.append(
                pltpu.make_async_copy(
                    block.at[:, pl.ds(column, width)],
                    target.at[pl.ds(start, rows), pl.ds(out_column, width)],
                    sem.at[base + len(copies)],
                )
            )
    return copies


def dot_nt(left, right):
    return lax.dot_general(left, right, (((1,), (1,)), ((), ())), preferred_element_type=f32)


def dot_tn(left, right):
    return lax.dot_general(left, right, (((0,), (0,)), ((), ())), preferred_element_type=f32)


def dot_nn(left, right):
    return jnp.dot(left, right, preferred_element_type=f32)


def mean_last(array):
    return jnp.mean(array, axis=-1, keepdims=True)


def sum_rows(array):
    return jnp.sum(array, axis=0, keepdims=True)


def head_masks(dtype):
    lanes = lax.broadcasted_iota(jnp.int32, (1, PAIR), 1)
    first = (lanes < HEAD_DIM).astype(f32).astype(dtype)
    return first, (1 - first).astype(dtype)


def two_heads(pair, masks):
    return jnp.concatenate([pair * masks[0], pair * masks[1]], axis=0)


def one_pair(stacked, masks):
    rows = stacked.shape[0] // 2
    return stacked[:rows] * masks[0] + stacked[rows:] * masks[1]


def attend(me, pieces, picked, back_rows, seg_row, seg_col, order):
    rows, width = picked.shape
    seqs = seg_row.shape[0]
    top = rows // seqs
    pairs = width // PAIR
    first = pieces[0].shape[2]
    rest = 3 * width - first
    spare = pieces[1].shape[2] - rest - width

    def body(me_ref, *refs):
        blocks, refs = refs[:8], refs[8:]
        x_ref, dy_ref, seg_row_ref, seg_col_ref, order_ref = refs[:5]
        own_ref, send_ref, df_ref, gate_ref, vec_ref, add_ref, h2_ref = refs[5:12]
        all_ref, out_ref, qkv_out, prob_out = refs[12:16]
        w_qkv, w_out, w_vec, qkv_ref, prob_ref, att_ref, sem = refs[16:]
        vec_copies = fetch(blocks, me_ref[0], sem, 0, (), ((w_vec, rest + width, 0, spare),))
        left = fetch(blocks, me_ref[0], sem, 8, ((w_qkv, 0, 0, first),), ())
        right = fetch(blocks, me_ref[0], sem, 16, (), ((w_qkv, 0, first, rest),))
        out_copies = fetch(blocks, me_ref[0], sem, 24, (), ((w_out, rest, 0, width),))
        start_all(vec_copies + left + right + out_copies)
        wait_all(vec_copies)
        vec = w_vec[...].astype(f32).T[:8]
        vec_ref[...] = vec
        x = x_ref[...].astype(f32)
        h1 = (x * lax.rsqrt(mean_last(x * x) + norm_eps) * vec[0:1]).astype(bf16)
        for copies, start, count in ((left, 0, first), (right, first, rest)):
            wait_all(copies)
            for part in range(start, start + count, 384):
                lanes = pl.ds(part, 384)
                qkv_ref[:, lanes] = dot_nn(h1, w_qkv[:, lanes]).astype(bf16)
        stored = [
            pltpu.make_async_copy(w_qkv, all_ref, sem.at[32]),
            pltpu.make_async_copy(qkv_ref, qkv_out, sem.at[33]),
            pltpu.make_async_copy(w_out, out_ref, sem.at[34]),
        ]
        wait_all(out_copies)
        start_all(stored)
        masks, masks_f = head_masks(bf16), head_masks(f32)
        ordered_pairs = lax.broadcasted_iota(jnp.int32, (top, top), 1) <= lax.broadcasted_iota(
            jnp.int32, (top, top), 0
        )
        for seq in range(seqs):
            here = pl.ds(seq * top, top)
            seen = ordered_pairs & (seg_col_ref[seq] == seg_row_ref[seq])
            hidden = jnp.where(seen, 0.0, masked_out)
            hidden = jnp.concatenate([hidden, hidden], axis=0)
            for pair in range(pairs):
                q, k, v = (
                    qkv_ref[here, pl.ds(part * width + pair * PAIR, PAIR)] for part in range(3)
                )
                scores = dot_nt(two_heads(q, masks), k) * head_scale
                scores = jnp.where(hidden < 0.0, masked_out, scores)
                power = jnp.exp(scores - jnp.max(scores, axis=-1, keepdims=True))
                probs = power / jnp.sum(power, axis=-1, keepdims=True)
                prob_ref[seq * pairs + pair] = probs
                mixed = one_pair(dot_nn(probs.astype(bf16), v), masks_f)
                att_ref[here, pl.ds(pair * PAIR, PAIR)] = mixed.astype(bf16)
            group = pl.ds(seq * pairs, pairs)
            stored.append(
                pltpu.make_async_copy(prob_ref.at[group], prob_out.at[group], sem.at[35 + seq])
            )
            stored[-1].start()
        gate = jax.nn.sigmoid(jnp.sum(x * vec[2:3], axis=-1, keepdims=True))
        gate_ref[...] = jnp.broadcast_to(gate, gate_ref.shape)
        df = (gate * dy_ref[...].astype(f32)).astype(bf16)
        df_ref[...] = df
        added = dot_nn(att_ref[...], w_out[...])
        add_ref[...] = added
        middle = x + added
        h2 = (middle * lax.rsqrt(mean_last(middle * middle) + norm_eps) * vec[1:2]).astype(bf16)
        h2_ref[...] = h2
        for half in range(2):
            lanes = slice(half * (width // 2), (half + 1) * (width // 2))
            send_ref[2 + half] = df[:, lanes]
            send_ref[4 + half] = h2[:, lanes]
        chosen = one_hot_columns(order_ref)
        for place, array in enumerate((h1, att_ref[...])):
            parted = dot_nn(array, chosen).astype(bf16)
            own_ref[place] = parted[:, : width // 2]
            send_ref[place] = parted[:, width // 2 :]
        wait_all(stored)

    outs = [
        ((2, rows, width // 2), bf16),
        ((6, rows, width // 2), bf16),
        ((rows, width), bf16),
        ((rows, 128), f32),
        ((8, width), f32),
        ((rows, width), f32),
        ((rows, width), bf16),
        ((width, 3 * width), bf16),
        ((width, width), bf16),
        ((rows, 3 * width), bf16),
        ((seqs * pairs, 2 * top, top), f32),
    ]
    scratch = [
        pltpu.VMEM((width, 3 * width), bf16),
        pltpu.VMEM((width, width), bf16),
        pltpu.VMEM((width, spare), bf16),
        pltpu.VMEM((rows, 3 * width), bf16),
        pltpu.VMEM((seqs * pairs, 2 * top, top), f32),
        pltpu.VMEM((rows, width), bf16),
        pltpu.SemaphoreType.DMA((35 + seqs,)),
    ]
    args = (me, *pieces, picked, back_rows, seg_row, seg_col, order)
    return kernel(body, "attend", outs, args, "s" + "a" * 8 + "vvvvv", scratch, 26, 4)


def one_hot_columns(order_ref):
    width = order_ref.shape[1]
    chosen = lax.broadcasted_iota(jnp.int32, (width, width), 0) == order_ref[...]
    return chosen.astype(f32).astype(bf16)


def climb(me, pieces, h2, sib, order):
    rows, width = h2.shape
    first = pieces[0].shape[2]
    block = 2 * first // 8

    def body(me_ref, *refs):
        blocks, refs = refs[:8], refs[8:]
        h2_ref, sib_ref, order_ref = refs[:3]
        own_ref, send_ref, far_ref, pair_ref, up_ref, slope_out = refs[3:9]
        w_up, slope_ref, both_ref, sem = refs[9:]
        copies = fetch(
            blocks, me_ref[0], sem, 0, ((w_up, 0, 0, first),), ((w_up, 0, first, first),)
        )
        start_all(copies)
        both_ref[:rows] = h2_ref[...]
        for half in range(2):
            lanes = pl.ds(half * (width // 2), width // 2)
            both_ref[rows:, lanes] = sib_ref[4 + half]
        chosen = one_hot_columns(order_ref)[:, : width // 2]
        parted = dot_nn(both_ref[...], chosen).astype(bf16)
        pair_ref[0] = parted[:rows]
        pair_ref[1] = parted[rows:]
        wait_all(copies)
        stored = [pltpu.make_async_copy(w_up, up_ref, sem.at[16])]
        start_all(stored)
        scale = math.sqrt(2.0 / math.pi)
        for flip in range(8):
            start = pl.multiple_of((me_ref[0] ^ flip) * block, block)
            place = flip // 2
            lanes = pl.ds(place * block, block)
            weights = w_up[:, pl.ds(start, block)]
            u = dot_nn(both_ref[:rows], weights)
            square = u * u
            bent = jnp.tanh(scale * (u + 0.044715 * (square * u)))
            half_up = 0.5 * (1.0 + bent)
            target = send_ref if flip % 2 else own_ref
            target[:, lanes] = (u * half_up).astype(bf16)
            where = (flip % 2) * 4 + place
            slope_ref[where] = half_up + (0.5 * u) * (1.0 - bent * bent) * (
                scale * (1.0 + (3.0 * 0.044715) * square)
            )
            stored.append(
                pltpu.make_async_copy(
                    slope_ref.at[where], slope_out.at[where], sem.at[17 + flip]
                )
            )
            stored[-1].start()
            if flip % 2 == 0:
                u = dot_nn(both_ref[rows:], weights)
                bent = jnp.tanh(scale * (u + 0.044715 * (u * u * u)))
                far_ref[:, lanes] = (0.5 * u * (1.0 + bent)).astype(bf16)
        wait_all(stored)

    outs = [
        ((rows, 4 * block), bf16),
        ((rows, 4 * block), bf16),
        ((rows, 4 * block), bf16),
        ((2, rows, width // 2), bf16),
        ((width, 8 * block), bf16),
        ((8, rows, block), f32),
    ]
    scratch = [
        pltpu.VMEM((width, 8 * block), bf16),
        pltpu.VMEM((8, rows, block), f32),
        pltpu.VMEM((2 * rows, width), bf16),
        pltpu.SemaphoreType.DMA((25,)),
    ]
    args = (me, *pieces, h2, sib, order)
    return kernel(body, "climb", outs, args, "s" + "a" * 8 + "vvv", scratch, 26, 2)


class View:
    def __init__(self, array, columns=None, first=0, lead=None):
        self.array, self.first, self.lead = array, first, lead
        self.columns = columns or array.shape[-1]

    def value(self):
        array = self.array if self.lead is None else self.array[self.lead]
        return array[:, self.first : self.first + self.columns]

    def read(self, ref, first, columns):
        lanes = pl.ds(self.first + first, columns)
        return ref[:, lanes] if self.lead is None else ref[self.lead, :, lanes]


def outer(name, products, split):
    length = products[0][0].columns // 4
    total = sum(product[1].columns for product in products)
    widths = (split, total - split)
    order = ((2, 3), (1, 3), (0, 1), (0, 2))

    def body(*refs):
        ins, outs = refs[: 4 * len(products)], refs[4 * len(products) :]
        base = 0
        for number, product in enumerate(products):
            reads = [
                functools.partial(view.read, ref)
                for view, ref in zip(product, ins[4 * number : 4 * number + 4])
            ]
            columns = product[1].columns
            step = min(768, columns)
            for start in range(0, columns, step):
                for first in range(0, 4 * length, 384):
                    value = dot_tn(reads[0](first, 384), reads[1](start, step))
                    value += dot_tn(reads[2](first, 384), reads[3](start, step))
                    for block in range(first // length, (first + 384) // length):
                        part = value[block * length - first : (block + 1) * length - first]
                        for half in range(2):
                            low = max(base + start, half * split)
                            high = min(base + start + step, split + half * (total - split))
                            if high <= low:
                                continue
                            piece = part[:, low - base - start : high - base - start]
                            out_lanes = pl.ds(low - half * split, high - low)
                            for out in (half, 2 + half):
                                if block in order[out]:
                                    outs[out][order[out].index(block), :, out_lanes] = piece.astype(
                                        outs[out].dtype
                                    )
            base += columns

    outs = [
        ((2, length, widths[out % 2]), bf16 if out < 2 else f32) for out in range(4)
    ]
    args = [view.array for product in products for view in product]
    return kernel(body, name, outs, args, "v" * len(args))


def descend(me, pieces, slope, df):
    rows, width = df.shape
    block = slope.shape[2]

    def body(me_ref, *refs):
        blocks, refs = refs[:8], refs[8:]
        slope_in, df_ref, du_ref, down_ref, w_down, slope_ref, sem = refs
        copies = [[] for _ in range(8)]
        for flip, side, part in each_block(blocks):
            lanes = pl.ds(side * (width // 2), width // 2)
            place = (flip % 2) * 4 + flip // 2
            target = w_down.at[pl.ds(place * block, block), lanes]
            copies[place].append(
                pltpu.make_async_copy(part, target, sem.at[place * 2 + side])
            )
        for place, pair in enumerate(copies):
            pair.append(
                pltpu.make_async_copy(
                    slope_in.at[place], slope_ref.at[place], sem.at[17 + place]
                )
            )
            start_all(pair)
        for place in range(8):
            wait_all(copies[place])
            flip = place % 4 * 2 + place // 4
            start = pl.multiple_of((me_ref[0] ^ flip) * block, block)
            dg = dot_nt(df_ref[...], w_down[pl.ds(place * block, block)])
            du_ref[:, pl.ds(start, block)] = (dg * slope_ref[place]).astype(bf16)
        stored = pltpu.make_async_copy(w_down, down_ref, sem.at[16])
        stored.start()
        stored.wait()

    outs = [((rows, 8 * block), bf16), ((8 * block, width), bf16)]
    scratch = [
        pltpu.VMEM((8 * block, width), bf16),
        pltpu.VMEM((8, rows, block), f32),
        pltpu.SemaphoreType.DMA((25,)),
    ]
    args = (me, *pieces, slope, df)
    return kernel(body, "descend", outs, args, "s" + "a" * 9 + "v", scratch, 24, 1)


def unclimb(w_up, du, picked, added, gate, back_rows, vec):
    rows, width = picked.shape

    def body(up_ref, du_ref, x_ref, add_ref, gate_ref, dy_ref, vec_ref, dm_ref, da_ref, dg_ref):
        dh = dot_nt(du_ref[...], up_ref[...])
        middle = x_ref[...].astype(f32) + add_ref[...]
        inverse = lax.rsqrt(mean_last(middle * middle) + norm_eps)
        unit = middle * inverse
        dg_ref[...] = jnp.broadcast_to(sum_rows(dh * unit), dg_ref.shape)
        scaled = dh * vec_ref[1:2]
        dm = inverse * (scaled - unit * mean_last(scaled * unit))
        dm_ref[...] = dm
        da_ref[...] = (gate_ref[:, 0:1] * dy_ref[...].astype(f32) + dm).astype(bf16)

    outs = [((rows, width), f32), ((rows, width), bf16), ((8, width), f32)]
    args = (w_up, du, picked, added, gate, back_rows, vec)
    return kernel(body, "unclimb", outs, args, "v" * 7)


def unattend(w_out, da, qkv, probs):
    rows, width = da.shape
    top = probs.shape[2]
    seqs, pairs = rows // top, width // PAIR

    def body(out_ref, da_ref, qkv_ref, prob_ref, dqkv_ref, do_ref):
        do_ref[...] = dot_nt(da_ref[...], out_ref[...]).astype(bf16)
        masks, masks_f = head_masks(bf16), head_masks(f32)
        for seq in range(seqs):
            here = pl.ds(seq * top, top)
            for pair in range(pairs):
                lanes = [pl.ds(part * width + pair * PAIR, PAIR) for part in range(3)]
                q, k, v = (qkv_ref[here, part] for part in lanes)
                do = two_heads(do_ref[here, pl.ds(pair * PAIR, PAIR)], masks)
                probs = prob_ref[seq * pairs + pair]
                dprobs = dot_nt(do, v)
                dscores = probs * (dprobs - jnp.sum(dprobs * probs, axis=-1, keepdims=True))
                dscores = dscores.astype(bf16)
                dq = one_pair(dot_nn(dscores, k), masks_f) * head_scale
                dk = dot_tn(dscores, two_heads(q, masks)) * head_scale
                dv = dot_tn(probs.astype(bf16), do)
                for part, value in zip(lanes, (dq, dk, dv)):
                    dqkv_ref[here, part] = value.astype(bf16)

    scratch = [pltpu.VMEM((rows, width), bf16)]
    outs = [((rows, 3 * width), bf16)]
    return kernel(body, "unattend", outs, (w_out, da, qkv, probs), "vvvv", scratch)[0]


def finish_mlp(w_down, own, send, picked, added, gate, back_rows):
    rows, width = picked.shape
    half = w_down.shape[0] // 2

    def body(down_ref, own_ref, send_ref, x_ref, add_ref, gate_ref, dy_ref, *outs):
        new_ref, dlogit_ref, dr_ref = outs
        out = dot_nn(own_ref[:, :half], down_ref[:half])
        out += dot_nn(send_ref[:, :half], down_ref[half:])
        both = add_ref[...] + out
        x = x_ref[...].astype(f32)
        gate = gate_ref[:, 0:1]
        new_ref[...] = (x + gate * both).astype(bf16)
        dlogit = jnp.sum(dy_ref[...].astype(f32) * both, axis=-1, keepdims=True)
        dlogit = dlogit * gate * (1.0 - gate)
        dlogit_ref[...] = jnp.broadcast_to(dlogit, dlogit_ref.shape)
        dr_ref[...] = jnp.broadcast_to(sum_rows(dlogit * x), dr_ref.shape)

    outs = [((rows, width), bf16), ((rows, 128), f32), ((8, width), f32)]
    args = (w_down, own, send, picked, added, gate, back_rows)
    return kernel(body, "finish_mlp", outs, args, "v" * 7)


def finish_rows(w_qkv, dqkv, picked, back_rows, dmiddle, dlogit, vec):
    rows, width = picked.shape

    def body(all_ref, dqkv_ref, x_ref, dy_ref, dm_ref, dlogit_ref, vec_ref, grad_ref, dg_ref):
        dh = dot_nt(dqkv_ref[...], all_ref[...])
        x = x_ref[...].astype(f32)
        inverse = lax.rsqrt(mean_last(x * x) + norm_eps)
        unit = x * inverse
        dg_ref[...] = jnp.broadcast_to(sum_rows(dh * unit), dg_ref.shape)
        scaled = dh * vec_ref[0:1]
        dx = inverse * (scaled - unit * mean_last(scaled * unit))
        grad = dy_ref[...].astype(f32) + dm_ref[...] + dx + dlogit_ref[:, 0:1] * vec_ref[2:3]
        grad_ref[...] = grad.astype(bf16)

    outs = [((rows, width), bf16), ((8, width), f32)]
    args = (w_qkv, dqkv, picked, back_rows, dmiddle, dlogit, vec)
    return kernel(body, "finish_rows", outs, args, "v" * 7)


def join_z(z, own, others, split):
    rows, width = own.shape

    def body(z_ref, *refs):
        ins, left_ref, right_ref, total = refs[:4], *refs[4:]
        for flip, block in enumerate(ins):
            start = pl.multiple_of((z_ref[0] ^ flip) * rows, rows)
            total[pl.ds(start, rows)] = block[...].astype(f32)
        left_ref[...] = total[:, :split].astype(bf16)
        right_ref[...] = total[:, split:].astype(bf16)

    outs = [((4 * rows, split), bf16), ((4 * rows, width - split), bf16)]
    scratch = [pltpu.VMEM((4 * rows, width), f32)]
    return kernel(body, "join_z", outs, (z, own, *others), "svvvv", scratch)


def join_z_pairs(z, left, right, near_l, near_r, others):
    rows, width = left.shape

    def body(z_ref, *refs):
        mine, others, outs = refs[:4], refs[4:7], refs[7:]
        for flip in range(4):
            start = pl.ds(pl.multiple_of((z_ref[0] ^ flip) * rows, rows), rows)
            for place in range(4):
                block = others[flip - 1][place] if flip else mine[place][...]
                outs[place // 2][place % 2, start] = block

    outs = [((2, 4 * rows, width), bf16)] * 2
    args = (z, left, near_l, right, near_r, *others)
    return kernel(body, "join_z_pairs", outs, args, "svvvvvvv")


def add_z_pairs(z, keep_l, keep_r, other_l, other_r):
    pair, rows, width = keep_l.shape
    part = rows // 4

    def body(z_ref, keep_l, keep_r, other_l, other_r, mine, send, total):
        for half, (keep, other) in enumerate(((keep_l, other_l), (keep_r, other_r))):
            for place in range(pair):
                total[half * pair + place] = keep[place] + other[place].astype(f32)
        for flip in range(4):
            start = pl.multiple_of((z_ref[0] ^ flip) * part, part)
            out = (mine, send)[flip % 2]
            out[flip // 2] = total[:, pl.ds(start, part)].astype(out.dtype)

    outs = [((2, 4, part, width), f32), ((2, 4, part, width), bf16)]
    scratch = [pltpu.VMEM((4, rows, width), f32)]
    args = (z, keep_l, keep_r, other_l, other_r)
    return kernel(body, "add_z_pairs", outs, args, "svvvv", scratch)


def add_four(mine, other):
    def body(mine, other, send_l, send_r, keep):
        def total(place):
            return mine[place] + other[place].astype(f32)

        width = mine.shape[2]
        keep[:, :width] = total(0)
        keep[:, width:] = total(2)
        send_l[...] = total(1).astype(bf16)
        send_r[...] = total(3).astype(bf16)

    _, rows, width = mine.shape
    outs = [((rows, width), bf16)] * 2 + [((rows, 2 * width), f32)]
    return kernel(body, "add_four", outs, (mine, other), "vv")


def add_pairs(keep_l, keep_r, other_l, other_r):
    def body(keep_l, keep_r, other_l, other_r, send_l, send_r, left, right):
        for keep, other, send, mine in (
            (keep_l, other_l, send_l, left),
            (keep_r, other_r, send_r, right),
        ):
            send[...] = (keep[1] + other[1].astype(f32)).astype(bf16)
            mine[...] = keep[0] + other[0].astype(f32)

    shapes = [keep_l.shape[1:], keep_r.shape[1:]]
    outs = [(shape, kind) for kind in (bf16, f32) for shape in shapes]
    return kernel(body, "add_pairs", outs, (keep_l, keep_r, other_l, other_r), "vvvv")


def add_split(z, keep_l, keep_r, other_l, other_r):
    rows, split = keep_l.shape
    width = split + keep_r.shape[1]
    part = rows // 4

    def body(z_ref, keep_l, keep_r, other_l, other_r, mine, one, two, three, total):
        total[:, :split] = keep_l[...] + other_l[...].astype(f32)
        total[:, split:] = keep_r[...] + other_r[...].astype(f32)
        for flip, out in enumerate((mine, one, two, three)):
            start = pl.multiple_of((z_ref[0] ^ flip) * part, part)
            out[...] = total[pl.ds(start, part)].astype(out.dtype)

    outs = [((part, width), f32)] + [((part, width), bf16)] * 3
    scratch = [pltpu.VMEM((rows, width), f32)]
    args = (z, keep_l, keep_r, other_l, other_r)
    return kernel(body, "add_split", outs, args, "svvvv", scratch)


def add_next(keep, other):
    def body(keep, other, mine, send):
        mine[...] = keep[0] + other[0].astype(f32)
        send[...] = (keep[1] + other[1].astype(f32)).astype(bf16)

    shape = keep.shape[1:]
    return kernel(body, "add_next", [(shape, f32), (shape, bf16)], (keep, other), "vv")


def settle_halves(keep, other_l, other_r):
    def body(keep, other_l, other_r, grad, square):
        width = other_l.shape[1]
        total = None
        for half, other in enumerate((other_l, other_r)):
            lanes = pl.ds(half * width, width)
            value = keep[:, lanes] + other[...].astype(f32)
            grad[:, lanes] = value
            part = jnp.sum(value * value)
            total = part if total is None else total + part
        square[...] = jnp.full(square.shape, total)

    outs = [(keep.shape, f32), ((8, 128), f32)]
    return kernel(body, "settle_halves", outs, (keep, other_l, other_r), "vvv")


def settle_z(mine, others):
    def body(mine, one, two, three, grad, square):
        value = mine[...] + one[...].astype(f32) + two[...].astype(f32) + three[...].astype(f32)
        grad[...] = value
        square[...] = jnp.full(square.shape, jnp.sum(value * value))

    outs = [(mine.shape, f32), ((8, 128), f32)]
    return kernel(body, "settle_z", outs, (mine, *others), "vvvv")


def update(squares, limit, grads, states, vec_grad, vec_states):
    count = len(grads)

    def body(square_ref, *refs):
        grad_refs, refs = refs[:count], refs[count:]
        state_refs, refs = refs[: 3 * count], refs[3 * count :]
        vec_ref, vec_m, vec_v, norm_ref, out_refs = *refs[:4], refs[4:]
        norm = jnp.sqrt(jnp.sum(square_ref[...], axis=0, keepdims=True)[:, 0:1])
        norm_ref[...] = jnp.broadcast_to(norm, norm_ref.shape)
        factor = jnp.minimum(1.0, limit / (norm + 1e-06))
        for place in range(count):
            w, m, v = (ref[...] for ref in state_refs[3 * place : 3 * place + 3])
            grad = grads[place].read(grad_refs[place], 0, grads[place].columns) * factor
            for ref, value in zip(out_refs[3 * place :], adam_update(w, grad, m, v)):
                ref[...] = value
        first, second = moment_update(vec_ref[...] * factor, vec_m[...], vec_v[...])
        out_refs[-2][...] = first
        out_refs[-1][...] = second

    flat = [array for state in states for array in state]
    outs = [((8, 128), f32)] + [(array.shape, f32) for array in (*flat, *vec_states)]
    args = (squares, *(grad.array for grad in grads), *flat, vec_grad, *vec_states)
    return kernel(body, "update", outs, args, "v" * len(args), (), 32)


class Steps:
    def __init__(self, chain):
        self.chain = chain
        self.result = None
        self.launch(next(chain))

    def launch(self, step):
        self.flips = [flip for _, flip in step]
        self.given = [array for array, _ in step]

    def advance(self, arrays):
        try:
            self.launch(self.chain.send(arrays))
        except StopIteration as stop:
            self.flips, self.given, self.result = (), (), stop.value


def slot(chains, value):
    arrays = [
        [swap(array, flip) for array, flip in zip(chain.given, chain.flips)] for chain in chains
    ]
    arrays, value = lax.optimization_barrier((arrays, value))
    for chain, array in zip(chains, arrays):
        chain.advance(array)
    return value


def ready(chains, value):
    arrays, value = lax.optimization_barrier(([chain.given for chain in chains], value))
    for chain, array in zip(chains, arrays):
        chain.given = array
    return value


def swap(array, bit):
    count = lax.axis_size("wide") * lax.axis_size("narrow")
    return lax.ppermute(array, AXES, [(i, i ^ bit) for i in range(count)])


def exchange(*arrays):
    return (yield [(array, 4) for array in arrays])


def around_z(shard, at_once):
    if at_once:
        return (yield [(shard, flip) for flip in (1, 2, 3)])
    (two,) = yield [(shard, 2)]
    (both,) = yield [(jnp.stack([shard, two]), 1)]
    return both[0], two, both[1]


def gather(shard, z, split, at_once):
    others = yield from around_z(shard, at_once)
    left, right = join_z(z, shard, others, split)
    near_l, near_r = yield [(left, 8), (right, 16)]
    return (yield from spread(jnp.stack([left, near_l]), jnp.stack([right, near_r])))


def gather_pairs(shard, z):
    half = shard.shape[1] // 2
    left, right = shard[:, :half], shard[:, half:]
    near_l, near_r = yield [(left, 8), (right, 16)]
    others = yield from around_z(jnp.stack([left, near_l, right, near_r]), False)
    keep_l, keep_r = join_z_pairs(z, left, right, near_l, near_r, others)
    return (yield from spread(keep_l, keep_r))


def spread(keep_l, keep_r):
    far_l, far_r, *near = yield [(keep_l, 16), (keep_r, 8), (keep_l, 4), (keep_r, 4)]
    far = yield [(far_l, 4), (far_r, 4)]
    return (keep_l, keep_r, far_l, far_r, *near, *far)


def scatter(z, send_l, send_r, keep_l, keep_r):
    other_l, other_r = yield [(send_l, 16), (send_r, 8)]
    send_l, send_r, left, right = add_pairs(keep_l, keep_r, other_l, other_r)
    other_l, other_r = yield [(send_l, 8), (send_r, 16)]
    mine, *sends = add_split(z, left, right, other_l, other_r)
    others = yield [(send, flip + 1) for flip, send in enumerate(sends)]
    return settle_z(mine, others)


def scatter_pairs(z, send_l, send_r, keep_l, keep_r):
    other_l, other_r = yield [(send_l, 16), (send_r, 8)]
    mine, send = add_z_pairs(z, keep_l, keep_r, other_l, other_r)
    (other,) = yield [(send, 1)]
    mine, send = add_next(mine, other)
    (other,) = yield [(send, 2)]
    send_l, send_r, keep = add_four(mine, other)
    other_l, other_r = yield [(send_l, 8), (send_r, 16)]
    return settle_halves(keep, other_l, other_r)


def cut(whole, split):
    blocks = whole.reshape(8, whole.shape[0] // 8, whole.shape[1])
    sides = (blocks[..., :split], blocks[..., split:])
    return tuple(
        jnp.stack([sides[flip[2]][flip[0] * 4 + flip[1] * 2 + core] for flip in flips])
        for core in range(2)
        for flips in GROUPS
    )


def uncut(own, send):
    parts = jnp.stack([array.reshape(array.shape[0], 4, -1) for array in (own, send)], axis=2)
    return parts.reshape(own.shape[0], -1)


def per_device(
    paired,
    tokens,
    cotangent,
    segments,
    picks,
    w_qkv,
    w_out,
    w_up,
    w_down,
    vectors,
    m_qkv,
    m_out,
    m_up,
    m_down,
    m_vectors,
    v_qkv,
    v_out,
    v_up,
    v_down,
    v_vectors,
):
    devices_all = lax.axis_size("wide") * lax.axis_size("narrow")
    lane = lax.axis_index(AXES)
    seq_count, top_count = picks.shape
    seq_len = segments.shape[1]
    model_width = tokens.shape[1]
    qkv_width = w_qkv.shape[1]
    ff_width = w_up.shape[1]
    shard_width = vectors.shape[1]
    split_a, split_b, split_c = 2 * model_width, ff_width // 2, model_width // 2
    z = (lane & 3).reshape(1)
    me = (lane >> 2).reshape(1) if paired else jnp.zeros((1,), jnp.int32)

    turned = jnp.pad(vectors.T, ((0, 0), (0, 125)))
    chunk_a = jnp.concatenate([w_qkv, w_out, turned], axis=1).astype(bf16)
    chunk_b = w_up.astype(bf16)
    chunk_c = w_down.astype(bf16)

    def start(chain, *args):
        return Steps(chain(*args)) if paired else None

    def tick(chains, value):
        return slot(chains, value) if paired else value

    def stage(chains, value):
        return ready(chains, value) if paired else value

    def whole(take, chunk, split):
        if paired:
            return take.result
        return cut(lax.all_gather(chunk, AXES, axis=0, tiled=True), split)

    hot = picks[:, :, None] == jnp.arange(seq_len, dtype=jnp.int32)[None, None, :]
    hot_low = hot.astype(bf16)
    tok_blocks = tokens.reshape(seq_count, seq_len, model_width)
    back_blocks = cotangent.reshape(seq_count, seq_len, model_width)

    def pick(blocks):
        rows = jnp.einsum("skl,sld->skd", hot_low, blocks, preferred_element_type=f32)
        return rows.astype(bf16).reshape(-1, model_width)

    def place(blocks, rows):
        rows = rows.reshape(seq_count, top_count, model_width)
        spread = jnp.einsum("skl,skd->sld", hot_low, rows, preferred_element_type=f32).astype(bf16)
        taken = jnp.any(hot, axis=1)
        return jnp.where(taken[:, :, None], spread, blocks).reshape(-1, model_width)

    take_a = start(gather, chunk_a, z, split_a, True)
    take_c = start(gather_pairs, chunk_c, z)
    picked = pick(tok_blocks)
    back_rows = pick(back_blocks)
    seg_sel = jnp.sum(jnp.where(hot, segments[:, None, :], 0), axis=-1)
    seg_row, seg_col = seg_sel[:, None, :], seg_sel[:, :, None]
    spot = jnp.arange(model_width, dtype=jnp.int32)
    half, eighth = model_width // 2, model_width // 8
    flip = spot % half // eighth * 2 + spot // half
    order = ((me[0] ^ flip) * eighth + spot % eighth)[None]
    inputs = (picked, back_rows, seg_row, seg_col, order, chunk_b)
    inputs = tick([take_a], inputs)
    take_b = start(gather, inputs[-1], z, split_b, False)
    inputs = tick([take_a, take_b, take_c], inputs[:-1])
    inputs = tick([take_a, take_b], inputs)
    inputs = tick([take_a, take_b, take_c], inputs)

    all_a = whole(take_a, chunk_a, split_a)
    picked, back_rows = inputs[:2]
    order = inputs[4]
    state = attend(me, all_a, *inputs)
    state = tick([take_b, take_c], state)
    own, send, df, gate, vec, added, h2, all_qkv, all_out, qkv, probs = state
    early = start(exchange, send)
    h2 = stage([take_c], h2)
    h2 = tick([take_b, early], h2)
    (sib,) = early.result if paired else (send,)
    all_b = whole(take_b, chunk_b, split_b)
    g_own, g_send, g_sib, h2_pair, all_up, slope = climb(me, all_b, h2, sib, order)

    def give(chain, name, products, split):
        if paired:
            return Steps(chain(z, *outer(name, products, split)))
        grads = [dot_tn(uncut(one.value(), far.value()), two.value()) for one, two, far, _ in products]
        grad = jnp.concatenate(grads, axis=1)
        grad = lax.psum_scatter(grad, AXES, scatter_dimension=0, tiled=True)
        return grad, jnp.full((8, 128), jnp.sum(grad * grad))

    df_sib = jnp.concatenate([sib[2], sib[3]], axis=1)
    left_c = View(g_sib) if paired else View(g_send)
    give_c = give(
        scatter_pairs, "outer_c", [(View(g_own), View(df), left_c, View(df_sib))], split_c
    )
    slope = stage([give_c], slope)
    slope = tick([take_c], slope)
    slope = tick([take_c], slope)
    all_c = whole(take_c, chunk_c, split_c)
    du, all_down = descend(me, all_c, slope, df)
    late_u = start(exchange, du)
    du = stage([late_u], du)
    dmiddle, da, dg2 = unclimb(all_up, du, picked, added, gate, back_rows, vec)
    da, dmiddle = tick([late_u, give_c], (da, dmiddle))
    (du_sib,) = late_u.result if paired else (du,)
    views = [View(h2_pair, lead=place) for place in range(2)]
    if not paired:
        cols = h2.reshape(h2.shape[0], 4, 2, -1)
        views = [View(cols[:, :, core].reshape(h2.shape[0], -1)) for core in range(2)]
    give_b = give(
        scatter_pairs, "outer_b", [(views[0], View(du), views[1], View(du_sib))], split_b
    )
    da = stage([give_b, give_c], da)
    dqkv = unattend(all_out, da, qkv, probs)
    late_q = start(exchange, dqkv, da)
    dqkv, dmiddle = tick([late_q], (dqkv, dmiddle))
    dqkv_sib, da_sib = late_q.result if paired else (dqkv, da)
    give_a = give(
        scatter,
        "outer_a",
        [
            (View(own, lead=0), View(dqkv), View(sib, lead=0), View(dqkv_sib)),
            (View(own, lead=1), View(da), View(sib, lead=1), View(da_sib)),
        ],
        split_a,
    )
    g_own, dqkv = stage([give_a], (g_own, dqkv))
    new_rows, dlogit, dr = finish_mlp(
        all_down, g_own, g_send, picked, added, gate, back_rows
    )
    grad_rows, dg1 = finish_rows(all_qkv, dqkv, picked, back_rows, dmiddle, dlogit, vec)
    new_rows, grad_rows, dg1 = tick([give_b, give_c], (new_rows, grad_rows, dg1))
    new_rows = stage([give_b, give_c], new_rows)
    mixed_rows = place(tok_blocks, new_rows)
    grad_vectors = jnp.stack([dg1[0], dg2[0], dr[0]], axis=0)
    vec_parts = grad_vectors.reshape(3, devices_all, shard_width).transpose(1, 0, 2)
    mixed_rows, vec_parts, grad_rows = tick(
        [give_a, give_b, give_c], (mixed_rows, vec_parts, grad_rows)
    )
    grad_rows = stage([give_a, give_b, give_c], grad_rows)
    grad_vec = jnp.sum(lax.all_to_all(vec_parts, AXES, 0, 0, tiled=True), axis=0)
    grad_rows, grad_vec = tick([give_a, give_b, give_c], (grad_rows, grad_vec))
    grad_rows = stage([give_a, give_b], grad_rows)
    input_grad = place(back_blocks, grad_rows)
    input_grad, grad_vec = tick([give_a, give_b], (input_grad, grad_vec))
    if paired:
        give_a, give_b, give_c = give_a.result, give_b.result, give_c.result
    local_sq = give_a[1] + give_b[1] + give_c[1] + jnp.sum(grad_vec * grad_vec)
    squares = jnp.broadcast_to(local_sq[:1], (devices_all, 128))
    squares = lax.all_to_all(squares, AXES, 0, 0, tiled=True)
    params_all = 4 * model_width * model_width + 2 * model_width * ff_width + 3 * model_width
    selected_all = seq_count * top_count * devices_all
    clip_limit = limit_scale * math.sqrt(params_all * selected_all)
    norm, *news = update(
        squares,
        clip_limit,
        [
            View(give_a[0], qkv_width),
            View(give_a[0], model_width, qkv_width),
            View(give_b[0]),
            View(give_c[0]),
        ],
        [
            (w_qkv, m_qkv, v_qkv),
            (w_out, m_out, v_out),
            (w_up, m_up, v_up),
            (w_down, m_down, v_down),
        ],
        grad_vec,
        (m_vectors, v_vectors),
    )
    return (
        mixed_rows,
        input_grad,
        norm[0, 0],
        *news[0:12:3],
        *news[1:12:3],
        news[12],
        *news[2:12:3],
        news[13],
    )


def solution(mesh):
    placed = (
        P(("wide", "narrow"), None),
        P(("wide", "narrow"), None),
        P(("wide", "narrow"), None),
        P(("wide", "narrow"), None),
        P(("wide", "narrow"), None),
        P(("wide", "narrow"), None),
        P(("wide", "narrow"), None),
        P(("wide", "narrow"), None),
        P(None, ("wide", "narrow")),
        P(("wide", "narrow"), None),
        P(("wide", "narrow"), None),
        P(("wide", "narrow"), None),
        P(("wide", "narrow"), None),
        P(None, ("wide", "narrow")),
        P(("wide", "narrow"), None),
        P(("wide", "narrow"), None),
        P(("wide", "narrow"), None),
        P(("wide", "narrow"), None),
        P(None, ("wide", "narrow")),
    )
    paired = mesh.shape["wide"] == 8 and mesh.shape["narrow"] == 4
    return jax.shard_map(
        functools.partial(per_device, paired),
        mesh=mesh,
        in_specs=placed,
        out_specs=(
            P(("wide", "narrow"), None),
            P(("wide", "narrow"), None),
            P(),
            P(("wide", "narrow"), None),
            P(("wide", "narrow"), None),
            P(("wide", "narrow"), None),
            P(("wide", "narrow"), None),
            P(("wide", "narrow"), None),
            P(("wide", "narrow"), None),
            P(("wide", "narrow"), None),
            P(("wide", "narrow"), None),
            P(None, ("wide", "narrow")),
            P(("wide", "narrow"), None),
            P(("wide", "narrow"), None),
            P(("wide", "narrow"), None),
            P(("wide", "narrow"), None),
            P(None, ("wide", "narrow")),
        ),
        check_vma=False,
    )
```

time: 918 us -> 240 us (0.26)
  waiting for transfers between devices: 487 us -> 67.7 us
  local copies, waits for them, and re-layouts: 152 us -> 11.4 us
  blocking collectives: 149 us -> 23.2 us
  matrix products: 75.2 us -> 13.9 us
  Pallas kernels: 0 us -> 59.1 us
  starting transfers between devices: 0.33 us -> 51.5 us
  between operations: 20.3 us -> 1.77 us
  other arithmetic: 24 us -> 8.69 us
    reduce_scatter x4 -> x0, waiting for transfers between devices: 360 us -> none  [the longest x1 139 us: per_device(): lax.psum_scatter(mlp_parts[1], ('wide', 'narrow'), scatter_dimension=0, t...]
    all_gather x4 -> x0, waiting for transfers between devices: 127 us -> none  [the longest x1 62.6 us: per_device(): lax.all_gather(low_masters[2], ('wide', 'narrow'), axis=0, tiled=True)]
    scatter x2 -> x0, local copies, waits for them, and re-layouts: 105 us -> none  [the longest x1 52.6 us: per_device(): back_blocks.at[seq_index, picks].set(grad_rows).reshape(cotangent.shape)]
    all_gather x1 -> x0, blocking collectives: 69.9 us -> none  [per_device(): lax.all_gather(low_masters[4], ('wide', 'narrow'), axis=1, tiled=True)]
    ppermute x0 -> x54, waiting for transfers between devices: none -> 67.7 us  [swap(): return lax.ppermute(array, AXES, [(i, i ^ bit) for i in range(count)])]
    dot_general x18 -> x4, matrix products: 75.2 us -> 13.9 us  [the longest x2 9.55 us: place(): jnp.einsum('skl,skd->sld', hot_low, rows, preferred_element_type=f32)]
    pallas_call x0 -> x25, Pallas kernels: none -> 59.1 us  [kernel(): pl.pallas_call(body, out_shape=[jax.ShapeDtypeStruct(*out) if place < hel...]
    ppermute x0 -> x54, starting transfers between devices: none -> 51.5 us  [swap(): return lax.ppermute(array, AXES, [(i, i ^ bit) for i in range(count)])]
  transfers between devices with their start and end apart: 8 -> 54, of which waited for: 6 -> 24; matrix products, arithmetic and copies ran while one was open for 17% -> 9% of each run, Pallas kernels for 0% -> 14%
where the time goes in v1:
time: 240 us; the launch traced here: 237 us
  waiting for transfers between devices  67.7 us (28%)
  Pallas kernels  59.1 us (25%)
  starting transfers between devices  51.5 us (21%)
  blocking collectives  23.2 us (10%)
  matrix products  13.9 us (6%)
  local copies, waits for them, and re-layouts  11.4 us (5%)
  other arithmetic  8.69 us (4%)
    ppermute x54, waiting for transfers between devices, swap(): return lax.ppermute(array, AXES, [(i, i ^ bit) for i in range(count)])  67.7 us
    pallas_call x25, Pallas kernels, kernel(): pl.pallas_call(body, out_shape=[jax.ShapeDtypeStruct(*out) if place < hel...  59.1 us
    ppermute x54, starting transfers between devices, swap(): return lax.ppermute(array, AXES, [(i, i ^ bit) for i in range(count)])  51.5 us
    all_to_all x1, blocking collectives, per_device(): lax.all_to_all(vec_parts, AXES, 0, 0, tiled=True)  11.8 us
    all_to_all x1, blocking collectives, per_device(): squares = lax.all_to_all(squares, AXES, 0, 0, tiled=True)  11.4 us
    dot_general x2, matrix products, place(): jnp.einsum('skl,skd->sld', hot_low, rows, preferred_element_type=f32)  9.55 us
    unnamed x116, local copies, waits for them, and re-layouts  7.93 us
  transfers between devices with their start and end apart: 54, of which 24 were waited for; matrix products, arithmetic and copies ran while one was open for 9% of the time, Pallas kernels for 14%

profile of v1, /device:TPU:0, one launch (start us, length us, event | category | flops | bytes accessed | tf_op | source)
XLA Modules:
  0.0 237.2 jit_solution(5276912904359474605)
XLA Ops:
  3.3 3.1 %collective-permute-start = (bf16[24,3200]{1,0:T(8,128)(2,1)S(1)}, bf16[24,3200]{1,0:T(8,128)(2,1)S(1)}, u32[]{:S(2)}, u32[]{:S(2)}) collective-permute-start(bf16[24,3200]{1,0:T(8,128)(2,1)S(1)} %fusion.10.refs_0_), channel_id=1, source_target_pairs={{0,1},{1,0},{2,3},{3,2},{4,5},{5,4},{6,7},{7,6},{8,9},{9,8},{10,11... | collective-permute-start | bytes 460808 | tf_op jit(solution)/shard_map/ppermute | solution.py:713
  6.4 2.6 %collective-permute-start.1 = (bf16[24,3200]{1,0:T(8,128)(2,1)S(1)}, bf16[24,3200]{1,0:T(8,128)(2,1)S(1)}, u32[]{:S(2)}, u32[]{:S(2)}) collective-permute-start(bf16[24,3200]{1,0:T(8,128)(2,1)S(1)} %fusion.10.refs_0_), channel_id=1, source_target_pairs={{0,2},{1,3},{2,0},{3,1},{4,6},{5,7},{6,4},{7,5},{8,10},{9,11},{10,... | collective-permute-start | bytes 460808 | tf_op jit(solution)/shard_map/ppermute | solution.py:713
  9.0 3.4 %fusion.3 = bf16[3,128,768]{2,1,0:T(8,128)(2,1)S(1)} fusion(bf16[3,1024,768]{2,1,0:T(8,128)(2,1)} %bitcast.76, s32[3,128]{1,0:T(4,128)} %param.22), kind=kOutput, calls=%fused_computation.7 | convolution fusion | flops 604667904 | bytes 5309952 | tf_op jit(solution)/shard_map/skl,sld->skd/dot_general | solution.py:844
  14.6 6.2 %collective-permute-done.1.refs_2_ = bf16[24,3200]{1,0:T(8,128)(2,1)S(1)} collective-permute-done((bf16[24,3200]{1,0:T(8,128)(2,1)S(1)}, bf16[24,3200]{1,0:T(8,128)(2,1)S(1)}, u32[]{:S(2)}, u32[]{:S(2)}) %collective-permute-start.1) | collective-permute-done | bytes 153632 | tf_op jit(solution)/shard_map/ppermute | solution.py:713
  20.9 1.6 collective-permute-start.4
  22.5 1.6 collective-permute-start.3
  24.1 3.4 %collective-permute-start.5 = (bf16[24,3072]{1,0:T(8,128)(2,1)S(1)}, bf16[24,3072]{1,0:T(8,128)(2,1)S(1)}, u32[]{:S(2)}, u32[]{:S(2)}) collective-permute-start(bf16[24,3072]{1,0:T(8,128)(2,1)S(1)} %convert_element_type.24.refs_0_), channel_id=1, source_target_pairs={{0,2},{1,3},{2,0},{3,1},{4,6},{5,7},{6,4},{7,5},{8,10},{9,11},{10,... | collective-permute-start | bytes 442376 | tf_op jit(solution)/shard_map/ppermute | solution.py:713
  28.7 3.3 %collective-permute-done.6.refs_1_ = bf16[96,384]{1,0:T(8,128)(2,1)S(1)} collective-permute-done((bf16[96,384]{1,0:T(8,128)(2,1)S(1)}, bf16[96,384]{1,0:T(8,128)(2,1)S(1)}, u32[]{:S(2)}, u32[]{:S(2)}) %collective-permute-start.6) | collective-permute-done | bytes 73760 | tf_op jit(solution)/shard_map/ppermute | solution.py:713
  35.1 1.7 collective-permute-start.12
  36.9 7.3 %collective-permute-done.12 = bf16[2,24,3072]{2,1,0:T(8,128)(2,1)S(1)} collective-permute-done((bf16[2,24,3072]{2,1,0:T(8,128)(2,1)S(1)}, bf16[2,24,3072]{2,1,0:T(8,128)(2,1)S(1)}, u32[]{:S(2)}, u32[]{:S(2)}) %collective-permute-start.12) | collective-permute-done | bytes 294944 | tf_op jit(solution)/shard_map/ppermute | solution.py:713
  44.1 2.8 %collective-permute-start.17 = (bf16[4,96,384]{2,1,0:T(8,128)(2,1)S(1)}, bf16[4,96,384]{2,1,0:T(8,128)(2,1)S(1)}, u32[]{:S(2)}, u32[]{:S(2)}) collective-permute-start(bf16[4,96,384]{2,1,0:T(8,128)(2,1)S(1)} %get-tuple-element.470), channel_id=1, source_target_pairs={{0,2},{1,3},{2,0},{3,1},{4,6},{5,7},{6,4},{7,5},{8,10},{9,11},{10,... | collective-permute-start | bytes 884744 | tf_op jit(solution)/shard_map/ppermute | solution.py:713
  47.0 3.2 %collective-permute-done.8.refs_2_ = bf16[2,96,1536]{2,1,0:T(8,128)(2,1)S(1)} collective-permute-done((bf16[2,96,1536]{2,1,0:T(8,128)(2,1)S(1)}, bf16[2,96,1536]{2,1,0:T(8,128)(2,1)S(1)}, u32[]{:S(2)}, u32[]{:S(2)}) %collective-permute-start.8) | collective-permute-done | bytes 589856 | tf_op jit(solution)/shard_map/ppermute | solution.py:713
  52.8 6.9 %collective-permute-done.17.refs_5_ = bf16[4,96,384]{2,1,0:T(8,128)(2,1)S(1)} collective-permute-done((bf16[4,96,384]{2,1,0:T(8,128)(2,1)S(1)}, bf16[4,96,384]{2,1,0:T(8,128)(2,1)S(1)}, u32[]{:S(2)}, u32[]{:S(2)}) %collective-permute-start.17) | collective-permute-done | bytes 294944 | tf_op jit(solution)/shard_map/ppermute | solution.py:713
  62.8 1.4 collective-permute-start.22
  66.0 8.0 %attend.1 = (bf16[2,384,384]{2,1,0:T(8,128)(2,1)S(1)}, bf16[6,384,384]{2,1,0:T(8,128)(2,1)S(1)}, bf16[384,768]{1,0:T(8,128)(2,1)S(1)}, f32[384,128]{1,0:T(8,128)...) custom-call(s32[1]{0:T(128)} %bitcast.25.me_ref, ...), custom_call_target="tpu_custom_call" | custom-call | tf_op jit(solution)/shard_map/attend/pallas_call | solution.py:55
  74.0 4.9 %collective-permute-done.22 = bf16[2,4,96,384]{3,2,1,0:T(8,128)(2,1)} collective-permute-done((bf16[2,4,96,384]{3,2,1,0:T(8,128)(2,1)}, bf16[2,4,96,384]{3,2,1,0:T(8,128)(2,1)}, u32[]{:S(2)}, u32[]{:S(2)}) %collective-permute-start.22) | collective-permute-done | bytes 589856 | tf_op jit(solution)/shard_map/ppermute | solution.py:713
  78.9 2.0 collective-permute-done.18.refs_2_
  87.0 10.1 %climb.1 = (bf16[384,1536]{1,0:T(8,128)(2,1)S(1)}, bf16[384,1536]{1,0:T(8,128)(2,1)S(1)}, bf16[384,1536]{1,0:T(8,128)(2,1)S(1)}, bf16[2,384,384]{2,1,0:T(8,128)(...) custom-call(s32[1]{0:T(128)} %bitcast.25.me_ref, bf16[2,96,1536]{2,1,0:T(8,128)(2,1)} %pad_maximum_fusion.2.refs_0_, ...), custom_call_target="tpu_custom_call" | custom-call | tf_op jit(solution)/shard_map/climb/pallas_call | solution.py:55
  97.3 2.6 %outer_c.1 = (bf16[2,384,384]{2,1,0:T(8,128)(2,1)S(1)}, bf16[2,384,384]{2,1,0:T(8,128)(2,1)S(1)}, f32[2,384,384]{2,1,0:T(8,128)S(1)}, f32[2,384,384]{2,1,0:T(8,128)S(1)}) custom-call(bf16[384,1536]{1,0:T(8,128)(2,1)S(1)} %get-tuple-element.368.refs_0_.own_ref, bf16[384,768]{1,0:T(8,128)(2,1)S(1)} %get-tuple-element.317.refs_1_.refs_9_, ...), custom_call_target="tpu_custom_call" | custom-call | tf_op jit(solution)/shard_map/outer_c/pallas_call | solution.py:55
  100.6 1.5 collective-permute-done.30.refs_6_
  103.8 7.1 %descend.1 = (bf16[384,3072]{1,0:T(8,128)(2,1)S(1)}, bf16[3072,768]{1,0:T(8,128)(2,1)}) custom-call(s32[1]{0:T(128)} %bitcast.25.me_ref, bf16[2,384,384]{2,1,0:T(8,128)(2,1)} %copy-done.11, bf16[2,384,384]{2,1,0:T(8,128)(2,1)} %copy-done.12, bf16[2,384,384]{2,1,0:T(8,128)(2,1)} %copy-done.44, bf16[2,384,384]{2,1,0:T(8,128)(2,1)} %copy-done.45, ...), custom_call_target="tpu_custom_call" | custom-call | tf_op jit(solution)/shard_map/descend/pallas_call | solution.py:55
  112.7 2.4 %unclimb.1 = (f32[384,768]{1,0:T(8,128)S(1)}, bf16[384,768]{1,0:T(8,128)(2,1)S(1)}, f32[8,768]{1,0:T(8,128)S(1)}) custom-call(bf16[768,3072]{1,0:T(8,128)(2,1)S(1)} %bitcast.63, bf16[384,3072]{1,0:T(8,128)(2,1)S(1)} %get-tuple-element.333.du_ref.refs_1_, bf16[384,768]{1,0:T(8,128)(2,1)S(1)} %bitcast.53, f32[384,768]{1,0:T(8,128)S(1)} %get-tuple-element.337.add_ref, ...), custom_call_target="tpu_custom_call" | custom-call | tf_op jit(solution)/shard_map/unclimb/pallas_call | solution.py:55
  115.1 11.6 %collective-permute-done.33.other_l = bf16[2,384,384]{2,1,0:T(8,128)(2,1)S(1)} collective-permute-done((bf16[2,384,384]{2,1,0:T(8,128)(2,1)S(1)}, bf16[2,384,384]{2,1,0:T(8,128)(2,1)S(1)}, u32[]{:S(2)}, u32[]{:S(2)}) %collective-permute-start.33) | collective-permute-done | bytes 589856 | tf_op jit(solution)/shard_map/ppermute | solution.py:713
  127.1 2.6 %outer_b.1 = (bf16[2,96,1536]{2,1,0:T(8,128)(2,1)S(1)}, bf16[2,96,1536]{2,1,0:T(8,128)(2,1)S(1)}, f32[2,96,1536]{2,1,0:T(8,128)S(1)}, f32[2,96,1536]{2,1,0:T(8,128)S(1)}) custom-call(bf16[2,384,384]{2,1,0:T(8,128)(2,1)S(1)} %get-tuple-element.311.refs_0_.refs_2_, bf16[384,3072]{1,0:T(8,128)(2,1)S(1)} %get-tuple-element.333.du_ref.refs_1_, ...), custom_call_target="tpu_custom_call" | custom-call | tf_op jit(solution)/shard_map/outer_b/pallas_call | solution.py:55
  131.7 6.2 %unattend.1.refs_1_.dqkv_ref = bf16[384,2304]{1,0:T(8,128)(2,1)S(1)} custom-call(bf16[768,768]{1,0:T(8,128)(2,1)S(1)} %copy-done.7, bf16[384,768]{1,0:T(8,128)(2,1)S(1)} %get-tuple-element.351.da_ref.refs_5_, bf16[384,2304]{1,0:T(8,128)(2,1)S(1)} %copy-done.2, f32[18,256,128]{2,1,0:T(8,128)S(1)} %copy-done.1), custom_call_target="tpu_custom_call" | custom-call | tf_op jit(solution)/shard_map/unattend/pallas_call | solution.py:55
  138.5 1.3 collective-permute-start.39
  142.5 3.5 %outer_a.1 = (bf16[2,96,1536]{2,1,0:T(8,128)(2,1)}, bf16[2,96,1536]{2,1,0:T(8,128)(2,1)}, f32[2,96,1536]{2,1,0:T(8,128)S(1)}, f32[2,96,1536]{2,1,0:T(8,128)S(1)}) custom-call(bf16[2,384,384]{2,1,0:T(8,128)(2,1)S(1)} %get-tuple-element.295.refs_0_.refs_4_, bf16[384,2304]{1,0:T(8,128)(2,1)S(1)} %unattend.1.refs_1_.dqkv_ref, ...), custom_call_target="tpu_custom_call" | custom-call | tf_op jit(solution)/shard_map/outer_a/pallas_call | solution.py:55
  146.0 2.4 finish_mlp.1
  148.4 2.0 finish_rows.1
  150.4 3.4 %collective-permute-done.39.other_l = bf16[2,96,1536]{2,1,0:T(8,128)(2,1)S(1)} collective-permute-done((bf16[2,96,1536]{2,1,0:T(8,128)(2,1)S(1)}, bf16[2,96,1536]{2,1,0:T(8,128)(2,1)S(1)}, u32[]{:S(2)}, u32[]{:S(2)}) %collective-permute-start.39) | collective-permute-done | bytes 589856 | tf_op jit(solution)/shard_map/ppermute | solution.py:713
  156.9 1.2 add_z_pairs.3
  161.1 1.4 reshape.190
  162.5 2.8 %collective-permute-start.43 = (bf16[4,96,384]{2,1,0:T(8,128)(2,1)}, bf16[4,96,384]{2,1,0:T(8,128)(2,1)S(1)}, u32[]{:S(2)}, u32[]{:S(2)}) collective-permute-start(bf16[4,96,384]{2,1,0:T(8,128)(2,1)} %copy-done.32), channel_id=1, source_target_pairs={{0,2},{1,3},{2,0},{3,1},{4,6},{5,7},{6,4},{7,5},{8,10},{9,11},{10,... | collective-permute-start | bytes 884744 | tf_op jit(solution)/shard_map/ppermute | solution.py:713
  165.4 4.8 %convert_select_fusion.1 = bf16[3,1024,768]{2,1,0:T(8,128)(2,1)} fusion(bf16[3,1024,768]{2,1,0:T(8,128)(2,1)} %bitcast.77, pred[3,1024]{1,0:T(4,128)(4,1)S(1)} %fusion, bf16[3,128,768]{2,1,0:T(8,128)(2,1)S(1)} %bitcast.67, s32[3,128]{1,0:T(4,128)S(1)} %copy-done.37), kind=kOutput, calls=%fused_computation.1 | convolution fusion | flops 609091584 | bytes 10031616 | tf_op jit(solution)/shard_map/skl,skd->sld/dot_general | solution.py:849
  170.2 6.8 %collective-permute-done.43.other = bf16[4,96,384]{2,1,0:T(8,128)(2,1)S(1)} collective-permute-done((bf16[4,96,384]{2,1,0:T(8,128)(2,1)}, bf16[4,96,384]{2,1,0:T(8,128)(2,1)S(1)}, u32[]{:S(2)}, u32[]{:S(2)}) %collective-permute-start.43) | collective-permute-done | bytes 294944 | tf_op jit(solution)/shard_map/ppermute | solution.py:713
  177.0 1.5 collective-permute-done.42.other
  180.0 1.9 add_next.3
  181.8 2.2 add_pairs.1
  184.9 1.3 collective-permute-start.44
  189.1 1.5 collective-permute-start.48
  190.7 11.8 %all_to_all.13 = f32[32,3,24]{2,1,0:T(4,128)} all-to-all(f32[32,3,24]{2,1,0:T(4,128)S(1)} %copy.48), channel_id=1, replica_groups=mesh['wide'=8,'narrow'=4] {'wide','narrow'}, dimensions={0} | all-to-all | bytes 18432 | tf_op jit(solution)/shard_map/all_to_all | solution.py:941
  207.1 2.7 %collective-permute-start.50 = (bf16[24,3072]{1,0:T(8,128)(2,1)S(1)}, bf16[24,3072]{1,0:T(8,128)(2,1)S(1)}, u32[]{:S(2)}, u32[]{:S(2)}) collective-permute-start(bf16[24,3072]{1,0:T(8,128)(2,1)S(1)} %get-tuple-element.426), channel_id=1, source_target_pairs={{0,2},{1,3},{2,0},{3,1},{4,6},{5,7},{6,4},{7,5},{8,10},{9,11},{10,... | collective-permute-start | bytes 442376 | tf_op jit(solution)/shard_map/ppermute | solution.py:713
  210.8 1.4 collective-permute-start.52
  212.9 4.7 %convert_select_fusion = bf16[3,1024,768]{2,1,0:T(8,128)(2,1)} fusion(bf16[3,1024,768]{2,1,0:T(8,128)(2,1)} %bitcast.78, pred[3,1024]{1,0:T(4,128)(4,1)S(1)} %fusion, bf16[3,128,768]{2,1,0:T(8,128)(2,1)S(1)} %bitcast.66, s32[3,128]{1,0:T(4,128)S(1)} %copy-done.37), kind=kOutput, calls=%fused_computation | convolution fusion | flops 609091584 | bytes 10031616 | tf_op jit(solution)/shard_map/skl,skd->sld/dot_general | solution.py:849
  217.7 1.2 settle_halves.3
  219.0 2.1 collective-permute-done.50.two
  222.8 11.4 %all_to_all.14 = f32[32,1,128]{2,1,0:T(1,128)S(1)} all-to-all(f32[32,1,128]{2,1,0:T(1,128)S(1)} %broadcast_in_dim.45), channel_id=1, replica_groups=mesh['wide'=8,'narrow'=4] {'wide','narrow'}, dimensions={0} | all-to-all | bytes 32768 | tf_op jit(solution)/shard_map/all_to_all | solution.py:950
  234.3 2.2 update.1
  (245 shorter events, 52.4 us)
Async XLA Ops:
  3.3 11.3 %collective-permute-start = (bf16[24,3200]{1,0:T(8,128)(2,1)S(1)}, bf16[24,3200]{1,0:T(8,128)(2,1)S(1)}, u32[]{:S(2)}, u32[]{:S(2)}) collective-permute-start(bf16[24,3200]{1,0:T(8,128)(2,1)S(1)} %fusion.10.refs_0_), channel_id=1, source_target_pairs={{0,1},{1,0},{2,3},{3,2},{4,5},{5,4},{6,7},{7,6},{8,9},{9,8},{10,11... | collective-permute-start | bytes 460808 | tf_op jit(solution)/shard_map/ppermute | solution.py:713
  6.4 14.4 %collective-permute-start.1 = (bf16[24,3200]{1,0:T(8,128)(2,1)S(1)}, bf16[24,3200]{1,0:T(8,128)(2,1)S(1)}, u32[]{:S(2)}, u32[]{:S(2)}) collective-permute-start(bf16[24,3200]{1,0:T(8,128)(2,1)S(1)} %fusion.10.refs_0_), channel_id=1, source_target_pairs={{0,2},{1,3},{2,0},{3,1},{4,6},{5,7},{6,4},{7,5},{8,10},{9,11},{10,... | collective-permute-start | bytes 460808 | tf_op jit(solution)/shard_map/ppermute | solution.py:713
  9.0 11.8 %collective-permute-start.2 = (bf16[24,3200]{1,0:T(8,128)(2,1)S(1)}, bf16[24,3200]{1,0:T(8,128)(2,1)S(1)}, u32[]{:S(2)}, u32[]{:S(2)}) collective-permute-start(bf16[24,3200]{1,0:T(8,128)(2,1)S(1)} %fusion.10.refs_0_), channel_id=1, source_target_pairs={{0,3},{1,2},{2,1},{3,0},{4,7},{5,6},{6,5},{7,4},{8,11},{9,10},{10,... | collective-permute-start | bytes 460808 | tf_op jit(solution)/shard_map/ppermute | solution.py:713
  20.9 12.1 %collective-permute-start.4 = (bf16[96,1664]{1,0:T(8,128)(2,1)S(1)}, bf16[96,1664]{1,0:T(8,128)(2,1)S(1)}, u32[]{:S(2)}, u32[]{:S(2)}) collective-permute-start(bf16[96,1664]{1,0:T(8,128)(2,1)S(1)} %get-tuple-element.246), channel_id=1, source_target_pairs={{0,16},{1,17},{2,18},{3,19},{4,20},{5,21},{6,22},{7,23},{8,24},{9,... | collective-permute-start | bytes 958472 | tf_op jit(solution)/shard_map/ppermute | solution.py:713
  22.5 10.5 %collective-permute-start.3 = (bf16[96,1536]{1,0:T(8,128)(2,1)S(1)}, bf16[96,1536]{1,0:T(8,128)(2,1)S(1)}, u32[]{:S(2)}, u32[]{:S(2)}) collective-permute-start(bf16[96,1536]{1,0:T(8,128)(2,1)S(1)} %get-tuple-element.245), channel_id=1, source_target_pairs={{0,8},{1,9},{2,10},{3,11},{4,12},{5,13},{6,14},{7,15},{8,0},{9,1},... | collective-permute-start | bytes 884744 | tf_op jit(solution)/shard_map/ppermute | solution.py:713
  24.1 8.9 %collective-permute-start.5 = (bf16[24,3072]{1,0:T(8,128)(2,1)S(1)}, bf16[24,3072]{1,0:T(8,128)(2,1)S(1)}, u32[]{:S(2)}, u32[]{:S(2)}) collective-permute-start(bf16[24,3072]{1,0:T(8,128)(2,1)S(1)} %convert_element_type.24.refs_0_), channel_id=1, source_target_pairs={{0,2},{1,3},{2,0},{3,1},{4,6},{5,7},{6,4},{7,5},{8,10},{9,11},{10,... | collective-permute-start | bytes 442376 | tf_op jit(solution)/shard_map/ppermute | solution.py:713
  33.1 17.0 %collective-permute-start.11 = (bf16[2,96,1664]{2,1,0:T(8,128)(2,1)S(1)}, bf16[2,96,1664]{2,1,0:T(8,128)(2,1)S(1)}, u32[]{:S(2)}, u32[]{:S(2)}) collective-permute-start(bf16[2,96,1664]{2,1,0:T(8,128)(2,1)S(1)} %pad_maximum_fusion.refs_1_), channel_id=1, source_target_pairs={{0,4},{1,5},{2,6},{3,7},{4,0},{5,1},{6,2},{7,3},{8,12},{9,13},{10,... | collective-permute-start | bytes 1916936 | tf_op jit(solution)/shard_map/ppermute | solution.py:713
  33.2 16.9 %collective-permute-start.9 = (bf16[2,96,1664]{2,1,0:T(8,128)(2,1)S(1)}, bf16[2,96,1664]{2,1,0:T(8,128)(2,1)S(1)}, u32[]{:S(2)}, u32[]{:S(2)}) collective-permute-start(bf16[2,96,1664]{2,1,0:T(8,128)(2,1)S(1)} %pad_maximum_fusion.refs_1_), channel_id=1, source_target_pairs={{0,8},{1,9},{2,10},{3,11},{4,12},{5,13},{6,14},{7,15},{8,0},{9,1},... | collective-permute-start | bytes 1916936 | tf_op jit(solution)/shard_map/ppermute | solution.py:713
  34.3 12.6 %collective-permute-start.10 = (bf16[2,96,1536]{2,1,0:T(8,128)(2,1)S(1)}, bf16[2,96,1536]{2,1,0:T(8,128)(2,1)S(1)}, u32[]{:S(2)}, u32[]{:S(2)}) collective-permute-start(bf16[2,96,1536]{2,1,0:T(8,128)(2,1)S(1)} %pad_maximum_fusion.1.refs_0_), channel_id=1, source_target_pairs={{0,4},{1,5},{2,6},{3,7},{4,0},{5,1},{6,2},{7,3},{8,12},{9,13},{10,... | collective-permute-start | bytes 1769480 | tf_op jit(solution)/shard_map/ppermute | solution.py:713
  34.6 15.6 %collective-permute-start.8 = (bf16[2,96,1536]{2,1,0:T(8,128)(2,1)S(1)}, bf16[2,96,1536]{2,1,0:T(8,128)(2,1)S(1)}, u32[]{:S(2)}, u32[]{:S(2)}) collective-permute-start(bf16[2,96,1536]{2,1,0:T(8,128)(2,1)S(1)} %pad_maximum_fusion.1.refs_0_), channel_id=1, source_target_pairs={{0,16},{1,17},{2,18},{3,19},{4,20},{5,21},{6,22},{7,23},{8,24},{9,... | collective-permute-start | bytes 1769480 | tf_op jit(solution)/shard_map/ppermute | solution.py:713
  35.1 9.0 %collective-permute-start.12 = (bf16[2,24,3072]{2,1,0:T(8,128)(2,1)S(1)}, bf16[2,24,3072]{2,1,0:T(8,128)(2,1)S(1)}, u32[]{:S(2)}, u32[]{:S(2)}) collective-permute-start(bf16[2,24,3072]{2,1,0:T(8,128)(2,1)S(1)} %pad_maximum_fusion.6), channel_id=1, source_target_pairs={{0,1},{1,0},{2,3},{3,2},{4,5},{5,4},{6,7},{7,6},{8,9},{9,8},{10,11... | collective-permute-start | bytes 884744 | tf_op jit(solution)/shard_map/ppermute | solution.py:713
  44.1 15.5 %collective-permute-start.17 = (bf16[4,96,384]{2,1,0:T(8,128)(2,1)S(1)}, bf16[4,96,384]{2,1,0:T(8,128)(2,1)S(1)}, u32[]{:S(2)}, u32[]{:S(2)}) collective-permute-start(bf16[4,96,384]{2,1,0:T(8,128)(2,1)S(1)} %get-tuple-element.470), channel_id=1, source_target_pairs={{0,2},{1,3},{2,0},{3,1},{4,6},{5,7},{6,4},{7,5},{8,10},{9,11},{10,... | collective-permute-start | bytes 884744 | tf_op jit(solution)/shard_map/ppermute | solution.py:713
  50.2 10.6 %collective-permute-start.14 = (bf16[2,96,1664]{2,1,0:T(8,128)(2,1)S(1)}, bf16[2,96,1664]{2,1,0:T(8,128)(2,1)S(1)}, u32[]{:S(2)}, u32[]{:S(2)}) collective-permute-start(bf16[2,96,1664]{2,1,0:T(8,128)(2,1)S(1)} %collective-permute-done.9.refs_3_), channel_id=1, source_target_pairs={{0,4},{1,5},{2,6},{3,7},{4,0},{5,1},{6,2},{7,3},{8,12},{9,13},{10,... | collective-permute-start | bytes 1916936 | tf_op jit(solution)/shard_map/ppermute | solution.py:713
  50.2 10.5 %collective-permute-start.13 = (bf16[2,96,1536]{2,1,0:T(8,128)(2,1)S(1)}, bf16[2,96,1536]{2,1,0:T(8,128)(2,1)S(1)}, u32[]{:S(2)}, u32[]{:S(2)}) collective-permute-start(bf16[2,96,1536]{2,1,0:T(8,128)(2,1)S(1)} %collective-permute-done.8.refs_2_), channel_id=1, source_target_pairs={{0,4},{1,5},{2,6},{3,7},{4,0},{5,1},{6,2},{7,3},{8,12},{9,13},{10,... | collective-permute-start | bytes 1769480 | tf_op jit(solution)/shard_map/ppermute | solution.py:713
  51.2 8.8 %collective-permute-start.15 = (bf16[96,1536]{1,0:T(8,128)(2,1)S(1)}, bf16[96,1536]{1,0:T(8,128)(2,1)S(1)}, u32[]{:S(2)}, u32[]{:S(2)}) collective-permute-start(bf16[96,1536]{1,0:T(8,128)(2,1)S(1)} %get-tuple-element.261), channel_id=1, source_target_pairs={{0,8},{1,9},{2,10},{3,11},{4,12},{5,13},{6,14},{7,15},{8,0},{9,1},... | collective-permute-start | bytes 884744 | tf_op jit(solution)/shard_map/ppermute | solution.py:713
  52.3 8.5 %collective-permute-start.16 = (bf16[96,1536]{1,0:T(8,128)(2,1)S(1)}, bf16[96,1536]{1,0:T(8,128)(2,1)S(1)}, u32[]{:S(2)}, u32[]{:S(2)}) collective-permute-start(bf16[96,1536]{1,0:T(8,128)(2,1)S(1)} %get-tuple-element.264), channel_id=1, source_target_pairs={{0,16},{1,17},{2,18},{3,19},{4,20},{5,21},{6,22},{7,23},{8,24},{9,... | collective-permute-start | bytes 884744 | tf_op jit(solution)/shard_map/ppermute | solution.py:713
  60.9 18.0 %collective-permute-start.19 = (bf16[2,96,1536]{2,1,0:T(8,128)(2,1)S(1)}, bf16[2,96,1536]{2,1,0:T(8,128)(2,1)}, u32[]{:S(2)}, u32[]{:S(2)}) collective-permute-start(bf16[2,96,1536]{2,1,0:T(8,128)(2,1)S(1)} %pad_maximum_fusion.3.refs_1_), channel_id=1, source_target_pairs={{0,8},{1,9},{2,10},{3,11},{4,12},{5,13},{6,14},{7,15},{8,0},{9,1},... | collective-permute-start | bytes 1769480 | tf_op jit(solution)/shard_map/ppermute | solution.py:713
  61.9 16.9 %collective-permute-start.21 = (bf16[2,96,1536]{2,1,0:T(8,128)(2,1)S(1)}, bf16[2,96,1536]{2,1,0:T(8,128)(2,1)}, u32[]{:S(2)}, u32[]{:S(2)}) collective-permute-start(bf16[2,96,1536]{2,1,0:T(8,128)(2,1)S(1)} %pad_maximum_fusion.3.refs_1_), channel_id=1, source_target_pairs={{0,4},{1,5},{2,6},{3,7},{4,0},{5,1},{6,2},{7,3},{8,12},{9,13},{10,... | collective-permute-start | bytes 1769480 | tf_op jit(solution)/shard_map/ppermute | solution.py:713
  62.8 16.1 %collective-permute-start.22 = (bf16[2,4,96,384]{3,2,1,0:T(8,128)(2,1)}, bf16[2,4,96,384]{3,2,1,0:T(8,128)(2,1)}, u32[]{:S(2)}, u32[]{:S(2)}) collective-permute-start(bf16[2,4,96,384]{3,2,1,0:T(8,128)(2,1)} %pad_maximum_fusion.4), channel_id=1, source_target_pairs={{0,1},{1,0},{2,3},{3,2},{4,5},{5,4},{6,7},{7,6},{8,9},{9,8},{10,11... | collective-permute-start | bytes 1769480 | tf_op jit(solution)/shard_map/ppermute | solution.py:713
  65.1 15.8 %collective-permute-start.18 = (bf16[2,96,1536]{2,1,0:T(8,128)(2,1)}, bf16[2,96,1536]{2,1,0:T(8,128)(2,1)}, u32[]{:S(2)}, u32[]{:S(2)}) collective-permute-start(bf16[2,96,1536]{2,1,0:T(8,128)(2,1)} %pad_maximum_fusion.2.refs_0_), channel_id=1, source_target_pairs={{0,16},{1,17},{2,18},{3,19},{4,20},{5,21},{6,22},{7,23},{8,24},{9,... | collective-permute-start | bytes 1769480 | tf_op jit(solution)/shard_map/ppermute | solution.py:713
  65.8 15.1 %collective-permute-start.20 = (bf16[2,96,1536]{2,1,0:T(8,128)(2,1)}, bf16[2,96,1536]{2,1,0:T(8,128)(2,1)}, u32[]{:S(2)}, u32[]{:S(2)}) collective-permute-start(bf16[2,96,1536]{2,1,0:T(8,128)(2,1)} %pad_maximum_fusion.2.refs_0_), channel_id=1, source_target_pairs={{0,4},{1,5},{2,6},{3,7},{4,0},{5,1},{6,2},{7,3},{8,12},{9,13},{10,... | collective-permute-start | bytes 1769480 | tf_op jit(solution)/shard_map/ppermute | solution.py:713
  80.9 5.6 %collective-permute-start.25 = (bf16[6,384,384]{2,1,0:T(8,128)(2,1)S(1)}, bf16[6,384,384]{2,1,0:T(8,128)(2,1)S(1)}, u32[]{:S(2)}, u32[]{:S(2)}) collective-permute-start(bf16[6,384,384]{2,1,0:T(8,128)(2,1)S(1)} %get-tuple-element.301), channel_id=1, source_target_pairs={{0,4},{1,5},{2,6},{3,7},{4,0},{5,1},{6,2},{7,3},{8,12},{9,13},{10,... | collective-permute-start | bytes 5308424 | tf_op jit(solution)/shard_map/ppermute | solution.py:713
  81.4 4.7 %collective-permute-start.24 = (bf16[2,96,1536]{2,1,0:T(8,128)(2,1)}, bf16[2,96,1536]{2,1,0:T(8,128)(2,1)S(1)}, u32[]{:S(2)}, u32[]{:S(2)}) collective-permute-start(bf16[2,96,1536]{2,1,0:T(8,128)(2,1)} %collective-permute-done.19.refs_3_), channel_id=1, source_target_pairs={{0,4},{1,5},{2,6},{3,7},{4,0},{5,1},{6,2},{7,3},{8,12},{9,13},{10,... | collective-permute-start | bytes 1769480 | tf_op jit(solution)/shard_map/ppermute | solution.py:713
  82.7 17.2 %collective-permute-start.26 = (bf16[2,384,384]{2,1,0:T(8,128)(2,1)S(1)}, bf16[2,384,384]{2,1,0:T(8,128)(2,1)S(1)}, u32[]{:S(2)}, u32[]{:S(2)}) collective-permute-start(bf16[2,384,384]{2,1,0:T(8,128)(2,1)S(1)} %get-tuple-element.314.refs_0_), channel_id=1, source_target_pairs={{0,16},{1,17},{2,18},{3,19},{4,20},{5,21},{6,22},{7,23},{8,24},{9,... | collective-permute-start | bytes 1769480 | tf_op jit(solution)/shard_map/ppermute | solution.py:713
  83.4 16.5 %collective-permute-start.27 = (bf16[2,384,384]{2,1,0:T(8,128)(2,1)S(1)}, bf16[2,384,384]{2,1,0:T(8,128)(2,1)S(1)}, u32[]{:S(2)}, u32[]{:S(2)}) collective-permute-start(bf16[2,384,384]{2,1,0:T(8,128)(2,1)S(1)} %get-tuple-element.315.refs_1_), channel_id=1, source_target_pairs={{0,8},{1,9},{2,10},{3,11},{4,12},{5,13},{6,14},{7,15},{8,0},{9,1},... | collective-permute-start | bytes 1769480 | tf_op jit(solution)/shard_map/ppermute | solution.py:713
  85.3 14.7 %collective-permute-start.28 = (bf16[2,384,384]{2,1,0:T(8,128)(2,1)S(1)}, bf16[2,384,384]{2,1,0:T(8,128)(2,1)S(1)}, u32[]{:S(2)}, u32[]{:S(2)}) collective-permute-start(bf16[2,384,384]{2,1,0:T(8,128)(2,1)S(1)} %get-tuple-element.314.refs_0_), channel_id=1, source_target_pairs={{0,4},{1,5},{2,6},{3,7},{4,0},{5,1},{6,2},{7,3},{8,12},{9,13},{10,... | collective-permute-start | bytes 1769480 | tf_op jit(solution)/shard_map/ppermute | solution.py:713
  86.1 13.8 %collective-permute-start.29 = (bf16[2,384,384]{2,1,0:T(8,128)(2,1)S(1)}, bf16[2,384,384]{2,1,0:T(8,128)(2,1)S(1)}, u32[]{:S(2)}, u32[]{:S(2)}) collective-permute-start(bf16[2,384,384]{2,1,0:T(8,128)(2,1)S(1)} %get-tuple-element.315.refs_1_), channel_id=1, source_target_pairs={{0,4},{1,5},{2,6},{3,7},{4,0},{5,1},{6,2},{7,3},{8,12},{9,13},{10,... | collective-permute-start | bytes 1769480 | tf_op jit(solution)/shard_map/ppermute | solution.py:713
  110.9 16.2 %collective-permute-start.32 = (bf16[384,3072]{1,0:T(8,128)(2,1)S(1)}, bf16[384,3072]{1,0:T(8,128)(2,1)S(1)}, u32[]{:S(2)}, u32[]{:S(2)}) collective-permute-start(bf16[384,3072]{1,0:T(8,128)(2,1)S(1)} %get-tuple-element.333.du_ref.refs_1_), channel_id=1, source_target_pairs={{0,4},{1,5},{2,6},{3,7},{4,0},{5,1},{6,2},{7,3},{8,12},{9,13},{10,... | collective-permute-start | bytes 7077896 | tf_op jit(solution)/shard_map/ppermute | solution.py:713
  111.3 15.4 %collective-permute-start.33 = (bf16[2,384,384]{2,1,0:T(8,128)(2,1)S(1)}, bf16[2,384,384]{2,1,0:T(8,128)(2,1)S(1)}, u32[]{:S(2)}, u32[]{:S(2)}) collective-permute-start(bf16[2,384,384]{2,1,0:T(8,128)(2,1)S(1)} %get-tuple-element.334), channel_id=1, source_target_pairs={{0,16},{1,17},{2,18},{3,19},{4,20},{5,21},{6,22},{7,23},{8,24},{9,... | collective-permute-start | bytes 1769480 | tf_op jit(solution)/shard_map/ppermute | solution.py:713
  112.0 15.1 %collective-permute-start.34 = (bf16[2,384,384]{2,1,0:T(8,128)(2,1)S(1)}, bf16[2,384,384]{2,1,0:T(8,128)(2,1)S(1)}, u32[]{:S(2)}, u32[]{:S(2)}) collective-permute-start(bf16[2,384,384]{2,1,0:T(8,128)(2,1)S(1)} %get-tuple-element.335), channel_id=1, source_target_pairs={{0,8},{1,9},{2,10},{3,11},{4,12},{5,13},{6,14},{7,15},{8,0},{9,1},... | collective-permute-start | bytes 1769480 | tf_op jit(solution)/shard_map/ppermute | solution.py:713
  137.9 4.6 %collective-permute-start.35 = (bf16[384,2304]{1,0:T(8,128)(2,1)S(1)}, bf16[384,2304]{1,0:T(8,128)(2,1)S(1)}, u32[]{:S(2)}, u32[]{:S(2)}) collective-permute-start(bf16[384,2304]{1,0:T(8,128)(2,1)S(1)} %unattend.1.refs_1_.dqkv_ref), channel_id=1, source_target_pairs={{0,4},{1,5},{2,6},{3,7},{4,0},{5,1},{6,2},{7,3},{8,12},{9,13},{10,... | collective-permute-start | bytes 5308424 | tf_op jit(solution)/shard_map/ppermute | solution.py:713
  138.5 15.3 %collective-permute-start.39 = (bf16[2,96,1536]{2,1,0:T(8,128)(2,1)S(1)}, bf16[2,96,1536]{2,1,0:T(8,128)(2,1)S(1)}, u32[]{:S(2)}, u32[]{:S(2)}) collective-permute-start(bf16[2,96,1536]{2,1,0:T(8,128)(2,1)S(1)} %get-tuple-element.364), channel_id=1, source_target_pairs={{0,16},{1,17},{2,18},{3,19},{4,20},{5,21},{6,22},{7,23},{8,24},{9,... | collective-permute-start | bytes 1769480 | tf_op jit(solution)/shard_map/ppermute | solution.py:713
  139.8 15.0 %collective-permute-start.40 = (bf16[2,96,1536]{2,1,0:T(8,128)(2,1)S(1)}, bf16[2,96,1536]{2,1,0:T(8,128)(2,1)S(1)}, u32[]{:S(2)}, u32[]{:S(2)}) collective-permute-start(bf16[2,96,1536]{2,1,0:T(8,128)(2,1)S(1)} %get-tuple-element.365), channel_id=1, source_target_pairs={{0,8},{1,9},{2,10},{3,11},{4,12},{5,13},{6,14},{7,15},{8,0},{9,1},... | collective-permute-start | bytes 1769480 | tf_op jit(solution)/shard_map/ppermute | solution.py:713
  140.5 14.8 %collective-permute-start.41 = (bf16[2,4,96,384]{3,2,1,0:T(8,128)(2,1)S(1)}, bf16[2,4,96,384]{3,2,1,0:T(8,128)(2,1)S(1)}, u32[]{:S(2)}, u32[]{:S(2)}) collective-permute-start(bf16[2,4,96,384]{3,2,1,0:T(8,128)(2,1)S(1)} %get-tuple-element.366), channel_id=1, source_target_pairs={{0,1},{1,0},{2,3},{3,2},{4,5},{5,4},{6,7},{7,6},{8,9},{9,8},{10,11... | collective-permute-start | bytes 1769480 | tf_op jit(solution)/shard_map/ppermute | solution.py:713
  158.1 20.5 %collective-permute-start.42 = (bf16[2,4,24,1536]{3,2,1,0:T(8,128)(2,1)}, bf16[2,4,24,1536]{3,2,1,0:T(8,128)(2,1)}, u32[]{:S(2)}, u32[]{:S(2)}) collective-permute-start(bf16[2,4,24,1536]{3,2,1,0:T(8,128)(2,1)} %get-tuple-element.384), channel_id=1, source_target_pairs={{0,1},{1,0},{2,3},{3,2},{4,5},{5,4},{6,7},{7,6},{8,9},{9,8},{10,11... | collective-permute-start | bytes 1769480 | tf_op jit(solution)/shard_map/ppermute | solution.py:713
  159.0 19.5 %collective-permute-start.37 = (bf16[2,96,1536]{2,1,0:T(8,128)(2,1)}, bf16[2,96,1536]{2,1,0:T(8,128)(2,1)}, u32[]{:S(2)}, u32[]{:S(2)}) collective-permute-start(bf16[2,96,1536]{2,1,0:T(8,128)(2,1)} %get-tuple-element.360), channel_id=1, source_target_pairs={{0,16},{1,17},{2,18},{3,19},{4,20},{5,21},{6,22},{7,23},{8,24},{9,... | collective-permute-start | bytes 1769480 | tf_op jit(solution)/shard_map/ppermute | solution.py:713
  159.5 19.0 %collective-permute-start.38 = (bf16[2,96,1536]{2,1,0:T(8,128)(2,1)}, bf16[2,96,1536]{2,1,0:T(8,128)(2,1)}, u32[]{:S(2)}, u32[]{:S(2)}) collective-permute-start(bf16[2,96,1536]{2,1,0:T(8,128)(2,1)} %get-tuple-element.361), channel_id=1, source_target_pairs={{0,8},{1,9},{2,10},{3,11},{4,12},{5,13},{6,14},{7,15},{8,0},{9,1},... | collective-permute-start | bytes 1769480 | tf_op jit(solution)/shard_map/ppermute | solution.py:713
  162.5 14.5 %collective-permute-start.43 = (bf16[4,96,384]{2,1,0:T(8,128)(2,1)}, bf16[4,96,384]{2,1,0:T(8,128)(2,1)S(1)}, u32[]{:S(2)}, u32[]{:S(2)}) collective-permute-start(bf16[4,96,384]{2,1,0:T(8,128)(2,1)} %copy-done.32), channel_id=1, source_target_pairs={{0,2},{1,3},{2,0},{3,1},{4,6},{5,7},{6,4},{7,5},{8,10},{9,11},{10,... | collective-permute-start | bytes 884744 | tf_op jit(solution)/shard_map/ppermute | solution.py:713
  184.9 18.5 %collective-permute-start.44 = (bf16[96,1536]{1,0:T(8,128)(2,1)}, bf16[96,1536]{1,0:T(8,128)(2,1)S(1)}, u32[]{:S(2)}, u32[]{:S(2)}) collective-permute-start(bf16[96,1536]{1,0:T(8,128)(2,1)} %get-tuple-element.408), channel_id=1, source_target_pairs={{0,8},{1,9},{2,10},{3,11},{4,12},{5,13},{6,14},{7,15},{8,0},{9,1},... | collective-permute-start | bytes 884744 | tf_op jit(solution)/shard_map/ppermute | solution.py:713
  186.2 17.9 %collective-permute-start.45 = (bf16[96,1536]{1,0:T(8,128)(2,1)}, bf16[96,1536]{1,0:T(8,128)(2,1)}, u32[]{:S(2)}, u32[]{:S(2)}) collective-permute-start(bf16[96,1536]{1,0:T(8,128)(2,1)} %get-tuple-element.409), channel_id=1, source_target_pairs={{0,16},{1,17},{2,18},{3,19},{4,20},{5,21},{6,22},{7,23},{8,24},{9,... | collective-permute-start | bytes 884744 | tf_op jit(solution)/shard_map/ppermute | solution.py:713
  186.9 17.2 %collective-permute-start.46 = (bf16[4,24,1536]{2,1,0:T(8,128)(2,1)}, bf16[4,24,1536]{2,1,0:T(8,128)(2,1)S(1)}, u32[]{:S(2)}, u32[]{:S(2)}) collective-permute-start(bf16[4,24,1536]{2,1,0:T(8,128)(2,1)} %get-tuple-element.410), channel_id=1, source_target_pairs={{0,2},{1,3},{2,0},{3,1},{4,6},{5,7},{6,4},{7,5},{8,10},{9,11},{10,... | collective-permute-start | bytes 884744 | tf_op jit(solution)/shard_map/ppermute | solution.py:713
  188.1 15.3 %collective-permute-start.47 = (bf16[96,384]{1,0:T(8,128)(2,1)}, bf16[96,384]{1,0:T(8,128)(2,1)}, u32[]{:S(2)}, u32[]{:S(2)}) collective-permute-start(bf16[96,384]{1,0:T(8,128)(2,1)} %get-tuple-element.411), channel_id=1, source_target_pairs={{0,8},{1,9},{2,10},{3,11},{4,12},{5,13},{6,14},{7,15},{8,0},{9,1},... | collective-permute-start | bytes 221192 | tf_op jit(solution)/shard_map/ppermute | solution.py:713
  189.1 14.2 %collective-permute-start.48 = (bf16[96,384]{1,0:T(8,128)(2,1)}, bf16[96,384]{1,0:T(8,128)(2,1)}, u32[]{:S(2)}, u32[]{:S(2)}) collective-permute-start(bf16[96,384]{1,0:T(8,128)(2,1)} %get-tuple-element.412), channel_id=1, source_target_pairs={{0,16},{1,17},{2,18},{3,19},{4,20},{5,21},{6,22},{7,23},{8,24},{9,... | collective-permute-start | bytes 221192 | tf_op jit(solution)/shard_map/ppermute | solution.py:713
  206.3 12.7 %collective-permute-start.49 = (bf16[24,3072]{1,0:T(8,128)(2,1)S(1)}, bf16[24,3072]{1,0:T(8,128)(2,1)S(1)}, u32[]{:S(2)}, u32[]{:S(2)}) collective-permute-start(bf16[24,3072]{1,0:T(8,128)(2,1)S(1)} %get-tuple-element.425), channel_id=1, source_target_pairs={{0,1},{1,0},{2,3},{3,2},{4,5},{5,4},{6,7},{7,6},{8,9},{9,8},{10,11... | collective-permute-start | bytes 442376 | tf_op jit(solution)/shard_map/ppermute | solution.py:713
  207.1 14.0 %collective-permute-start.50 = (bf16[24,3072]{1,0:T(8,128)(2,1)S(1)}, bf16[24,3072]{1,0:T(8,128)(2,1)S(1)}, u32[]{:S(2)}, u32[]{:S(2)}) collective-permute-start(bf16[24,3072]{1,0:T(8,128)(2,1)S(1)} %get-tuple-element.426), channel_id=1, source_target_pairs={{0,2},{1,3},{2,0},{3,1},{4,6},{5,7},{6,4},{7,5},{8,10},{9,11},{10,... | collective-permute-start | bytes 442376 | tf_op jit(solution)/shard_map/ppermute | solution.py:713
  209.7 11.3 %collective-permute-start.51 = (bf16[24,3072]{1,0:T(8,128)(2,1)S(1)}, bf16[24,3072]{1,0:T(8,128)(2,1)S(1)}, u32[]{:S(2)}, u32[]{:S(2)}) collective-permute-start(bf16[24,3072]{1,0:T(8,128)(2,1)S(1)} %get-tuple-element.427), channel_id=1, source_target_pairs={{0,3},{1,2},{2,1},{3,0},{4,7},{5,6},{6,5},{7,4},{8,11},{9,10},{10,... | collective-permute-start | bytes 442376 | tf_op jit(solution)/shard_map/ppermute | solution.py:713
  210.8 8.2 %collective-permute-start.52 = (bf16[24,1536]{1,0:T(8,128)(2,1)S(1)}, bf16[24,1536]{1,0:T(8,128)(2,1)S(1)}, u32[]{:S(2)}, u32[]{:S(2)}) collective-permute-start(bf16[24,1536]{1,0:T(8,128)(2,1)S(1)} %get-tuple-element.428), channel_id=1, source_target_pairs={{0,8},{1,9},{2,10},{3,11},{4,12},{5,13},{6,14},{7,15},{8,0},{9,1},... | collective-permute-start | bytes 221192 | tf_op jit(solution)/shard_map/ppermute | solution.py:713
  212.2 6.8 %collective-permute-start.53 = (bf16[24,1536]{1,0:T(8,128)(2,1)S(1)}, bf16[24,1536]{1,0:T(8,128)(2,1)S(1)}, u32[]{:S(2)}, u32[]{:S(2)}) collective-permute-start(bf16[24,1536]{1,0:T(8,128)(2,1)S(1)} %get-tuple-element.429), channel_id=1, source_target_pairs={{0,16},{1,17},{2,18},{3,19},{4,20},{5,21},{6,22},{7,23},{8,24},{9,... | collective-permute-start | bytes 221192 | tf_op jit(solution)/shard_map/ppermute | solution.py:713
  (64 other events, 534.0 us)

commit v2 on v1

--- a/solution.py
+++ b/solution.py
@@ -50,7 +50,7 @@
 
 
 def kernel(body, name, outs, args, kinds, scratch=(), limit=24, loose=0):
-    spaces = {"s": pltpu.SMEM, "v": pltpu.VMEM, "a": pltpu.HBM}
+    spaces = {"s": pltpu.SMEM, "v": pltpu.VMEM, "h": pltpu.VMEM, "a": pltpu.HBM}
     held = len(outs) - loose
     return pl.pallas_call(
         body,
@@ -65,10 +65,11 @@
         ],
         scratch_shapes=list(scratch),
         compiler_params=pltpu.CompilerParams(vmem_limit_bytes=limit << 20),
+        cost_estimate=pl.CostEstimate(flops=1, bytes_accessed=1, transcendentals=0),
         name=name,
     )(
         *(
-            pltpu.with_memory_space_constraint(arg, pltpu.HBM) if kind == "a" else arg
+            pltpu.with_memory_space_constraint(arg, pltpu.HBM) if kind in "ah" else arg
             for arg, kind in zip(args, kinds)
         )
     )
@@ -140,6 +141,26 @@
 def one_pair(stacked, masks):
     rows = stacked.shape[0] // 2
     return stacked[:rows] * masks[0] + stacked[rows:] * masks[1]
+
+
+def gather_input(w_qkv, w_out, vectors):
+    rows, first = w_qkv.shape
+    second = w_out.shape[1]
+
+    def body(qkv_ref, out_ref, vec_ref, chunk_ref, turned):
+        chunk_ref[:, :first] = qkv_ref[...].astype(bf16)
+        chunk_ref[:, first : first + second] = out_ref[...].astype(bf16)
+        turned[...] = jnp.zeros_like(turned)
+        turned[:3] = vec_ref[...]
+        same = lax.broadcasted_iota(jnp.int32, (rows, rows), 0) == lax.broadcasted_iota(
+            jnp.int32, (rows, rows), 1
+        )
+        columns = dot_nt(same.astype(f32).astype(bf16), turned[...].astype(bf16))
+        chunk_ref[:, first + second :] = columns.astype(bf16)
+
+    outs = [((rows, first + second + 128), bf16)]
+    scratch = [pltpu.VMEM((128, rows), f32)]
+    return kernel(body, "gather_input", outs, (w_qkv, w_out, vectors), "hhh", scratch)[0]
 
 
 def attend(me, pieces, picked, back_rows, seg_row, seg_col, order):
@@ -327,6 +348,27 @@
     return kernel(body, "climb", outs, args, "s" + "a" * 8 + "vvv", scratch, 26, 2)
 
 
+def vector_columns(order, mine, other):
+    width = order.shape[1]
+    half = width // 2
+
+    def body(order_ref, *refs):
+        ins, (left, right, rows) = refs[:6], refs[6:]
+        chosen = one_hot_columns(order_ref)[:, :half]
+        rows[...] = jnp.zeros_like(rows)
+        for place in range(3):
+            rows[place : place + 1] = ins[place][0:1] + ins[3 + place][0:1]
+        columns = rows[...].T.astype(bf16)
+        for part in range(2):
+            left[part] = chosen[part * half : (part + 1) * half]
+            right[part] = columns[part * half : (part + 1) * half]
+
+    outs = [((2, half, half), bf16), ((2, half, 128), bf16)]
+    scratch = [pltpu.VMEM((128, width), f32)]
+    args = (order, *mine, *other)
+    return kernel(body, "vector_columns", outs, args, "v" * 7, scratch)
+
+
 class View:
     def __init__(self, array, columns=None, first=0, lead=None):
         self.array, self.first, self.lead = array, first, lead
@@ -640,13 +682,19 @@
 
 
 def settle_z(mine, others):
-    def body(mine, one, two, three, grad, square):
+    rows, width = mine.shape
+
+    def body(mine, one, two, three, grad, square, last, turned):
         value = mine[...] + one[...].astype(f32) + two[...].astype(f32) + three[...].astype(f32)
         grad[...] = value
         square[...] = jnp.full(square.shape, jnp.sum(value * value))
-
-    outs = [(mine.shape, f32), ((8, 128), f32)]
-    return kernel(body, "settle_z", outs, (mine, *others), "vvvv")
+        turned[...] = jnp.zeros_like(turned)
+        turned[:rows] = value[:, width - 128 :]
+        last[...] = turned[...].T[:8]
+
+    outs = [(mine.shape, f32), ((8, 128), f32), ((8, 128), f32)]
+    scratch = [pltpu.VMEM((128, 128), f32)]
+    return kernel(body, "settle_z", outs, (mine, *others), "vvvv", scratch)
 
 
 def update(squares, limit, grads, states, vec_grad, vec_states):
@@ -664,7 +712,8 @@
             grad = grads[place].read(grad_refs[place], 0, grads[place].columns) * factor
             for ref, value in zip(out_refs[3 * place :], adam_update(w, grad, m, v)):
                 ref[...] = value
-        first, second = moment_update(vec_ref[...] * factor, vec_m[...], vec_v[...])
+        grad = vec_ref[:3, : vec_m.shape[1]] * factor
+        first, second = moment_update(grad, vec_m[...], vec_v[...])
         out_refs[-2][...] = first
         out_refs[-1][...] = second
 
@@ -816,8 +865,7 @@
     z = (lane & 3).reshape(1)
     me = (lane >> 2).reshape(1) if paired else jnp.zeros((1,), jnp.int32)
 
-    turned = jnp.pad(vectors.T, ((0, 0), (0, 125)))
-    chunk_a = jnp.concatenate([w_qkv, w_out, turned], axis=1).astype(bf16)
+    chunk_a = gather_input(w_qkv, w_out, vectors)
     chunk_b = w_up.astype(bf16)
     chunk_c = w_down.astype(bf16)
 
@@ -898,11 +946,16 @@
     slope = tick([take_c], slope)
     all_c = whole(take_c, chunk_c, split_c)
     du, all_down = descend(me, all_c, slope, df)
+    dmiddle, da, dg2 = unclimb(all_up, du, picked, added, gate, back_rows, vec)
+    new_rows, dlogit, dr = finish_mlp(
+        all_down, g_own, g_send, picked, added, gate, back_rows
+    )
+    du, da, dmiddle, new_rows, dlogit = tick([give_c], (du, da, dmiddle, new_rows, dlogit))
     late_u = start(exchange, du)
-    du = stage([late_u], du)
-    dmiddle, da, dg2 = unclimb(all_up, du, picked, added, gate, back_rows, vec)
-    da, dmiddle = tick([late_u, give_c], (da, dmiddle))
+    dqkv = unattend(all_out, da, qkv, probs)
+    dqkv = tick([late_u], dqkv)
     (du_sib,) = late_u.result if paired else (du,)
+    late_q = start(exchange, dqkv, da)
     views = [View(h2_pair, lead=place) for place in range(2)]
     if not paired:
         cols = h2.reshape(h2.shape[0], 4, 2, -1)
@@ -910,42 +963,42 @@
     give_b = give(
         scatter_pairs, "outer_b", [(views[0], View(du), views[1], View(du_sib))], split_b
     )
-    da = stage([give_b, give_c], da)
-    dqkv = unattend(all_out, da, qkv, probs)
-    late_q = start(exchange, dqkv, da)
-    dqkv, dmiddle = tick([late_q], (dqkv, dmiddle))
+    dqkv = stage([give_b, give_c], dqkv)
+    grad_rows, dg1 = finish_rows(all_qkv, dqkv, picked, back_rows, dmiddle, dlogit, vec)
+    late_v = start(exchange, dg1, dg2, dr)
+    dqkv = stage([late_v], dqkv)
+    dqkv = tick([late_q, late_v], dqkv)
     dqkv_sib, da_sib = late_q.result if paired else (dqkv, da)
-    give_a = give(
-        scatter,
-        "outer_a",
-        [
-            (View(own, lead=0), View(dqkv), View(sib, lead=0), View(dqkv_sib)),
-            (View(own, lead=1), View(da), View(sib, lead=1), View(da_sib)),
-        ],
-        split_a,
-    )
-    g_own, dqkv = stage([give_a], (g_own, dqkv))
-    new_rows, dlogit, dr = finish_mlp(
-        all_down, g_own, g_send, picked, added, gate, back_rows
-    )
-    grad_rows, dg1 = finish_rows(all_qkv, dqkv, picked, back_rows, dmiddle, dlogit, vec)
-    new_rows, grad_rows, dg1 = tick([give_b, give_c], (new_rows, grad_rows, dg1))
-    new_rows = stage([give_b, give_c], new_rows)
+    products = [
+        (View(own, lead=0), View(dqkv), View(sib, lead=0), View(dqkv_sib)),
+        (View(own, lead=1), View(da), View(sib, lead=1), View(da_sib)),
+    ]
+    if paired:
+        left, right = vector_columns(order, (dg1, dg2, dr), late_v.result)
+        products.append(tuple(View(array, lead=part) for part in range(2) for array in (left, right)))
+    give_a = give(scatter, "outer_a", products, split_a)
+    grad_rows = stage([give_a], grad_rows)
+    grad_rows = tick([give_b, give_c], grad_rows)
+    grad_rows, new_rows = stage([give_b, give_c], (grad_rows, new_rows))
     mixed_rows = place(tok_blocks, new_rows)
-    grad_vectors = jnp.stack([dg1[0], dg2[0], dr[0]], axis=0)
-    vec_parts = grad_vectors.reshape(3, devices_all, shard_width).transpose(1, 0, 2)
-    mixed_rows, vec_parts, grad_rows = tick(
-        [give_a, give_b, give_c], (mixed_rows, vec_parts, grad_rows)
-    )
-    grad_rows = stage([give_a, give_b, give_c], grad_rows)
-    grad_vec = jnp.sum(lax.all_to_all(vec_parts, AXES, 0, 0, tiled=True), axis=0)
-    grad_rows, grad_vec = tick([give_a, give_b, give_c], (grad_rows, grad_vec))
-    grad_rows = stage([give_a, give_b], grad_rows)
+    grad_rows, mixed_rows = tick([give_a], (grad_rows, mixed_rows))
+    grad_rows = stage([give_a], grad_rows)
+    grad_rows = tick([give_b, give_c], grad_rows)
+    grad_rows = stage([give_b, give_c], grad_rows)
     input_grad = place(back_blocks, grad_rows)
-    input_grad, grad_vec = tick([give_a, give_b], (input_grad, grad_vec))
+    grad_rows = tick([give_a, give_c], input_grad)
+    input_grad = stage([give_a], input_grad)
+    input_grad = tick([give_b], input_grad)
+    input_grad = tick([give_a, give_b], input_grad)
     if paired:
         give_a, give_b, give_c = give_a.result, give_b.result, give_c.result
-    local_sq = give_a[1] + give_b[1] + give_c[1] + jnp.sum(grad_vec * grad_vec)
+        vec_grad = give_a[2]
+        local_sq = give_a[1] + give_b[1] + give_c[1]
+    else:
+        rows = jnp.stack([dg1[0], dg2[0], dr[0]], axis=0)
+        rows = lax.psum_scatter(rows, AXES, scatter_dimension=1, tiled=True)
+        vec_grad = jnp.pad(rows, ((0, 5), (0, 128 - shard_width)))
+        local_sq = give_a[1] + give_b[1] + give_c[1] + jnp.sum(rows * rows)
     squares = jnp.broadcast_to(local_sq[:1], (devices_all, 128))
     squares = lax.all_to_all(squares, AXES, 0, 0, tiled=True)
     params_all = 4 * model_width * model_width + 2 * model_width * ff_width + 3 * model_width
@@ -966,7 +1019,7 @@
             (w_up, m_up, v_up),
             (w_down, m_down, v_down),
         ],
-        grad_vec,
+        vec_grad,
         (m_vectors, v_vectors),
     )
     return (

time: 240 us -> 211 us (0.88)
  blocking collectives: 23.2 us -> 8.87 us
  Pallas kernels: 59.1 us -> 52.8 us
  other arithmetic: 8.69 us -> 3.38 us
  starting transfers between devices: 51.5 us -> 55.4 us
  local copies, waits for them, and re-layouts: 11.4 us -> 7.91 us
  matrix products: 13.9 us -> 10.5 us
    all_to_all x1 -> x0, blocking collectives: 11.8 us -> none  [per_device(): lax.all_to_all(vec_parts, AXES, 0, 0, tiled=True)]
    pallas_call x25 -> x27, Pallas kernels: 59.1 us -> 52.8 us  [kernel(): pl.pallas_call(body, out_shape=[jax.ShapeDtypeStruct(*out) if place < hel...]
    ppermute x54 -> x57, starting transfers between devices: 51.5 us -> 55.4 us  [swap(): return lax.ppermute(array, AXES, [(i, i ^ bit) for i in range(count)])]
    dot_general x2, matrix products: 9.55 us -> 6.11 us  [place(): jnp.einsum('skl,skd->sld', hot_low, rows, preferred_element_type=f32)]
    another operation x4 -> x0, other arithmetic: 3.14 us -> none
    all_to_all x1, blocking collectives: 11.4 us -> 8.87 us  [per_device(): squares = lax.all_to_all(squares, AXES, 0, 0, tiled=True)]
    unnamed x116 -> x94, local copies, waits for them, and re-layouts: 7.93 us -> 6.03 us
    ppermute x54 -> x57, waiting for transfers between devices: 67.7 us -> 68.1 us  [swap(): return lax.ppermute(array, AXES, [(i, i ^ bit) for i in range(count)])]
  transfers between devices with their start and end apart: 54 -> 57, of which waited for: 24 -> 25; matrix products, arithmetic and copies ran while one was open for 9% -> 7% of each run, Pallas kernels for 14% -> 23%
where the time goes in v2:
time: 211 us; the launch traced here: 209 us
  waiting for transfers between devices  68.1 us (32%)
  starting transfers between devices  55.4 us (26%)
  Pallas kernels  52.8 us (25%)
  matrix products  10.5 us (5%)
  blocking collectives  8.87 us (4%)
  local copies, waits for them, and re-layouts  7.91 us (4%)
  other arithmetic  3.38 us (2%)
    ppermute x57, waiting for transfers between devices, swap(): return lax.ppermute(array, AXES, [(i, i ^ bit) for i in range(count)])  68.1 us
    ppermute x57, starting transfers between devices, swap(): return lax.ppermute(array, AXES, [(i, i ^ bit) for i in range(count)])  55.4 us
    pallas_call x27, Pallas kernels, kernel(): pl.pallas_call(body, out_shape=[jax.ShapeDtypeStruct(*out) if place < hel...  52.8 us
    all_to_all x1, blocking collectives, per_device(): squares = lax.all_to_all(squares, AXES, 0, 0, tiled=True)  8.87 us
    dot_general x2, matrix products, place(): jnp.einsum('skl,skd->sld', hot_low, rows, preferred_element_type=f32)  6.11 us
    unnamed x94, local copies, waits for them, and re-layouts  6.03 us
    dot_general x2, matrix products, pick(): jnp.einsum('skl,sld->skd', hot_low, blocks, preferred_element_type=f32)  4.37 us
  transfers between devices with their start and end apart: 57, of which 25 were waited for; matrix products, arithmetic and copies ran while one was open for 7% of the time, Pallas kernels for 23%

profile of v2, /device:TPU:0, one launch (start us, length us, event | category | flops | bytes accessed | tf_op | source)
XLA Modules:
  0.0 208.8 jit_solution(14429854983234006627)
XLA Ops:
  1.8 3.0 %collective-permute-start = (bf16[24,3200]{1,0:T(8,128)(2,1)S(1)}, bf16[24,3200]{1,0:T(8,128)(2,1)S(1)}, u32[]{:S(2)}, u32[]{:S(2)}) collective-permute-start(bf16[24,3200]{1,0:T(8,128)(2,1)S(1)} %gather_input.1.refs_0_), channel_id=1, source_target_pairs={{0,1},{1,0},{2,3},{3,2},{4,5},{5,4},{6,7},{7,6},{8,9},{9,8},{10,11... | collective-permute-start | bytes 460808 | tf_op jit(solution)/shard_map/ppermute | solution.py:762
  4.8 2.6 %collective-permute-start.1 = (bf16[24,3200]{1,0:T(8,128)(2,1)S(1)}, bf16[24,3200]{1,0:T(8,128)(2,1)S(1)}, u32[]{:S(2)}, u32[]{:S(2)}) collective-permute-start(bf16[24,3200]{1,0:T(8,128)(2,1)S(1)} %gather_input.1.refs_0_), channel_id=1, source_target_pairs={{0,2},{1,3},{2,0},{3,1},{4,6},{5,7},{6,4},{7,5},{8,10},{9,11},{10,... | collective-permute-start | bytes 460808 | tf_op jit(solution)/shard_map/ppermute | solution.py:762
  7.4 3.4 %fusion.3 = bf16[3,128,768]{2,1,0:T(8,128)(2,1)S(1)} fusion(bf16[3,1024,768]{2,1,0:T(8,128)(2,1)} %bitcast.72, s32[3,128]{1,0:T(4,128)} %param.22), kind=kOutput, calls=%fused_computation.7 | convolution fusion | flops 604667904 | bytes 5309952 | tf_op jit(solution)/shard_map/skl,sld->skd/dot_general | solution.py:892
  13.0 6.2 %collective-permute-done.1.refs_2_ = bf16[24,3200]{1,0:T(8,128)(2,1)S(1)} collective-permute-done((bf16[24,3200]{1,0:T(8,128)(2,1)S(1)}, bf16[24,3200]{1,0:T(8,128)(2,1)S(1)}, u32[]{:S(2)}, u32[]{:S(2)}) %collective-permute-start.1) | collective-permute-done | bytes 153632 | tf_op jit(solution)/shard_map/ppermute | solution.py:762
  19.4 1.6 collective-permute-start.4
  21.0 1.6 collective-permute-start.3
  22.5 3.4 %collective-permute-start.5 = (bf16[24,3072]{1,0:T(8,128)(2,1)S(1)}, bf16[24,3072]{1,0:T(8,128)(2,1)S(1)}, u32[]{:S(2)}, u32[]{:S(2)}) collective-permute-start(bf16[24,3072]{1,0:T(8,128)(2,1)S(1)} %convert_element_type.21.refs_0_), channel_id=1, source_target_pairs={{0,2},{1,3},{2,0},{3,1},{4,6},{5,7},{6,4},{7,5},{8,10},{9,11},{10,... | collective-permute-start | bytes 442376 | tf_op jit(solution)/shard_map/ppermute | solution.py:762
  27.1 3.3 %collective-permute-done.6.refs_1_ = bf16[96,384]{1,0:T(8,128)(2,1)S(1)} collective-permute-done((bf16[96,384]{1,0:T(8,128)(2,1)S(1)}, bf16[96,384]{1,0:T(8,128)(2,1)S(1)}, u32[]{:S(2)}, u32[]{:S(2)}) %collective-permute-start.6) | collective-permute-done | bytes 73760 | tf_op jit(solution)/shard_map/ppermute | solution.py:762
  33.5 1.7 collective-permute-start.12
  35.3 7.5 %collective-permute-done.12 = bf16[2,24,3072]{2,1,0:T(8,128)(2,1)S(1)} collective-permute-done((bf16[2,24,3072]{2,1,0:T(8,128)(2,1)S(1)}, bf16[2,24,3072]{2,1,0:T(8,128)(2,1)S(1)}, u32[]{:S(2)}, u32[]{:S(2)}) %collective-permute-start.12) | collective-permute-done | bytes 294944 | tf_op jit(solution)/shard_map/ppermute | solution.py:762
  42.8 2.8 %collective-permute-start.17 = (bf16[4,96,384]{2,1,0:T(8,128)(2,1)S(1)}, bf16[4,96,384]{2,1,0:T(8,128)(2,1)S(1)}, u32[]{:S(2)}, u32[]{:S(2)}) collective-permute-start(bf16[4,96,384]{2,1,0:T(8,128)(2,1)S(1)} %get-tuple-element.482), channel_id=1, source_target_pairs={{0,2},{1,3},{2,0},{3,1},{4,6},{5,7},{6,4},{7,5},{8,10},{9,11},{10,... | collective-permute-start | bytes 884744 | tf_op jit(solution)/shard_map/ppermute | solution.py:762
  45.6 2.9 %collective-permute-done.8.refs_2_ = bf16[2,96,1536]{2,1,0:T(8,128)(2,1)S(1)} collective-permute-done((bf16[2,96,1536]{2,1,0:T(8,128)(2,1)S(1)}, bf16[2,96,1536]{2,1,0:T(8,128)(2,1)S(1)}, u32[]{:S(2)}, u32[]{:S(2)}) %collective-permute-start.8) | collective-permute-done | bytes 589856 | tf_op jit(solution)/shard_map/ppermute | solution.py:762
  52.0 6.6 %collective-permute-done.17.refs_5_ = bf16[4,96,384]{2,1,0:T(8,128)(2,1)S(1)} collective-permute-done((bf16[4,96,384]{2,1,0:T(8,128)(2,1)S(1)}, bf16[4,96,384]{2,1,0:T(8,128)(2,1)S(1)}, u32[]{:S(2)}, u32[]{:S(2)}) %collective-permute-start.17) | collective-permute-done | bytes 294944 | tf_op jit(solution)/shard_map/ppermute | solution.py:762
  63.4 1.7 collective-permute-start.22
  65.3 8.0 %attend.1 = (bf16[2,384,384]{2,1,0:T(8,128)(2,1)S(1)}, bf16[6,384,384]{2,1,0:T(8,128)(2,1)S(1)}, bf16[384,768]{1,0:T(8,128)(2,1)S(1)}, f32[384,128]{1,0:T(8,128)...) custom-call(s32[1]{0:T(128)} %bitcast.24.me_ref, ...), custom_call_target="tpu_custom_call" | custom-call | flops 1 | bytes 1 | tf_op jit(solution)/shard_map/attend/pallas_call | solution.py:55
  73.8 3.6 %collective-permute-done.19.refs_3_ = bf16[2,96,1536]{2,1,0:T(8,128)(2,1)} collective-permute-done((bf16[2,96,1536]{2,1,0:T(8,128)(2,1)}, bf16[2,96,1536]{2,1,0:T(8,128)(2,1)}, u32[]{:S(2)}, u32[]{:S(2)}) %collective-permute-start.19) | collective-permute-done | bytes 589856 | tf_op jit(solution)/shard_map/ppermute | solution.py:762
  77.4 1.9 collective-permute-done.22
  81.1 1.6 collective-permute-start.28
  85.4 10.1 %climb.1 = (bf16[384,1536]{1,0:T(8,128)(2,1)S(1)}, bf16[384,1536]{1,0:T(8,128)(2,1)S(1)}, bf16[384,1536]{1,0:T(8,128)(2,1)S(1)}, bf16[2,384,384]{2,1,0:T(8,128)(...) custom-call(s32[1]{0:T(128)} %bitcast.24.me_ref, bf16[2,96,1536]{2,1,0:T(8,128)(2,1)} %copy-done.24, ...), custom_call_target="tpu_custom_call" | custom-call | flops 1 | bytes 1 | tf_op jit(solution)/shard_map/climb/pallas_call | solution.py:55
  95.7 2.6 %outer_c.1 = (bf16[2,384,384]{2,1,0:T(8,128)(2,1)S(1)}, bf16[2,384,384]{2,1,0:T(8,128)(2,1)S(1)}, f32[2,384,384]{2,1,0:T(8,128)S(1)}, f32[2,384,384]{2,1,0:T(8,128)S(1)}) custom-call(bf16[384,1536]{1,0:T(8,128)(2,1)S(1)} %get-tuple-element.316.refs_0_.own_ref, bf16[384,768]{1,0:T(8,128)(2,1)S(1)} %get-tuple-element.317.refs_1_.refs_9_, ...), custom_call_target="tpu_custom_call" | custom-call | flops 1 | bytes 1 | tf_op jit(solution)/shard_map/outer_c/pallas_call | solution.py:55
  99.0 1.5 collective-permute-start.26
  103.2 7.1 %descend.1 = (bf16[384,3072]{1,0:T(8,128)(2,1)S(1)}, bf16[3072,768]{1,0:T(8,128)(2,1)}) custom-call(s32[1]{0:T(128)} %bitcast.24.me_ref, bf16[2,384,384]{2,1,0:T(8,128)(2,1)} %copy-done.8, bf16[2,384,384]{2,1,0:T(8,128)(2,1)} %copy-done.9, bf16[2,384,384]{2,1,0:T(8,128)(2,1)} %copy-done.31, bf16[2,384,384]{2,1,0:T(8,128)(2,1)} %copy-done.33, ...), custom_call_target="tpu_custom_call" | custom-call | flops 1 | bytes 1 | tf_op jit(solution)/shard_map/descend/pallas_call | solution.py:55
  110.3 2.3 %copy-done = bf16[3072,768]{1,0:T(8,128)(2,1)S(1)} copy-done((bf16[3072,768]{1,0:T(8,128)(2,1)S(1)}, bf16[3072,768]{1,0:T(8,128)(2,1)}, u32[]{:S(2)}) %copy-start) | copy-done | bytes 4718616
  112.7 2.4 %finish_mlp.1 = (bf16[384,768]{1,0:T(8,128)(2,1)S(1)}, f32[384,128]{1,0:T(8,128)S(1)}, f32[8,768]{1,0:T(8,128)S(1)}) custom-call(bf16[3072,768]{1,0:T(8,128)(2,1)S(1)} %copy-done, bf16[384,1536]{1,0:T(8,128)(2,1)S(1)} %get-tuple-element.316.refs_0_.own_ref, bf16[384,1536]{1,0:T(8,128)(2,1)S(1)} %get-tuple-element.345.send_ref, ...), custom_call_target="tpu_custom_call" | custom-call | flops 1 | bytes 1 | tf_op jit(solution)/shard_map/finish_mlp/pallas_call | solution.py:55
  115.1 2.4 %unclimb.1 = (f32[384,768]{1,0:T(8,128)S(1)}, bf16[384,768]{1,0:T(8,128)(2,1)S(1)}, f32[8,768]{1,0:T(8,128)S(1)}) custom-call(bf16[768,3072]{1,0:T(8,128)(2,1)S(1)} %bitcast.59, bf16[384,3072]{1,0:T(8,128)(2,1)S(1)} %get-tuple-element.348.du_ref.refs_1_, bf16[384,768]{1,0:T(8,128)(2,1)S(1)} %bitcast.52, f32[384,768]{1,0:T(8,128)S(1)} %get-tuple-element.339.add_ref, ...), custom_call_target="tpu_custom_call" | custom-call | flops 1 | bytes 1 | tf_op jit(solution)/shard_map/unclimb/pallas_call | solution.py:55
  117.6 6.6 %unattend.1.dqkv_ref.refs_1_ = bf16[384,2304]{1,0:T(8,128)(2,1)S(1)} custom-call(bf16[768,768]{1,0:T(8,128)(2,1)S(1)} %copy-done.6, bf16[384,768]{1,0:T(8,128)(2,1)S(1)} %get-tuple-element.350.da_ref.refs_5_, bf16[384,2304]{1,0:T(8,128)(2,1)S(1)} %copy-done.3, f32[18,256,128]{2,1,0:T(8,128)S(1)} %copy-done.2), custom_call_target="tpu_custom_call" | custom-call | flops 1 | bytes 1 | tf_op jit(solution)/shard_map/unattend/pallas_call | solution.py:55
  125.2 2.6 %outer_b.1 = (bf16[2,96,1536]{2,1,0:T(8,128)(2,1)S(1)}, bf16[2,96,1536]{2,1,0:T(8,128)(2,1)S(1)}, f32[2,96,1536]{2,1,0:T(8,128)S(1)}, f32[2,96,1536]{2,1,0:T(8,128)S(1)}) custom-call(bf16[2,384,384]{2,1,0:T(8,128)(2,1)S(1)} %get-tuple-element.355.refs_0_.refs_2_, bf16[384,3072]{1,0:T(8,128)(2,1)S(1)} %get-tuple-element.348.du_ref.refs_1_, ...), custom_call_target="tpu_custom_call" | custom-call | flops 1 | bytes 1 | tf_op jit(solution)/shard_map/outer_b/pallas_call | solution.py:55
  129.7 1.3 collective-permute-start.44
  131.0 2.0 finish_rows.1
  137.1 2.8 %outer_a.1 = (bf16[2,96,1536]{2,1,0:T(8,128)(2,1)S(1)}, bf16[2,96,1664]{2,1,0:T(8,128)(2,1)S(1)}, f32[2,96,1536]{2,1,0:T(8,128)S(1)}, f32[2,96,1664]{2,1,0:T(8,128)S(1)}) custom-call(bf16[2,384,384]{2,1,0:T(8,128)(2,1)S(1)} %get-tuple-element.301.refs_0_.refs_4_, bf16[384,2304]{1,0:T(8,128)(2,1)S(1)} %unattend.1.dqkv_ref.refs_1_, ...), custom_call_target="tpu_custom_call" | custom-call | flops 1 | bytes 1 | tf_op jit(solution)/shard_map/outer_a/pallas_call | solution.py:55
  141.8 1.8 collective-permute-done.42.other_l
  145.3 1.6 collective-permute-start.47
  147.4 1.4 collective-permute-start.48
  148.8 3.1 %convert_select_fusion.1 = bf16[3,1024,768]{2,1,0:T(8,128)(2,1)} fusion(bf16[3,1024,768]{2,1,0:T(8,128)(2,1)S(1)} %bitcast.75, pred[3,1024]{1,0:T(4,128)(4,1)S(1)} %fusion, bf16[3,128,768]{2,1,0:T(8,128)(2,1)S(1)} %bitcast.62, s32[3,128]{1,0:T(4,128)S(1)} %copy-done.25), kind=kOutput, calls=%fused_computation.1 | convolution fusion | flops 609091584 | bytes 10031616 | tf_op jit(solution)/shard_map/skl,skd->sld/dot_general | solution.py:897
  152.0 4.2 %collective-permute-done.40.other_l = bf16[2,96,1536]{2,1,0:T(8,128)(2,1)S(1)} collective-permute-done((bf16[2,96,1536]{2,1,0:T(8,128)(2,1)S(1)}, bf16[2,96,1536]{2,1,0:T(8,128)(2,1)S(1)}, u32[]{:S(2)}, u32[]{:S(2)}) %collective-permute-start.40) | collective-permute-done | bytes 589856 | tf_op jit(solution)/shard_map/ppermute | solution.py:762
  156.2 1.3 collective-permute-done.41.other_r
  158.8 1.5 collective-permute-start.46
  160.3 4.5 %collective-permute-done.48.other = bf16[4,96,384]{2,1,0:T(8,128)(2,1)S(1)} collective-permute-done((bf16[4,96,384]{2,1,0:T(8,128)(2,1)S(1)}, bf16[4,96,384]{2,1,0:T(8,128)(2,1)S(1)}, u32[]{:S(2)}, u32[]{:S(2)}) %collective-permute-start.48) | collective-permute-done | bytes 294944 | tf_op jit(solution)/shard_map/ppermute | solution.py:762
  166.6 1.8 collective-permute-start.50
  168.5 1.9 collective-permute-start.54
  170.4 3.0 %convert_select_fusion = bf16[3,1024,768]{2,1,0:T(8,128)(2,1)} fusion(bf16[3,1024,768]{2,1,0:T(8,128)(2,1)S(1)} %bitcast.79, pred[3,1024]{1,0:T(4,128)(4,1)S(1)} %fusion, bf16[3,128,768]{2,1,0:T(8,128)(2,1)S(1)} %bitcast.63, s32[3,128]{1,0:T(4,128)S(1)} %copy-done.25), kind=kOutput, calls=%fused_computation | convolution fusion | flops 609091584 | bytes 10031616 | tf_op jit(solution)/shard_map/skl,skd->sld/dot_general | solution.py:897
  174.4 2.6 %collective-permute-start.52 = (bf16[24,3200]{1,0:T(8,128)(2,1)S(1)}, bf16[24,3200]{1,0:T(8,128)(2,1)S(1)}, u32[]{:S(2)}, u32[]{:S(2)}) collective-permute-start(bf16[24,3200]{1,0:T(8,128)(2,1)S(1)} %get-tuple-element.435), channel_id=1, source_target_pairs={{0,2},{1,3},{2,0},{3,1},{4,6},{5,7},{6,4},{7,5},{8,10},{9,11},{10,... | collective-permute-start | bytes 460808 | tf_op jit(solution)/shard_map/ppermute | solution.py:762
  178.2 12.1 %collective-permute-done.54.other = bf16[4,24,1536]{2,1,0:T(8,128)(2,1)S(1)} collective-permute-done((bf16[4,24,1536]{2,1,0:T(8,128)(2,1)S(1)}, bf16[4,24,1536]{2,1,0:T(8,128)(2,1)S(1)}, u32[]{:S(2)}, u32[]{:S(2)}) %collective-permute-start.54) | collective-permute-done | bytes 294944 | tf_op jit(solution)/shard_map/ppermute | solution.py:762
  190.3 1.7 collective-permute-start.55
  192.8 2.0 collective-permute-done.55.other_l
  194.8 1.7 collective-permute-done.56.other_r
  196.9 8.9 %all_to_all.8 = f32[32,1,128]{2,1,0:T(1,128)S(1)} all-to-all(f32[32,1,128]{2,1,0:T(1,128)S(1)} %broadcast_in_dim.45), channel_id=1, replica_groups=mesh['wide'=8,'narrow'=4] {'wide','narrow'}, dimensions={0} | all-to-all | bytes 32768 | tf_op jit(solution)/shard_map/all_to_all | solution.py:1003
  205.9 2.2 %update.1 = (f32[8,128]{1,0:T(8,128)S(1)}, f32[24,2304]{1,0:T(8,128)}, f32[24,2304]{1,0:T(8,128)}, f32[24,2304]{1,0:T(8,128)}, f32[24,768]{1,0:T(8,128)}, /*inde...) custom-call(f32[32,128]{1,0:T(8,128)S(1)} %bitcast.71, ...), custom_call_target="tpu_custom_call" | custom-call | flops 1 | bytes 1 | tf_op jit(solution)/shard_map/update/pallas_call | solution.py:55
  (218 shorter events, 42.6 us)
Async XLA Ops:
  1.8 11.3 %collective-permute-start = (bf16[24,3200]{1,0:T(8,128)(2,1)S(1)}, bf16[24,3200]{1,0:T(8,128)(2,1)S(1)}, u32[]{:S(2)}, u32[]{:S(2)}) collective-permute-start(bf16[24,3200]{1,0:T(8,128)(2,1)S(1)} %gather_input.1.refs_0_), channel_id=1, source_target_pairs={{0,1},{1,0},{2,3},{3,2},{4,5},{5,4},{6,7},{7,6},{8,9},{9,8},{10,11... | collective-permute-start | bytes 460808 | tf_op jit(solution)/shard_map/ppermute | solution.py:762
  4.8 14.4 %collective-permute-start.1 = (bf16[24,3200]{1,0:T(8,128)(2,1)S(1)}, bf16[24,3200]{1,0:T(8,128)(2,1)S(1)}, u32[]{:S(2)}, u32[]{:S(2)}) collective-permute-start(bf16[24,3200]{1,0:T(8,128)(2,1)S(1)} %gather_input.1.refs_0_), channel_id=1, source_target_pairs={{0,2},{1,3},{2,0},{3,1},{4,6},{5,7},{6,4},{7,5},{8,10},{9,11},{10,... | collective-permute-start | bytes 460808 | tf_op jit(solution)/shard_map/ppermute | solution.py:762
  7.4 11.8 %collective-permute-start.2 = (bf16[24,3200]{1,0:T(8,128)(2,1)S(1)}, bf16[24,3200]{1,0:T(8,128)(2,1)S(1)}, u32[]{:S(2)}, u32[]{:S(2)}) collective-permute-start(bf16[24,3200]{1,0:T(8,128)(2,1)S(1)} %gather_input.1.refs_0_), channel_id=1, source_target_pairs={{0,3},{1,2},{2,1},{3,0},{4,7},{5,6},{6,5},{7,4},{8,11},{9,10},{10,... | collective-permute-start | bytes 460808 | tf_op jit(solution)/shard_map/ppermute | solution.py:762
  19.4 12.1 %collective-permute-start.4 = (bf16[96,1664]{1,0:T(8,128)(2,1)S(1)}, bf16[96,1664]{1,0:T(8,128)(2,1)S(1)}, u32[]{:S(2)}, u32[]{:S(2)}) collective-permute-start(bf16[96,1664]{1,0:T(8,128)(2,1)S(1)} %get-tuple-element.252), channel_id=1, source_target_pairs={{0,16},{1,17},{2,18},{3,19},{4,20},{5,21},{6,22},{7,23},{8,24},{9,... | collective-permute-start | bytes 958472 | tf_op jit(solution)/shard_map/ppermute | solution.py:762
  21.0 10.5 %collective-permute-start.3 = (bf16[96,1536]{1,0:T(8,128)(2,1)S(1)}, bf16[96,1536]{1,0:T(8,128)(2,1)S(1)}, u32[]{:S(2)}, u32[]{:S(2)}) collective-permute-start(bf16[96,1536]{1,0:T(8,128)(2,1)S(1)} %get-tuple-element.251), channel_id=1, source_target_pairs={{0,8},{1,9},{2,10},{3,11},{4,12},{5,13},{6,14},{7,15},{8,0},{9,1},... | collective-permute-start | bytes 884744 | tf_op jit(solution)/shard_map/ppermute | solution.py:762
  22.5 8.9 %collective-permute-start.5 = (bf16[24,3072]{1,0:T(8,128)(2,1)S(1)}, bf16[24,3072]{1,0:T(8,128)(2,1)S(1)}, u32[]{:S(2)}, u32[]{:S(2)}) collective-permute-start(bf16[24,3072]{1,0:T(8,128)(2,1)S(1)} %convert_element_type.21.refs_0_), channel_id=1, source_target_pairs={{0,2},{1,3},{2,0},{3,1},{4,6},{5,7},{6,4},{7,5},{8,10},{9,11},{10,... | collective-permute-start | bytes 442376 | tf_op jit(solution)/shard_map/ppermute | solution.py:762
  26.0 4.4 %collective-permute-start.6 = (bf16[96,384]{1,0:T(8,128)(2,1)S(1)}, bf16[96,384]{1,0:T(8,128)(2,1)S(1)}, u32[]{:S(2)}, u32[]{:S(2)}) collective-permute-start(bf16[96,384]{1,0:T(8,128)(2,1)S(1)} %get-tuple-element.488.refs_0_), channel_id=1, source_target_pairs={{0,8},{1,9},{2,10},{3,11},{4,12},{5,13},{6,14},{7,15},{8,0},{9,1},... | collective-permute-start | bytes 221192 | tf_op jit(solution)/shard_map/ppermute | solution.py:762
  31.6 16.9 %collective-permute-start.9 = (bf16[2,96,1664]{2,1,0:T(8,128)(2,1)S(1)}, bf16[2,96,1664]{2,1,0:T(8,128)(2,1)S(1)}, u32[]{:S(2)}, u32[]{:S(2)}) collective-permute-start(bf16[2,96,1664]{2,1,0:T(8,128)(2,1)S(1)} %pad_maximum_fusion.refs_1_), channel_id=1, source_target_pairs={{0,8},{1,9},{2,10},{3,11},{4,12},{5,13},{6,14},{7,15},{8,0},{9,1},... | collective-permute-start | bytes 1916936 | tf_op jit(solution)/shard_map/ppermute | solution.py:762
  32.6 15.9 %collective-permute-start.11 = (bf16[2,96,1664]{2,1,0:T(8,128)(2,1)S(1)}, bf16[2,96,1664]{2,1,0:T(8,128)(2,1)S(1)}, u32[]{:S(2)}, u32[]{:S(2)}) collective-permute-start(bf16[2,96,1664]{2,1,0:T(8,128)(2,1)S(1)} %pad_maximum_fusion.refs_1_), channel_id=1, source_target_pairs={{0,4},{1,5},{2,6},{3,7},{4,0},{5,1},{6,2},{7,3},{8,12},{9,13},{10,... | collective-permute-start | bytes 1916936 | tf_op jit(solution)/shard_map/ppermute | solution.py:762
  32.7 15.8 %collective-permute-start.8 = (bf16[2,96,1536]{2,1,0:T(8,128)(2,1)S(1)}, bf16[2,96,1536]{2,1,0:T(8,128)(2,1)S(1)}, u32[]{:S(2)}, u32[]{:S(2)}) collective-permute-start(bf16[2,96,1536]{2,1,0:T(8,128)(2,1)S(1)} %pad_maximum_fusion.1.refs_0_), channel_id=1, source_target_pairs={{0,16},{1,17},{2,18},{3,19},{4,20},{5,21},{6,22},{7,23},{8,24},{9,... | collective-permute-start | bytes 1769480 | tf_op jit(solution)/shard_map/ppermute | solution.py:762
  33.3 15.2 %collective-permute-start.10 = (bf16[2,96,1536]{2,1,0:T(8,128)(2,1)S(1)}, bf16[2,96,1536]{2,1,0:T(8,128)(2,1)S(1)}, u32[]{:S(2)}, u32[]{:S(2)}) collective-permute-start(bf16[2,96,1536]{2,1,0:T(8,128)(2,1)S(1)} %pad_maximum_fusion.1.refs_0_), channel_id=1, source_target_pairs={{0,4},{1,5},{2,6},{3,7},{4,0},{5,1},{6,2},{7,3},{8,12},{9,13},{10,... | collective-permute-start | bytes 1769480 | tf_op jit(solution)/shard_map/ppermute | solution.py:762
  33.5 9.3 %collective-permute-start.12 = (bf16[2,24,3072]{2,1,0:T(8,128)(2,1)S(1)}, bf16[2,24,3072]{2,1,0:T(8,128)(2,1)S(1)}, u32[]{:S(2)}, u32[]{:S(2)}) collective-permute-start(bf16[2,24,3072]{2,1,0:T(8,128)(2,1)S(1)} %pad_maximum_fusion.6), channel_id=1, source_target_pairs={{0,1},{1,0},{2,3},{3,2},{4,5},{5,4},{6,7},{7,6},{8,9},{9,8},{10,11... | collective-permute-start | bytes 884744 | tf_op jit(solution)/shard_map/ppermute | solution.py:762
  42.8 15.8 %collective-permute-start.17 = (bf16[4,96,384]{2,1,0:T(8,128)(2,1)S(1)}, bf16[4,96,384]{2,1,0:T(8,128)(2,1)S(1)}, u32[]{:S(2)}, u32[]{:S(2)}) collective-permute-start(bf16[4,96,384]{2,1,0:T(8,128)(2,1)S(1)} %get-tuple-element.482), channel_id=1, source_target_pairs={{0,2},{1,3},{2,0},{3,1},{4,6},{5,7},{6,4},{7,5},{8,10},{9,11},{10,... | collective-permute-start | bytes 884744 | tf_op jit(solution)/shard_map/ppermute | solution.py:762
  49.4 10.5 %collective-permute-start.13 = (bf16[2,96,1536]{2,1,0:T(8,128)(2,1)S(1)}, bf16[2,96,1536]{2,1,0:T(8,128)(2,1)S(1)}, u32[]{:S(2)}, u32[]{:S(2)}) collective-permute-start(bf16[2,96,1536]{2,1,0:T(8,128)(2,1)S(1)} %collective-permute-done.8.refs_2_), channel_id=1, source_target_pairs={{0,4},{1,5},{2,6},{3,7},{4,0},{5,1},{6,2},{7,3},{8,12},{9,13},{10,... | collective-permute-start | bytes 1769480 | tf_op jit(solution)/shard_map/ppermute | solution.py:762
  49.4 10.5 %collective-permute-start.14 = (bf16[2,96,1664]{2,1,0:T(8,128)(2,1)S(1)}, bf16[2,96,1664]{2,1,0:T(8,128)(2,1)S(1)}, u32[]{:S(2)}, u32[]{:S(2)}) collective-permute-start(bf16[2,96,1664]{2,1,0:T(8,128)(2,1)S(1)} %collective-permute-done.9.refs_3_), channel_id=1, source_target_pairs={{0,4},{1,5},{2,6},{3,7},{4,0},{5,1},{6,2},{7,3},{8,12},{9,13},{10,... | collective-permute-start | bytes 1916936 | tf_op jit(solution)/shard_map/ppermute | solution.py:762
  50.3 8.7 %collective-permute-start.15 = (bf16[96,1536]{1,0:T(8,128)(2,1)S(1)}, bf16[96,1536]{1,0:T(8,128)(2,1)S(1)}, u32[]{:S(2)}, u32[]{:S(2)}) collective-permute-start(bf16[96,1536]{1,0:T(8,128)(2,1)S(1)} %get-tuple-element.267), channel_id=1, source_target_pairs={{0,8},{1,9},{2,10},{3,11},{4,12},{5,13},{6,14},{7,15},{8,0},{9,1},... | collective-permute-start | bytes 884744 | tf_op jit(solution)/shard_map/ppermute | solution.py:762
  51.4 8.4 %collective-permute-start.16 = (bf16[96,1536]{1,0:T(8,128)(2,1)S(1)}, bf16[96,1536]{1,0:T(8,128)(2,1)S(1)}, u32[]{:S(2)}, u32[]{:S(2)}) collective-permute-start(bf16[96,1536]{1,0:T(8,128)(2,1)S(1)} %get-tuple-element.270), channel_id=1, source_target_pairs={{0,16},{1,17},{2,18},{3,19},{4,20},{5,21},{6,22},{7,23},{8,24},{9,... | collective-permute-start | bytes 884744 | tf_op jit(solution)/shard_map/ppermute | solution.py:762
  59.9 13.9 %collective-permute-start.18 = (bf16[2,96,1536]{2,1,0:T(8,128)(2,1)S(1)}, bf16[2,96,1536]{2,1,0:T(8,128)(2,1)}, u32[]{:S(2)}, u32[]{:S(2)}) collective-permute-start(bf16[2,96,1536]{2,1,0:T(8,128)(2,1)S(1)} %pad_maximum_fusion.2.refs_0_), channel_id=1, source_target_pairs={{0,16},{1,17},{2,18},{3,19},{4,20},{5,21},{6,22},{7,23},{8,24},{9,... | collective-permute-start | bytes 1769480 | tf_op jit(solution)/shard_map/ppermute | solution.py:762
  60.5 16.9 %collective-permute-start.20 = (bf16[2,96,1536]{2,1,0:T(8,128)(2,1)S(1)}, bf16[2,96,1536]{2,1,0:T(8,128)(2,1)}, u32[]{:S(2)}, u32[]{:S(2)}) collective-permute-start(bf16[2,96,1536]{2,1,0:T(8,128)(2,1)S(1)} %pad_maximum_fusion.2.refs_0_), channel_id=1, source_target_pairs={{0,4},{1,5},{2,6},{3,7},{4,0},{5,1},{6,2},{7,3},{8,12},{9,13},{10,... | collective-permute-start | bytes 1769480 | tf_op jit(solution)/shard_map/ppermute | solution.py:762
  61.3 16.1 %collective-permute-start.19 = (bf16[2,96,1536]{2,1,0:T(8,128)(2,1)}, bf16[2,96,1536]{2,1,0:T(8,128)(2,1)}, u32[]{:S(2)}, u32[]{:S(2)}) collective-permute-start(bf16[2,96,1536]{2,1,0:T(8,128)(2,1)} %pad_maximum_fusion.3.refs_1_), channel_id=1, source_target_pairs={{0,8},{1,9},{2,10},{3,11},{4,12},{5,13},{6,14},{7,15},{8,0},{9,1},... | collective-permute-start | bytes 1769480 | tf_op jit(solution)/shard_map/ppermute | solution.py:762
  62.3 15.1 %collective-permute-start.21 = (bf16[2,96,1536]{2,1,0:T(8,128)(2,1)}, bf16[2,96,1536]{2,1,0:T(8,128)(2,1)}, u32[]{:S(2)}, u32[]{:S(2)}) collective-permute-start(bf16[2,96,1536]{2,1,0:T(8,128)(2,1)} %pad_maximum_fusion.3.refs_1_), channel_id=1, source_target_pairs={{0,4},{1,5},{2,6},{3,7},{4,0},{5,1},{6,2},{7,3},{8,12},{9,13},{10,... | collective-permute-start | bytes 1769480 | tf_op jit(solution)/shard_map/ppermute | solution.py:762
  63.4 15.9 %collective-permute-start.22 = (bf16[2,4,96,384]{3,2,1,0:T(8,128)(2,1)}, bf16[2,4,96,384]{3,2,1,0:T(8,128)(2,1)}, u32[]{:S(2)}, u32[]{:S(2)}) collective-permute-start(bf16[2,4,96,384]{3,2,1,0:T(8,128)(2,1)} %pad_maximum_fusion.4), channel_id=1, source_target_pairs={{0,1},{1,0},{2,3},{3,2},{4,5},{5,4},{6,7},{7,6},{8,9},{9,8},{10,11... | collective-permute-start | bytes 1769480 | tf_op jit(solution)/shard_map/ppermute | solution.py:762
  79.3 5.6 %collective-permute-start.25 = (bf16[6,384,384]{2,1,0:T(8,128)(2,1)S(1)}, bf16[6,384,384]{2,1,0:T(8,128)(2,1)S(1)}, u32[]{:S(2)}, u32[]{:S(2)}) collective-permute-start(bf16[6,384,384]{2,1,0:T(8,128)(2,1)S(1)} %get-tuple-element.306), channel_id=1, source_target_pairs={{0,4},{1,5},{2,6},{3,7},{4,0},{5,1},{6,2},{7,3},{8,12},{9,13},{10,... | collective-permute-start | bytes 5308424 | tf_op jit(solution)/shard_map/ppermute | solution.py:762
  79.9 4.7 %collective-permute-start.24 = (bf16[2,96,1536]{2,1,0:T(8,128)(2,1)}, bf16[2,96,1536]{2,1,0:T(8,128)(2,1)S(1)}, u32[]{:S(2)}, u32[]{:S(2)}) collective-permute-start(bf16[2,96,1536]{2,1,0:T(8,128)(2,1)} %collective-permute-done.19.refs_3_), channel_id=1, source_target_pairs={{0,4},{1,5},{2,6},{3,7},{4,0},{5,1},{6,2},{7,3},{8,12},{9,13},{10,... | collective-permute-start | bytes 1769480 | tf_op jit(solution)/shard_map/ppermute | solution.py:762
  81.1 17.2 %collective-permute-start.28 = (bf16[2,384,384]{2,1,0:T(8,128)(2,1)S(1)}, bf16[2,384,384]{2,1,0:T(8,128)(2,1)S(1)}, u32[]{:S(2)}, u32[]{:S(2)}) collective-permute-start(bf16[2,384,384]{2,1,0:T(8,128)(2,1)S(1)} %get-tuple-element.326.refs_0_), channel_id=1, source_target_pairs={{0,16},{1,17},{2,18},{3,19},{4,20},{5,21},{6,22},{7,23},{8,24},{9,... | collective-permute-start | bytes 1769480 | tf_op jit(solution)/shard_map/ppermute | solution.py:762
  82.7 15.7 %collective-permute-start.29 = (bf16[2,384,384]{2,1,0:T(8,128)(2,1)S(1)}, bf16[2,384,384]{2,1,0:T(8,128)(2,1)S(1)}, u32[]{:S(2)}, u32[]{:S(2)}) collective-permute-start(bf16[2,384,384]{2,1,0:T(8,128)(2,1)S(1)} %get-tuple-element.327.refs_1_), channel_id=1, source_target_pairs={{0,8},{1,9},{2,10},{3,11},{4,12},{5,13},{6,14},{7,15},{8,0},{9,1},... | collective-permute-start | bytes 1769480 | tf_op jit(solution)/shard_map/ppermute | solution.py:762
  83.7 14.6 %collective-permute-start.30 = (bf16[2,384,384]{2,1,0:T(8,128)(2,1)S(1)}, bf16[2,384,384]{2,1,0:T(8,128)(2,1)S(1)}, u32[]{:S(2)}, u32[]{:S(2)}) collective-permute-start(bf16[2,384,384]{2,1,0:T(8,128)(2,1)S(1)} %get-tuple-element.326.refs_0_), channel_id=1, source_target_pairs={{0,4},{1,5},{2,6},{3,7},{4,0},{5,1},{6,2},{7,3},{8,12},{9,13},{10,... | collective-permute-start | bytes 1769480 | tf_op jit(solution)/shard_map/ppermute | solution.py:762
  84.6 13.8 %collective-permute-start.31 = (bf16[2,384,384]{2,1,0:T(8,128)(2,1)S(1)}, bf16[2,384,384]{2,1,0:T(8,128)(2,1)S(1)}, u32[]{:S(2)}, u32[]{:S(2)}) collective-permute-start(bf16[2,384,384]{2,1,0:T(8,128)(2,1)S(1)} %get-tuple-element.327.refs_1_), channel_id=1, source_target_pairs={{0,4},{1,5},{2,6},{3,7},{4,0},{5,1},{6,2},{7,3},{8,12},{9,13},{10,... | collective-permute-start | bytes 1769480 | tf_op jit(solution)/shard_map/ppermute | solution.py:762
  99.0 18.5 %collective-permute-start.26 = (bf16[2,384,384]{2,1,0:T(8,128)(2,1)S(1)}, bf16[2,384,384]{2,1,0:T(8,128)(2,1)S(1)}, u32[]{:S(2)}, u32[]{:S(2)}) collective-permute-start(bf16[2,384,384]{2,1,0:T(8,128)(2,1)S(1)} %get-tuple-element.322), channel_id=1, source_target_pairs={{0,16},{1,17},{2,18},{3,19},{4,20},{5,21},{6,22},{7,23},{8,24},{9,... | collective-permute-start | bytes 1769480 | tf_op jit(solution)/shard_map/ppermute | solution.py:762
  100.5 17.0 %collective-permute-start.27 = (bf16[2,384,384]{2,1,0:T(8,128)(2,1)S(1)}, bf16[2,384,384]{2,1,0:T(8,128)(2,1)S(1)}, u32[]{:S(2)}, u32[]{:S(2)}) collective-permute-start(bf16[2,384,384]{2,1,0:T(8,128)(2,1)S(1)} %get-tuple-element.323), channel_id=1, source_target_pairs={{0,8},{1,9},{2,10},{3,11},{4,12},{5,13},{6,14},{7,15},{8,0},{9,1},... | collective-permute-start | bytes 1769480 | tf_op jit(solution)/shard_map/ppermute | solution.py:762
  117.5 6.7 %collective-permute-start.34 = (bf16[384,3072]{1,0:T(8,128)(2,1)S(1)}, bf16[384,3072]{1,0:T(8,128)(2,1)S(1)}, u32[]{:S(2)}, u32[]{:S(2)}) collective-permute-start(bf16[384,3072]{1,0:T(8,128)(2,1)S(1)} %get-tuple-element.348.du_ref.refs_1_), channel_id=1, source_target_pairs={{0,4},{1,5},{2,6},{3,7},{4,0},{5,1},{6,2},{7,3},{8,12},{9,13},{10,... | collective-permute-start | bytes 7077896 | tf_op jit(solution)/shard_map/ppermute | solution.py:762
  124.2 12.5 %collective-permute-start.35 = (bf16[384,2304]{1,0:T(8,128)(2,1)S(1)}, bf16[384,2304]{1,0:T(8,128)(2,1)S(1)}, u32[]{:S(2)}, u32[]{:S(2)}) collective-permute-start(bf16[384,2304]{1,0:T(8,128)(2,1)S(1)} %unattend.1.dqkv_ref.refs_1_), channel_id=1, source_target_pairs={{0,4},{1,5},{2,6},{3,7},{4,0},{5,1},{6,2},{7,3},{8,12},{9,13},{10,... | collective-permute-start | bytes 5308424 | tf_op jit(solution)/shard_map/ppermute | solution.py:762
  124.7 8.3 %collective-permute-start.36 = (bf16[384,768]{1,0:T(8,128)(2,1)S(1)}, bf16[384,768]{1,0:T(8,128)(2,1)S(1)}, u32[]{:S(2)}, u32[]{:S(2)}) collective-permute-start(bf16[384,768]{1,0:T(8,128)(2,1)S(1)} %get-tuple-element.350.da_ref.refs_5_), channel_id=1, source_target_pairs={{0,4},{1,5},{2,6},{3,7},{4,0},{5,1},{6,2},{7,3},{8,12},{9,13},{10,... | collective-permute-start | bytes 1769480 | tf_op jit(solution)/shard_map/ppermute | solution.py:762
  127.8 15.7 %collective-permute-start.42 = (bf16[2,96,1536]{2,1,0:T(8,128)(2,1)S(1)}, bf16[2,96,1536]{2,1,0:T(8,128)(2,1)S(1)}, u32[]{:S(2)}, u32[]{:S(2)}) collective-permute-start(bf16[2,96,1536]{2,1,0:T(8,128)(2,1)S(1)} %get-tuple-element.389), channel_id=1, source_target_pairs={{0,16},{1,17},{2,18},{3,19},{4,20},{5,21},{6,22},{7,23},{8,24},{9,... | collective-permute-start | bytes 1769480 | tf_op jit(solution)/shard_map/ppermute | solution.py:762
  128.7 16.1 %collective-permute-start.43 = (bf16[2,96,1536]{2,1,0:T(8,128)(2,1)S(1)}, bf16[2,96,1536]{2,1,0:T(8,128)(2,1)S(1)}, u32[]{:S(2)}, u32[]{:S(2)}) collective-permute-start(bf16[2,96,1536]{2,1,0:T(8,128)(2,1)S(1)} %get-tuple-element.390), channel_id=1, source_target_pairs={{0,8},{1,9},{2,10},{3,11},{4,12},{5,13},{6,14},{7,15},{8,0},{9,1},... | collective-permute-start | bytes 1769480 | tf_op jit(solution)/shard_map/ppermute | solution.py:762
  129.7 15.1 %collective-permute-start.44 = (bf16[2,4,96,384]{3,2,1,0:T(8,128)(2,1)S(1)}, bf16[2,4,96,384]{3,2,1,0:T(8,128)(2,1)S(1)}, u32[]{:S(2)}, u32[]{:S(2)}) collective-permute-start(bf16[2,4,96,384]{3,2,1,0:T(8,128)(2,1)S(1)} %get-tuple-element.391), channel_id=1, source_target_pairs={{0,1},{1,0},{2,3},{3,2},{4,5},{5,4},{6,7},{7,6},{8,9},{9,8},{10,11... | collective-permute-start | bytes 1769480 | tf_op jit(solution)/shard_map/ppermute | solution.py:762
  139.9 17.6 %collective-permute-start.41 = (bf16[2,96,1664]{2,1,0:T(8,128)(2,1)S(1)}, bf16[2,96,1664]{2,1,0:T(8,128)(2,1)S(1)}, u32[]{:S(2)}, u32[]{:S(2)}) collective-permute-start(bf16[2,96,1664]{2,1,0:T(8,128)(2,1)S(1)} %get-tuple-element.386), channel_id=1, source_target_pairs={{0,8},{1,9},{2,10},{3,11},{4,12},{5,13},{6,14},{7,15},{8,0},{9,1},... | collective-permute-start | bytes 1916936 | tf_op jit(solution)/shard_map/ppermute | solution.py:762
  141.0 15.2 %collective-permute-start.40 = (bf16[2,96,1536]{2,1,0:T(8,128)(2,1)S(1)}, bf16[2,96,1536]{2,1,0:T(8,128)(2,1)S(1)}, u32[]{:S(2)}, u32[]{:S(2)}) collective-permute-start(bf16[2,96,1536]{2,1,0:T(8,128)(2,1)S(1)} %get-tuple-element.385), channel_id=1, source_target_pairs={{0,16},{1,17},{2,18},{3,19},{4,20},{5,21},{6,22},{7,23},{8,24},{9,... | collective-permute-start | bytes 1769480 | tf_op jit(solution)/shard_map/ppermute | solution.py:762
  145.3 20.2 %collective-permute-start.47 = (bf16[2,4,24,1536]{3,2,1,0:T(8,128)(2,1)S(1)}, bf16[2,4,24,1536]{3,2,1,0:T(8,128)(2,1)S(1)}, u32[]{:S(2)}, u32[]{:S(2)}) collective-permute-start(bf16[2,4,24,1536]{3,2,1,0:T(8,128)(2,1)S(1)} %get-tuple-element.416), channel_id=1, source_target_pairs={{0,1},{1,0},{2,3},{3,2},{4,5},{5,4},{6,7},{7,6},{8,9},{9,8},{10,11... | collective-permute-start | bytes 1769480 | tf_op jit(solution)/shard_map/ppermute | solution.py:762
  147.4 17.4 %collective-permute-start.48 = (bf16[4,96,384]{2,1,0:T(8,128)(2,1)S(1)}, bf16[4,96,384]{2,1,0:T(8,128)(2,1)S(1)}, u32[]{:S(2)}, u32[]{:S(2)}) collective-permute-start(bf16[4,96,384]{2,1,0:T(8,128)(2,1)S(1)} %get-tuple-element.417), channel_id=1, source_target_pairs={{0,2},{1,3},{2,0},{3,1},{4,6},{5,7},{6,4},{7,5},{8,10},{9,11},{10,... | collective-permute-start | bytes 884744 | tf_op jit(solution)/shard_map/ppermute | solution.py:762
  157.8 15.6 %collective-permute-start.45 = (bf16[96,1536]{1,0:T(8,128)(2,1)S(1)}, bf16[96,1536]{1,0:T(8,128)(2,1)S(1)}, u32[]{:S(2)}, u32[]{:S(2)}) collective-permute-start(bf16[96,1536]{1,0:T(8,128)(2,1)S(1)} %get-tuple-element.413), channel_id=1, source_target_pairs={{0,8},{1,9},{2,10},{3,11},{4,12},{5,13},{6,14},{7,15},{8,0},{9,1},... | collective-permute-start | bytes 884744 | tf_op jit(solution)/shard_map/ppermute | solution.py:762
  158.8 14.5 %collective-permute-start.46 = (bf16[96,1664]{1,0:T(8,128)(2,1)S(1)}, bf16[96,1664]{1,0:T(8,128)(2,1)S(1)}, u32[]{:S(2)}, u32[]{:S(2)}) collective-permute-start(bf16[96,1664]{1,0:T(8,128)(2,1)S(1)} %get-tuple-element.414), channel_id=1, source_target_pairs={{0,16},{1,17},{2,18},{3,19},{4,20},{5,21},{6,22},{7,23},{8,24},{9,... | collective-permute-start | bytes 958472 | tf_op jit(solution)/shard_map/ppermute | solution.py:762
  165.8 7.6 %collective-permute-start.49 = (bf16[96,384]{1,0:T(8,128)(2,1)S(1)}, bf16[96,384]{1,0:T(8,128)(2,1)S(1)}, u32[]{:S(2)}, u32[]{:S(2)}) collective-permute-start(bf16[96,384]{1,0:T(8,128)(2,1)S(1)} %get-tuple-element.426), channel_id=1, source_target_pairs={{0,8},{1,9},{2,10},{3,11},{4,12},{5,13},{6,14},{7,15},{8,0},{9,1},... | collective-permute-start | bytes 221192 | tf_op jit(solution)/shard_map/ppermute | solution.py:762
  166.6 6.7 %collective-permute-start.50 = (bf16[96,384]{1,0:T(8,128)(2,1)S(1)}, bf16[96,384]{1,0:T(8,128)(2,1)S(1)}, u32[]{:S(2)}, u32[]{:S(2)}) collective-permute-start(bf16[96,384]{1,0:T(8,128)(2,1)S(1)} %get-tuple-element.427), channel_id=1, source_target_pairs={{0,16},{1,17},{2,18},{3,19},{4,20},{5,21},{6,22},{7,23},{8,24},{9,... | collective-permute-start | bytes 221192 | tf_op jit(solution)/shard_map/ppermute | solution.py:762
  168.5 21.8 %collective-permute-start.54 = (bf16[4,24,1536]{2,1,0:T(8,128)(2,1)S(1)}, bf16[4,24,1536]{2,1,0:T(8,128)(2,1)S(1)}, u32[]{:S(2)}, u32[]{:S(2)}) collective-permute-start(bf16[4,24,1536]{2,1,0:T(8,128)(2,1)S(1)} %get-tuple-element.438), channel_id=1, source_target_pairs={{0,2},{1,3},{2,0},{3,1},{4,6},{5,7},{6,4},{7,5},{8,10},{9,11},{10,... | collective-permute-start | bytes 884744 | tf_op jit(solution)/shard_map/ppermute | solution.py:762
  173.7 22.7 %collective-permute-start.51 = (bf16[24,3200]{1,0:T(8,128)(2,1)S(1)}, bf16[24,3200]{1,0:T(8,128)(2,1)S(1)}, u32[]{:S(2)}, u32[]{:S(2)}) collective-permute-start(bf16[24,3200]{1,0:T(8,128)(2,1)S(1)} %get-tuple-element.434), channel_id=1, source_target_pairs={{0,1},{1,0},{2,3},{3,2},{4,5},{5,4},{6,7},{7,6},{8,9},{9,8},{10,11... | collective-permute-start | bytes 460808 | tf_op jit(solution)/shard_map/ppermute | solution.py:762
  174.4 22.0 %collective-permute-start.52 = (bf16[24,3200]{1,0:T(8,128)(2,1)S(1)}, bf16[24,3200]{1,0:T(8,128)(2,1)S(1)}, u32[]{:S(2)}, u32[]{:S(2)}) collective-permute-start(bf16[24,3200]{1,0:T(8,128)(2,1)S(1)} %get-tuple-element.435), channel_id=1, source_target_pairs={{0,2},{1,3},{2,0},{3,1},{4,6},{5,7},{6,4},{7,5},{8,10},{9,11},{10,... | collective-permute-start | bytes 460808 | tf_op jit(solution)/shard_map/ppermute | solution.py:762
  177.0 19.4 %collective-permute-start.53 = (bf16[24,3200]{1,0:T(8,128)(2,1)S(1)}, bf16[24,3200]{1,0:T(8,128)(2,1)S(1)}, u32[]{:S(2)}, u32[]{:S(2)}) collective-permute-start(bf16[24,3200]{1,0:T(8,128)(2,1)S(1)} %get-tuple-element.436), channel_id=1, source_target_pairs={{0,3},{1,2},{2,1},{3,0},{4,7},{5,6},{6,5},{7,4},{8,11},{9,10},{10,... | collective-permute-start | bytes 460808 | tf_op jit(solution)/shard_map/ppermute | solution.py:762
  (56 other events, 688.9 us)

commit v3 on v2

--- a/solution.py
+++ b/solution.py
@@ -643,14 +643,15 @@
     width = split + keep_r.shape[1]
     part = rows // 4
 
-    def body(z_ref, keep_l, keep_r, other_l, other_r, mine, one, two, three, total):
+    def body(z_ref, keep_l, keep_r, other_l, other_r, mine, send, total):
         total[:, :split] = keep_l[...] + other_l[...].astype(f32)
         total[:, split:] = keep_r[...] + other_r[...].astype(f32)
-        for flip, out in enumerate((mine, one, two, three)):
+        for flip in range(4):
             start = pl.multiple_of((z_ref[0] ^ flip) * part, part)
-            out[...] = total[pl.ds(start, part)].astype(out.dtype)
-
-    outs = [((part, width), f32)] + [((part, width), bf16)] * 3
+            out = (mine, send)[flip % 2]
+            out[flip // 2] = total[pl.ds(start, part)].astype(out.dtype)
+
+    outs = [((2, part, width), f32), ((2, part, width), bf16)]
     scratch = [pltpu.VMEM((rows, width), f32)]
     args = (z, keep_l, keep_r, other_l, other_r)
     return kernel(body, "add_split", outs, args, "svvvv", scratch)
@@ -681,11 +682,11 @@
     return kernel(body, "settle_halves", outs, (keep, other_l, other_r), "vvv")
 
 
-def settle_z(mine, others):
+def settle_z(mine, other):
     rows, width = mine.shape
 
-    def body(mine, one, two, three, grad, square, last, turned):
-        value = mine[...] + one[...].astype(f32) + two[...].astype(f32) + three[...].astype(f32)
+    def body(mine, other, grad, square, last, turned):
+        value = mine[...] + other[...].astype(f32)
         grad[...] = value
         square[...] = jnp.full(square.shape, jnp.sum(value * value))
         turned[...] = jnp.zeros_like(turned)
@@ -694,7 +695,7 @@
 
     outs = [(mine.shape, f32), ((8, 128), f32), ((8, 128), f32)]
     scratch = [pltpu.VMEM((128, 128), f32)]
-    return kernel(body, "settle_z", outs, (mine, *others), "vvvv", scratch)
+    return kernel(body, "settle_z", outs, (mine, other), "vv", scratch)
 
 
 def update(squares, limit, grads, states, vec_grad, vec_states):
@@ -800,9 +801,11 @@
     other_l, other_r = yield [(send_l, 16), (send_r, 8)]
     send_l, send_r, left, right = add_pairs(keep_l, keep_r, other_l, other_r)
     other_l, other_r = yield [(send_l, 8), (send_r, 16)]
-    mine, *sends = add_split(z, left, right, other_l, other_r)
-    others = yield [(send, flip + 1) for flip, send in enumerate(sends)]
-    return settle_z(mine, others)
+    mine, send = add_split(z, left, right, other_l, other_r)
+    (other,) = yield [(send, 1)]
+    mine, send = add_next(mine, other)
+    (other,) = yield [(send, 2)]
+    return settle_z(mine, other)
 
 
 def scatter_pairs(z, send_l, send_r, keep_l, keep_r):
@@ -985,10 +988,11 @@
     grad_rows = stage([give_a], grad_rows)
     grad_rows = tick([give_b, give_c], grad_rows)
     grad_rows = stage([give_b, give_c], grad_rows)
+    grad_rows = tick([give_a, give_c], grad_rows)
+    grad_rows = stage([give_a], grad_rows)
     input_grad = place(back_blocks, grad_rows)
-    grad_rows = tick([give_a, give_c], input_grad)
-    input_grad = stage([give_a], input_grad)
-    input_grad = tick([give_b], input_grad)
+    input_grad = tick([give_a, give_b], input_grad)
+    input_grad = stage([give_a, give_b], input_grad)
     input_grad = tick([give_a, give_b], input_grad)
     if paired:
         give_a, give_b, give_c = give_a.result, give_b.result, give_c.result

time: 211 us -> 208 us (0.986)
  waiting for transfers between devices: 68.1 us -> 62.6 us
  blocking collectives: 8.87 us -> 11.1 us
    ppermute x57 -> x56, waiting for transfers between devices: 68.1 us -> 62.6 us  [swap(): return lax.ppermute(array, AXES, [(i, i ^ bit) for i in range(count)])]
    all_to_all x1, blocking collectives: 8.87 us -> 11.1 us  [per_device(): squares = lax.all_to_all(squares, AXES, 0, 0, tiled=True)]
    ppermute x57 -> x56, starting transfers between devices: 55.4 us -> 55.1 us  [swap(): return lax.ppermute(array, AXES, [(i, i ^ bit) for i in range(count)])]
    pallas_call x27 -> x28, Pallas kernels: 52.8 us -> 52.9 us  [kernel(): pl.pallas_call(body, out_shape=[jax.ShapeDtypeStruct(*out) if place < hel...]
  transfers between devices with their start and end apart: 57 -> 56, of which waited for: 25 -> 27; matrix products, arithmetic and copies ran while one was open for 7% -> 7% of each run, Pallas kernels for 23% -> 24%
where the time goes in v3:
time: 208 us; the launch traced here: 205 us
  waiting for transfers between devices  62.6 us (30%)
  starting transfers between devices  55.1 us (26%)
  Pallas kernels  52.9 us (25%)
  blocking collectives  11.1 us (5%)
  matrix products  10.5 us (5%)
  local copies, waits for them, and re-layouts  7.9 us (4%)
  other arithmetic  3.38 us (2%)
    ppermute x56, waiting for transfers between devices, swap(): return lax.ppermute(array, AXES, [(i, i ^ bit) for i in range(count)])  62.6 us
    ppermute x56, starting transfers between devices, swap(): return lax.ppermute(array, AXES, [(i, i ^ bit) for i in range(count)])  55.1 us
    pallas_call x28, Pallas kernels, kernel(): pl.pallas_call(body, out_shape=[jax.ShapeDtypeStruct(*out) if place < hel...  52.9 us
    all_to_all x1, blocking collectives, per_device(): squares = lax.all_to_all(squares, AXES, 0, 0, tiled=True)  11.1 us
    dot_general x2, matrix products, place(): jnp.einsum('skl,skd->sld', hot_low, rows, preferred_element_type=f32)  6.11 us
    unnamed x94, local copies, waits for them, and re-layouts  6.02 us
    dot_general x2, matrix products, pick(): jnp.einsum('skl,sld->skd', hot_low, blocks, preferred_element_type=f32)  4.37 us
  transfers between devices with their start and end apart: 56, of which 27 were waited for; matrix products, arithmetic and copies ran while one was open for 7% of the time, Pallas kernels for 24%

profile of v3, /device:TPU:0, one launch (start us, length us, event | category | flops | bytes accessed | tf_op | source)
XLA Modules:
  0.0 205.3 jit_solution(774948910196170632)
XLA Ops:
  1.8 3.0 %collective-permute-start = (bf16[24,3200]{1,0:T(8,128)(2,1)S(1)}, bf16[24,3200]{1,0:T(8,128)(2,1)S(1)}, u32[]{:S(2)}, u32[]{:S(2)}) collective-permute-start(bf16[24,3200]{1,0:T(8,128)(2,1)S(1)} %gather_input.1.refs_0_), channel_id=1, source_target_pairs={{0,1},{1,0},{2,3},{3,2},{4,5},{5,4},{6,7},{7,6},{8,9},{9,8},{10,11... | collective-permute-start | bytes 460808 | tf_op jit(solution)/shard_map/ppermute | solution.py:763
  4.8 2.6 %collective-permute-start.1 = (bf16[24,3200]{1,0:T(8,128)(2,1)S(1)}, bf16[24,3200]{1,0:T(8,128)(2,1)S(1)}, u32[]{:S(2)}, u32[]{:S(2)}) collective-permute-start(bf16[24,3200]{1,0:T(8,128)(2,1)S(1)} %gather_input.1.refs_0_), channel_id=1, source_target_pairs={{0,2},{1,3},{2,0},{3,1},{4,6},{5,7},{6,4},{7,5},{8,10},{9,11},{10,... | collective-permute-start | bytes 460808 | tf_op jit(solution)/shard_map/ppermute | solution.py:763
  7.4 3.4 %fusion.3 = bf16[3,128,768]{2,1,0:T(8,128)(2,1)S(1)} fusion(bf16[3,1024,768]{2,1,0:T(8,128)(2,1)} %bitcast.72, s32[3,128]{1,0:T(4,128)} %param.22), kind=kOutput, calls=%fused_computation.7 | convolution fusion | flops 604667904 | bytes 5309952 | tf_op jit(solution)/shard_map/skl,sld->skd/dot_general | solution.py:895
  13.0 6.2 %collective-permute-done.1.refs_2_ = bf16[24,3200]{1,0:T(8,128)(2,1)S(1)} collective-permute-done((bf16[24,3200]{1,0:T(8,128)(2,1)S(1)}, bf16[24,3200]{1,0:T(8,128)(2,1)S(1)}, u32[]{:S(2)}, u32[]{:S(2)}) %collective-permute-start.1) | collective-permute-done | bytes 153632 | tf_op jit(solution)/shard_map/ppermute | solution.py:763
  19.4 1.6 collective-permute-start.4
  21.0 1.6 collective-permute-start.3
  22.5 3.4 %collective-permute-start.5 = (bf16[24,3072]{1,0:T(8,128)(2,1)S(1)}, bf16[24,3072]{1,0:T(8,128)(2,1)S(1)}, u32[]{:S(2)}, u32[]{:S(2)}) collective-permute-start(bf16[24,3072]{1,0:T(8,128)(2,1)S(1)} %convert_element_type.21.refs_0_), channel_id=1, source_target_pairs={{0,2},{1,3},{2,0},{3,1},{4,6},{5,7},{6,4},{7,5},{8,10},{9,11},{10,... | collective-permute-start | bytes 442376 | tf_op jit(solution)/shard_map/ppermute | solution.py:763
  27.1 3.3 %collective-permute-done.6.refs_1_ = bf16[96,384]{1,0:T(8,128)(2,1)S(1)} collective-permute-done((bf16[96,384]{1,0:T(8,128)(2,1)S(1)}, bf16[96,384]{1,0:T(8,128)(2,1)S(1)}, u32[]{:S(2)}, u32[]{:S(2)}) %collective-permute-start.6) | collective-permute-done | bytes 73760 | tf_op jit(solution)/shard_map/ppermute | solution.py:763
  33.5 1.7 collective-permute-start.12
  35.3 7.5 %collective-permute-done.12 = bf16[2,24,3072]{2,1,0:T(8,128)(2,1)S(1)} collective-permute-done((bf16[2,24,3072]{2,1,0:T(8,128)(2,1)S(1)}, bf16[2,24,3072]{2,1,0:T(8,128)(2,1)S(1)}, u32[]{:S(2)}, u32[]{:S(2)}) %collective-permute-start.12) | collective-permute-done | bytes 294944 | tf_op jit(solution)/shard_map/ppermute | solution.py:763
  42.8 2.8 %collective-permute-start.17 = (bf16[4,96,384]{2,1,0:T(8,128)(2,1)S(1)}, bf16[4,96,384]{2,1,0:T(8,128)(2,1)S(1)}, u32[]{:S(2)}, u32[]{:S(2)}) collective-permute-start(bf16[4,96,384]{2,1,0:T(8,128)(2,1)S(1)} %get-tuple-element.486), channel_id=1, source_target_pairs={{0,2},{1,3},{2,0},{3,1},{4,6},{5,7},{6,4},{7,5},{8,10},{9,11},{10,... | collective-permute-start | bytes 884744 | tf_op jit(solution)/shard_map/ppermute | solution.py:763
  45.6 2.9 %collective-permute-done.8.refs_2_ = bf16[2,96,1536]{2,1,0:T(8,128)(2,1)S(1)} collective-permute-done((bf16[2,96,1536]{2,1,0:T(8,128)(2,1)S(1)}, bf16[2,96,1536]{2,1,0:T(8,128)(2,1)S(1)}, u32[]{:S(2)}, u32[]{:S(2)}) %collective-permute-start.8) | collective-permute-done | bytes 589856 | tf_op jit(solution)/shard_map/ppermute | solution.py:763
  52.0 6.6 %collective-permute-done.17.refs_5_ = bf16[4,96,384]{2,1,0:T(8,128)(2,1)S(1)} collective-permute-done((bf16[4,96,384]{2,1,0:T(8,128)(2,1)S(1)}, bf16[4,96,384]{2,1,0:T(8,128)(2,1)S(1)}, u32[]{:S(2)}, u32[]{:S(2)}) %collective-permute-start.17) | collective-permute-done | bytes 294944 | tf_op jit(solution)/shard_map/ppermute | solution.py:763
  63.4 1.7 collective-permute-start.22
  65.3 8.0 %attend.1 = (bf16[2,384,384]{2,1,0:T(8,128)(2,1)S(1)}, bf16[6,384,384]{2,1,0:T(8,128)(2,1)S(1)}, bf16[384,768]{1,0:T(8,128)(2,1)S(1)}, f32[384,128]{1,0:T(8,128)...) custom-call(s32[1]{0:T(128)} %bitcast.24.me_ref, ...), custom_call_target="tpu_custom_call" | custom-call | flops 1 | bytes 1 | tf_op jit(solution)/shard_map/attend/pallas_call | solution.py:55
  73.8 3.6 %collective-permute-done.19.refs_3_ = bf16[2,96,1536]{2,1,0:T(8,128)(2,1)} collective-permute-done((bf16[2,96,1536]{2,1,0:T(8,128)(2,1)}, bf16[2,96,1536]{2,1,0:T(8,128)(2,1)}, u32[]{:S(2)}, u32[]{:S(2)}) %collective-permute-start.19) | collective-permute-done | bytes 589856 | tf_op jit(solution)/shard_map/ppermute | solution.py:763
  77.4 1.9 collective-permute-done.22
  81.1 1.6 collective-permute-start.28
  85.4 10.1 %climb.1 = (bf16[384,1536]{1,0:T(8,128)(2,1)S(1)}, bf16[384,1536]{1,0:T(8,128)(2,1)S(1)}, bf16[384,1536]{1,0:T(8,128)(2,1)S(1)}, bf16[2,384,384]{2,1,0:T(8,128)(...) custom-call(s32[1]{0:T(128)} %bitcast.24.me_ref, bf16[2,96,1536]{2,1,0:T(8,128)(2,1)} %copy-done.24, ...), custom_call_target="tpu_custom_call" | custom-call | flops 1 | bytes 1 | tf_op jit(solution)/shard_map/climb/pallas_call | solution.py:55
  95.7 2.6 %outer_c.1 = (bf16[2,384,384]{2,1,0:T(8,128)(2,1)S(1)}, bf16[2,384,384]{2,1,0:T(8,128)(2,1)S(1)}, f32[2,384,384]{2,1,0:T(8,128)S(1)}, f32[2,384,384]{2,1,0:T(8,128)S(1)}) custom-call(bf16[384,1536]{1,0:T(8,128)(2,1)S(1)} %get-tuple-element.318.refs_0_.own_ref, bf16[384,768]{1,0:T(8,128)(2,1)S(1)} %get-tuple-element.319.refs_1_.refs_9_, ...), custom_call_target="tpu_custom_call" | custom-call | flops 1 | bytes 1 | tf_op jit(solution)/shard_map/outer_c/pallas_call | solution.py:55
  99.0 1.5 collective-permute-start.26
  103.2 7.1 %descend.1 = (bf16[384,3072]{1,0:T(8,128)(2,1)S(1)}, bf16[3072,768]{1,0:T(8,128)(2,1)}) custom-call(s32[1]{0:T(128)} %bitcast.24.me_ref, bf16[2,384,384]{2,1,0:T(8,128)(2,1)} %copy-done.8, bf16[2,384,384]{2,1,0:T(8,128)(2,1)} %copy-done.9, bf16[2,384,384]{2,1,0:T(8,128)(2,1)} %copy-done.31, bf16[2,384,384]{2,1,0:T(8,128)(2,1)} %copy-done.33, ...), custom_call_target="tpu_custom_call" | custom-call | flops 1 | bytes 1 | tf_op jit(solution)/shard_map/descend/pallas_call | solution.py:55
  110.3 2.3 %copy-done = bf16[3072,768]{1,0:T(8,128)(2,1)S(1)} copy-done((bf16[3072,768]{1,0:T(8,128)(2,1)S(1)}, bf16[3072,768]{1,0:T(8,128)(2,1)}, u32[]{:S(2)}) %copy-start) | copy-done | bytes 4718616
  112.7 2.4 %finish_mlp.1 = (bf16[384,768]{1,0:T(8,128)(2,1)S(1)}, f32[384,128]{1,0:T(8,128)S(1)}, f32[8,768]{1,0:T(8,128)S(1)}) custom-call(bf16[3072,768]{1,0:T(8,128)(2,1)S(1)} %copy-done, bf16[384,1536]{1,0:T(8,128)(2,1)S(1)} %get-tuple-element.318.refs_0_.own_ref, bf16[384,1536]{1,0:T(8,128)(2,1)S(1)} %get-tuple-element.347.send_ref, ...), custom_call_target="tpu_custom_call" | custom-call | flops 1 | bytes 1 | tf_op jit(solution)/shard_map/finish_mlp/pallas_call | solution.py:55
  115.1 2.4 %unclimb.1 = (f32[384,768]{1,0:T(8,128)S(1)}, bf16[384,768]{1,0:T(8,128)(2,1)S(1)}, f32[8,768]{1,0:T(8,128)S(1)}) custom-call(bf16[768,3072]{1,0:T(8,128)(2,1)S(1)} %bitcast.59, bf16[384,3072]{1,0:T(8,128)(2,1)S(1)} %get-tuple-element.350.du_ref.refs_1_, bf16[384,768]{1,0:T(8,128)(2,1)S(1)} %bitcast.52, f32[384,768]{1,0:T(8,128)S(1)} %get-tuple-element.341.add_ref, ...), custom_call_target="tpu_custom_call" | custom-call | flops 1 | bytes 1 | tf_op jit(solution)/shard_map/unclimb/pallas_call | solution.py:55
  117.6 6.6 %unattend.1.dqkv_ref.refs_1_ = bf16[384,2304]{1,0:T(8,128)(2,1)S(1)} custom-call(bf16[768,768]{1,0:T(8,128)(2,1)S(1)} %copy-done.6, bf16[384,768]{1,0:T(8,128)(2,1)S(1)} %get-tuple-element.352.da_ref.refs_5_, bf16[384,2304]{1,0:T(8,128)(2,1)S(1)} %copy-done.3, f32[18,256,128]{2,1,0:T(8,128)S(1)} %copy-done.2), custom_call_target="tpu_custom_call" | custom-call | flops 1 | bytes 1 | tf_op jit(solution)/shard_map/unattend/pallas_call | solution.py:55
  125.2 2.6 %outer_b.1 = (bf16[2,96,1536]{2,1,0:T(8,128)(2,1)S(1)}, bf16[2,96,1536]{2,1,0:T(8,128)(2,1)S(1)}, f32[2,96,1536]{2,1,0:T(8,128)S(1)}, f32[2,96,1536]{2,1,0:T(8,128)S(1)}) custom-call(bf16[2,384,384]{2,1,0:T(8,128)(2,1)S(1)} %get-tuple-element.357.refs_0_.refs_2_, bf16[384,3072]{1,0:T(8,128)(2,1)S(1)} %get-tuple-element.350.du_ref.refs_1_, ...), custom_call_target="tpu_custom_call" | custom-call | flops 1 | bytes 1 | tf_op jit(solution)/shard_map/outer_b/pallas_call | solution.py:55
  129.7 1.3 collective-permute-start.44
  131.0 2.0 finish_rows.1
  137.1 2.8 %outer_a.1 = (bf16[2,96,1536]{2,1,0:T(8,128)(2,1)S(1)}, bf16[2,96,1664]{2,1,0:T(8,128)(2,1)S(1)}, f32[2,96,1536]{2,1,0:T(8,128)S(1)}, f32[2,96,1664]{2,1,0:T(8,128)S(1)}) custom-call(bf16[2,384,384]{2,1,0:T(8,128)(2,1)S(1)} %get-tuple-element.303.refs_0_.refs_4_, bf16[384,2304]{1,0:T(8,128)(2,1)S(1)} %unattend.1.dqkv_ref.refs_1_, ...), custom_call_target="tpu_custom_call" | custom-call | flops 1 | bytes 1 | tf_op jit(solution)/shard_map/outer_a/pallas_call | solution.py:55
  145.3 1.6 collective-permute-start.47
  146.9 1.3 collective-permute-start.48
  148.3 3.2 %convert_select_fusion.1 = bf16[3,1024,768]{2,1,0:T(8,128)(2,1)} fusion(bf16[3,1024,768]{2,1,0:T(8,128)(2,1)S(1)} %bitcast.75, pred[3,1024]{1,0:T(4,128)(4,1)S(1)} %fusion, bf16[3,128,768]{2,1,0:T(8,128)(2,1)S(1)} %bitcast.63, s32[3,128]{1,0:T(4,128)S(1)} %copy-done.25), kind=kOutput, calls=%fused_computation.1 | convolution fusion | flops 609091584 | bytes 10031616 | tf_op jit(solution)/shard_map/skl,skd->sld/dot_general | solution.py:900
  151.4 4.8 %collective-permute-done.40.other_l = bf16[2,96,1536]{2,1,0:T(8,128)(2,1)S(1)} collective-permute-done((bf16[2,96,1536]{2,1,0:T(8,128)(2,1)S(1)}, bf16[2,96,1536]{2,1,0:T(8,128)(2,1)S(1)}, u32[]{:S(2)}, u32[]{:S(2)}) %collective-permute-start.40) | collective-permute-done | bytes 589856 | tf_op jit(solution)/shard_map/ppermute | solution.py:763
  156.2 1.3 collective-permute-done.41.other_r
  157.8 1.6 collective-permute-start.46
  160.3 4.5 %collective-permute-done.48.other = bf16[4,96,384]{2,1,0:T(8,128)(2,1)S(1)} collective-permute-done((bf16[4,96,384]{2,1,0:T(8,128)(2,1)S(1)}, bf16[4,96,384]{2,1,0:T(8,128)(2,1)S(1)}, u32[]{:S(2)}, u32[]{:S(2)}) %collective-permute-start.48) | collective-permute-done | bytes 294944 | tf_op jit(solution)/shard_map/ppermute | solution.py:763
  166.6 1.8 collective-permute-start.50
  168.5 1.9 collective-permute-start.52
  171.2 2.8 %collective-permute-start.51 = (bf16[2,24,3200]{2,1,0:T(8,128)(2,1)S(1)}, bf16[2,24,3200]{2,1,0:T(8,128)(2,1)S(1)}, u32[]{:S(2)}, u32[]{:S(2)}) collective-permute-start(bf16[2,24,3200]{2,1,0:T(8,128)(2,1)S(1)} %get-tuple-element.436), channel_id=1, source_target_pairs={{0,1},{1,0},{2,3},{3,2},{4,5},{5,4},{6,7},{7,6},{8,9},{9,8},{10,11... | collective-permute-start | bytes 921608 | tf_op jit(solution)/shard_map/ppermute | solution.py:763
  174.0 3.0 %convert_select_fusion = bf16[3,1024,768]{2,1,0:T(8,128)(2,1)} fusion(bf16[3,1024,768]{2,1,0:T(8,128)(2,1)S(1)} %bitcast.79, pred[3,1024]{1,0:T(4,128)(4,1)S(1)} %fusion, bf16[3,128,768]{2,1,0:T(8,128)(2,1)S(1)} %bitcast.62, s32[3,128]{1,0:T(4,128)S(1)} %copy-done.25), kind=kOutput, calls=%fused_computation | convolution fusion | flops 609091584 | bytes 10031616 | tf_op jit(solution)/shard_map/skl,skd->sld/dot_general | solution.py:900
  177.0 5.5 %collective-permute-done.52.other = bf16[4,24,1536]{2,1,0:T(8,128)(2,1)S(1)} collective-permute-done((bf16[4,24,1536]{2,1,0:T(8,128)(2,1)S(1)}, bf16[4,24,1536]{2,1,0:T(8,128)(2,1)S(1)}, u32[]{:S(2)}, u32[]{:S(2)}) %collective-permute-start.52) | collective-permute-done | bytes 294944 | tf_op jit(solution)/shard_map/ppermute | solution.py:763
  183.2 1.5 collective-permute-start.53
  184.7 1.7 collective-permute-start.54
  187.1 2.0 collective-permute-done.54.other_l
  189.1 1.7 collective-permute-done.55.other_r
  191.2 11.1 %all_to_all.8 = f32[32,1,128]{2,1,0:T(1,128)S(1)} all-to-all(f32[32,1,128]{2,1,0:T(1,128)S(1)} %broadcast_in_dim.45), channel_id=1, replica_groups=mesh['wide'=8,'narrow'=4] {'wide','narrow'}, dimensions={0} | all-to-all | bytes 32768 | tf_op jit(solution)/shard_map/all_to_all | solution.py:1007
  202.4 2.2 %update.1 = (f32[8,128]{1,0:T(8,128)S(1)}, f32[24,2304]{1,0:T(8,128)}, f32[24,2304]{1,0:T(8,128)}, f32[24,2304]{1,0:T(8,128)}, f32[24,768]{1,0:T(8,128)}, /*inde...) custom-call(f32[32,128]{1,0:T(8,128)S(1)} %bitcast.71, ...), custom_call_target="tpu_custom_call" | custom-call | flops 1 | bytes 1 | tf_op jit(solution)/shard_map/update/pallas_call | solution.py:55
  (217 shorter events, 43.2 us)
Async XLA Ops:
  1.8 11.3 %collective-permute-start = (bf16[24,3200]{1,0:T(8,128)(2,1)S(1)}, bf16[24,3200]{1,0:T(8,128)(2,1)S(1)}, u32[]{:S(2)}, u32[]{:S(2)}) collective-permute-start(bf16[24,3200]{1,0:T(8,128)(2,1)S(1)} %gather_input.1.refs_0_), channel_id=1, source_target_pairs={{0,1},{1,0},{2,3},{3,2},{4,5},{5,4},{6,7},{7,6},{8,9},{9,8},{10,11... | collective-permute-start | bytes 460808 | tf_op jit(solution)/shard_map/ppermute | solution.py:763
  4.8 14.4 %collective-permute-start.1 = (bf16[24,3200]{1,0:T(8,128)(2,1)S(1)}, bf16[24,3200]{1,0:T(8,128)(2,1)S(1)}, u32[]{:S(2)}, u32[]{:S(2)}) collective-permute-start(bf16[24,3200]{1,0:T(8,128)(2,1)S(1)} %gather_input.1.refs_0_), channel_id=1, source_target_pairs={{0,2},{1,3},{2,0},{3,1},{4,6},{5,7},{6,4},{7,5},{8,10},{9,11},{10,... | collective-permute-start | bytes 460808 | tf_op jit(solution)/shard_map/ppermute | solution.py:763
  7.4 11.8 %collective-permute-start.2 = (bf16[24,3200]{1,0:T(8,128)(2,1)S(1)}, bf16[24,3200]{1,0:T(8,128)(2,1)S(1)}, u32[]{:S(2)}, u32[]{:S(2)}) collective-permute-start(bf16[24,3200]{1,0:T(8,128)(2,1)S(1)} %gather_input.1.refs_0_), channel_id=1, source_target_pairs={{0,3},{1,2},{2,1},{3,0},{4,7},{5,6},{6,5},{7,4},{8,11},{9,10},{10,... | collective-permute-start | bytes 460808 | tf_op jit(solution)/shard_map/ppermute | solution.py:763
  19.4 12.1 %collective-permute-start.4 = (bf16[96,1664]{1,0:T(8,128)(2,1)S(1)}, bf16[96,1664]{1,0:T(8,128)(2,1)S(1)}, u32[]{:S(2)}, u32[]{:S(2)}) collective-permute-start(bf16[96,1664]{1,0:T(8,128)(2,1)S(1)} %get-tuple-element.254), channel_id=1, source_target_pairs={{0,16},{1,17},{2,18},{3,19},{4,20},{5,21},{6,22},{7,23},{8,24},{9,... | collective-permute-start | bytes 958472 | tf_op jit(solution)/shard_map/ppermute | solution.py:763
  21.0 10.5 %collective-permute-start.3 = (bf16[96,1536]{1,0:T(8,128)(2,1)S(1)}, bf16[96,1536]{1,0:T(8,128)(2,1)S(1)}, u32[]{:S(2)}, u32[]{:S(2)}) collective-permute-start(bf16[96,1536]{1,0:T(8,128)(2,1)S(1)} %get-tuple-element.253), channel_id=1, source_target_pairs={{0,8},{1,9},{2,10},{3,11},{4,12},{5,13},{6,14},{7,15},{8,0},{9,1},... | collective-permute-start | bytes 884744 | tf_op jit(solution)/shard_map/ppermute | solution.py:763
  22.5 8.9 %collective-permute-start.5 = (bf16[24,3072]{1,0:T(8,128)(2,1)S(1)}, bf16[24,3072]{1,0:T(8,128)(2,1)S(1)}, u32[]{:S(2)}, u32[]{:S(2)}) collective-permute-start(bf16[24,3072]{1,0:T(8,128)(2,1)S(1)} %convert_element_type.21.refs_0_), channel_id=1, source_target_pairs={{0,2},{1,3},{2,0},{3,1},{4,6},{5,7},{6,4},{7,5},{8,10},{9,11},{10,... | collective-permute-start | bytes 442376 | tf_op jit(solution)/shard_map/ppermute | solution.py:763
  26.0 4.4 %collective-permute-start.6 = (bf16[96,384]{1,0:T(8,128)(2,1)S(1)}, bf16[96,384]{1,0:T(8,128)(2,1)S(1)}, u32[]{:S(2)}, u32[]{:S(2)}) collective-permute-start(bf16[96,384]{1,0:T(8,128)(2,1)S(1)} %get-tuple-element.492.refs_0_), channel_id=1, source_target_pairs={{0,8},{1,9},{2,10},{3,11},{4,12},{5,13},{6,14},{7,15},{8,0},{9,1},... | collective-permute-start | bytes 221192 | tf_op jit(solution)/shard_map/ppermute | solution.py:763
  26.6 4.4 %collective-permute-start.7 = (bf16[96,384]{1,0:T(8,128)(2,1)S(1)}, bf16[96,384]{1,0:T(8,128)(2,1)S(1)}, u32[]{:S(2)}, u32[]{:S(2)}) collective-permute-start(bf16[96,384]{1,0:T(8,128)(2,1)S(1)} %get-tuple-element.491.refs_2_), channel_id=1, source_target_pairs={{0,16},{1,17},{2,18},{3,19},{4,20},{5,21},{6,22},{7,23},{8,24},{9,... | collective-permute-start | bytes 221192 | tf_op jit(solution)/shard_map/ppermute | solution.py:763
  31.6 16.9 %collective-permute-start.9 = (bf16[2,96,1664]{2,1,0:T(8,128)(2,1)S(1)}, bf16[2,96,1664]{2,1,0:T(8,128)(2,1)S(1)}, u32[]{:S(2)}, u32[]{:S(2)}) collective-permute-start(bf16[2,96,1664]{2,1,0:T(8,128)(2,1)S(1)} %pad_maximum_fusion.refs_1_), channel_id=1, source_target_pairs={{0,8},{1,9},{2,10},{3,11},{4,12},{5,13},{6,14},{7,15},{8,0},{9,1},... | collective-permute-start | bytes 1916936 | tf_op jit(solution)/shard_map/ppermute | solution.py:763
  32.6 15.9 %collective-permute-start.11 = (bf16[2,96,1664]{2,1,0:T(8,128)(2,1)S(1)}, bf16[2,96,1664]{2,1,0:T(8,128)(2,1)S(1)}, u32[]{:S(2)}, u32[]{:S(2)}) collective-permute-start(bf16[2,96,1664]{2,1,0:T(8,128)(2,1)S(1)} %pad_maximum_fusion.refs_1_), channel_id=1, source_target_pairs={{0,4},{1,5},{2,6},{3,7},{4,0},{5,1},{6,2},{7,3},{8,12},{9,13},{10,... | collective-permute-start | bytes 1916936 | tf_op jit(solution)/shard_map/ppermute | solution.py:763
  32.7 15.8 %collective-permute-start.8 = (bf16[2,96,1536]{2,1,0:T(8,128)(2,1)S(1)}, bf16[2,96,1536]{2,1,0:T(8,128)(2,1)S(1)}, u32[]{:S(2)}, u32[]{:S(2)}) collective-permute-start(bf16[2,96,1536]{2,1,0:T(8,128)(2,1)S(1)} %pad_maximum_fusion.1.refs_0_), channel_id=1, source_target_pairs={{0,16},{1,17},{2,18},{3,19},{4,20},{5,21},{6,22},{7,23},{8,24},{9,... | collective-permute-start | bytes 1769480 | tf_op jit(solution)/shard_map/ppermute | solution.py:763
  33.3 15.2 %collective-permute-start.10 = (bf16[2,96,1536]{2,1,0:T(8,128)(2,1)S(1)}, bf16[2,96,1536]{2,1,0:T(8,128)(2,1)S(1)}, u32[]{:S(2)}, u32[]{:S(2)}) collective-permute-start(bf16[2,96,1536]{2,1,0:T(8,128)(2,1)S(1)} %pad_maximum_fusion.1.refs_0_), channel_id=1, source_target_pairs={{0,4},{1,5},{2,6},{3,7},{4,0},{5,1},{6,2},{7,3},{8,12},{9,13},{10,... | collective-permute-start | bytes 1769480 | tf_op jit(solution)/shard_map/ppermute | solution.py:763
  33.5 9.3 %collective-permute-start.12 = (bf16[2,24,3072]{2,1,0:T(8,128)(2,1)S(1)}, bf16[2,24,3072]{2,1,0:T(8,128)(2,1)S(1)}, u32[]{:S(2)}, u32[]{:S(2)}) collective-permute-start(bf16[2,24,3072]{2,1,0:T(8,128)(2,1)S(1)} %pad_maximum_fusion.6), channel_id=1, source_target_pairs={{0,1},{1,0},{2,3},{3,2},{4,5},{5,4},{6,7},{7,6},{8,9},{9,8},{10,11... | collective-permute-start | bytes 884744 | tf_op jit(solution)/shard_map/ppermute | solution.py:763
  42.8 15.8 %collective-permute-start.17 = (bf16[4,96,384]{2,1,0:T(8,128)(2,1)S(1)}, bf16[4,96,384]{2,1,0:T(8,128)(2,1)S(1)}, u32[]{:S(2)}, u32[]{:S(2)}) collective-permute-start(bf16[4,96,384]{2,1,0:T(8,128)(2,1)S(1)} %get-tuple-element.486), channel_id=1, source_target_pairs={{0,2},{1,3},{2,0},{3,1},{4,6},{5,7},{6,4},{7,5},{8,10},{9,11},{10,... | collective-permute-start | bytes 884744 | tf_op jit(solution)/shard_map/ppermute | solution.py:763
  49.4 10.5 %collective-permute-start.13 = (bf16[2,96,1536]{2,1,0:T(8,128)(2,1)S(1)}, bf16[2,96,1536]{2,1,0:T(8,128)(2,1)S(1)}, u32[]{:S(2)}, u32[]{:S(2)}) collective-permute-start(bf16[2,96,1536]{2,1,0:T(8,128)(2,1)S(1)} %collective-permute-done.8.refs_2_), channel_id=1, source_target_pairs={{0,4},{1,5},{2,6},{3,7},{4,0},{5,1},{6,2},{7,3},{8,12},{9,13},{10,... | collective-permute-start | bytes 1769480 | tf_op jit(solution)/shard_map/ppermute | solution.py:763
  49.4 10.5 %collective-permute-start.14 = (bf16[2,96,1664]{2,1,0:T(8,128)(2,1)S(1)}, bf16[2,96,1664]{2,1,0:T(8,128)(2,1)S(1)}, u32[]{:S(2)}, u32[]{:S(2)}) collective-permute-start(bf16[2,96,1664]{2,1,0:T(8,128)(2,1)S(1)} %collective-permute-done.9.refs_3_), channel_id=1, source_target_pairs={{0,4},{1,5},{2,6},{3,7},{4,0},{5,1},{6,2},{7,3},{8,12},{9,13},{10,... | collective-permute-start | bytes 1916936 | tf_op jit(solution)/shard_map/ppermute | solution.py:763
  50.3 8.7 %collective-permute-start.15 = (bf16[96,1536]{1,0:T(8,128)(2,1)S(1)}, bf16[96,1536]{1,0:T(8,128)(2,1)S(1)}, u32[]{:S(2)}, u32[]{:S(2)}) collective-permute-start(bf16[96,1536]{1,0:T(8,128)(2,1)S(1)} %get-tuple-element.269), channel_id=1, source_target_pairs={{0,8},{1,9},{2,10},{3,11},{4,12},{5,13},{6,14},{7,15},{8,0},{9,1},... | collective-permute-start | bytes 884744 | tf_op jit(solution)/shard_map/ppermute | solution.py:763
  51.4 8.4 %collective-permute-start.16 = (bf16[96,1536]{1,0:T(8,128)(2,1)S(1)}, bf16[96,1536]{1,0:T(8,128)(2,1)S(1)}, u32[]{:S(2)}, u32[]{:S(2)}) collective-permute-start(bf16[96,1536]{1,0:T(8,128)(2,1)S(1)} %get-tuple-element.272), channel_id=1, source_target_pairs={{0,16},{1,17},{2,18},{3,19},{4,20},{5,21},{6,22},{7,23},{8,24},{9,... | collective-permute-start | bytes 884744 | tf_op jit(solution)/shard_map/ppermute | solution.py:763
  59.9 13.9 %collective-permute-start.18 = (bf16[2,96,1536]{2,1,0:T(8,128)(2,1)S(1)}, bf16[2,96,1536]{2,1,0:T(8,128)(2,1)}, u32[]{:S(2)}, u32[]{:S(2)}) collective-permute-start(bf16[2,96,1536]{2,1,0:T(8,128)(2,1)S(1)} %pad_maximum_fusion.2.refs_0_), channel_id=1, source_target_pairs={{0,16},{1,17},{2,18},{3,19},{4,20},{5,21},{6,22},{7,23},{8,24},{9,... | collective-permute-start | bytes 1769480 | tf_op jit(solution)/shard_map/ppermute | solution.py:763
  60.5 16.9 %collective-permute-start.20 = (bf16[2,96,1536]{2,1,0:T(8,128)(2,1)S(1)}, bf16[2,96,1536]{2,1,0:T(8,128)(2,1)}, u32[]{:S(2)}, u32[]{:S(2)}) collective-permute-start(bf16[2,96,1536]{2,1,0:T(8,128)(2,1)S(1)} %pad_maximum_fusion.2.refs_0_), channel_id=1, source_target_pairs={{0,4},{1,5},{2,6},{3,7},{4,0},{5,1},{6,2},{7,3},{8,12},{9,13},{10,... | collective-permute-start | bytes 1769480 | tf_op jit(solution)/shard_map/ppermute | solution.py:763
  61.3 16.1 %collective-permute-start.19 = (bf16[2,96,1536]{2,1,0:T(8,128)(2,1)}, bf16[2,96,1536]{2,1,0:T(8,128)(2,1)}, u32[]{:S(2)}, u32[]{:S(2)}) collective-permute-start(bf16[2,96,1536]{2,1,0:T(8,128)(2,1)} %pad_maximum_fusion.3.refs_1_), channel_id=1, source_target_pairs={{0,8},{1,9},{2,10},{3,11},{4,12},{5,13},{6,14},{7,15},{8,0},{9,1},... | collective-permute-start | bytes 1769480 | tf_op jit(solution)/shard_map/ppermute | solution.py:763
  62.3 15.1 %collective-permute-start.21 = (bf16[2,96,1536]{2,1,0:T(8,128)(2,1)}, bf16[2,96,1536]{2,1,0:T(8,128)(2,1)}, u32[]{:S(2)}, u32[]{:S(2)}) collective-permute-start(bf16[2,96,1536]{2,1,0:T(8,128)(2,1)} %pad_maximum_fusion.3.refs_1_), channel_id=1, source_target_pairs={{0,4},{1,5},{2,6},{3,7},{4,0},{5,1},{6,2},{7,3},{8,12},{9,13},{10,... | collective-permute-start | bytes 1769480 | tf_op jit(solution)/shard_map/ppermute | solution.py:763
  63.4 15.9 %collective-permute-start.22 = (bf16[2,4,96,384]{3,2,1,0:T(8,128)(2,1)}, bf16[2,4,96,384]{3,2,1,0:T(8,128)(2,1)}, u32[]{:S(2)}, u32[]{:S(2)}) collective-permute-start(bf16[2,4,96,384]{3,2,1,0:T(8,128)(2,1)} %pad_maximum_fusion.4), channel_id=1, source_target_pairs={{0,1},{1,0},{2,3},{3,2},{4,5},{5,4},{6,7},{7,6},{8,9},{9,8},{10,11... | collective-permute-start | bytes 1769480 | tf_op jit(solution)/shard_map/ppermute | solution.py:763
  79.3 5.6 %collective-permute-start.25 = (bf16[6,384,384]{2,1,0:T(8,128)(2,1)S(1)}, bf16[6,384,384]{2,1,0:T(8,128)(2,1)S(1)}, u32[]{:S(2)}, u32[]{:S(2)}) collective-permute-start(bf16[6,384,384]{2,1,0:T(8,128)(2,1)S(1)} %get-tuple-element.308), channel_id=1, source_target_pairs={{0,4},{1,5},{2,6},{3,7},{4,0},{5,1},{6,2},{7,3},{8,12},{9,13},{10,... | collective-permute-start | bytes 5308424 | tf_op jit(solution)/shard_map/ppermute | solution.py:763
  79.3 4.4 %collective-permute-start.23 = (bf16[2,96,1536]{2,1,0:T(8,128)(2,1)}, bf16[2,96,1536]{2,1,0:T(8,128)(2,1)S(1)}, u32[]{:S(2)}, u32[]{:S(2)}) collective-permute-start(bf16[2,96,1536]{2,1,0:T(8,128)(2,1)} %collective-permute-done.18.refs_2_), channel_id=1, source_target_pairs={{0,4},{1,5},{2,6},{3,7},{4,0},{5,1},{6,2},{7,3},{8,12},{9,13},{10,... | collective-permute-start | bytes 1769480 | tf_op jit(solution)/shard_map/ppermute | solution.py:763
  79.9 4.7 %collective-permute-start.24 = (bf16[2,96,1536]{2,1,0:T(8,128)(2,1)}, bf16[2,96,1536]{2,1,0:T(8,128)(2,1)S(1)}, u32[]{:S(2)}, u32[]{:S(2)}) collective-permute-start(bf16[2,96,1536]{2,1,0:T(8,128)(2,1)} %collective-permute-done.19.refs_3_), channel_id=1, source_target_pairs={{0,4},{1,5},{2,6},{3,7},{4,0},{5,1},{6,2},{7,3},{8,12},{9,13},{10,... | collective-permute-start | bytes 1769480 | tf_op jit(solution)/shard_map/ppermute | solution.py:763
  81.1 17.2 %collective-permute-start.28 = (bf16[2,384,384]{2,1,0:T(8,128)(2,1)S(1)}, bf16[2,384,384]{2,1,0:T(8,128)(2,1)S(1)}, u32[]{:S(2)}, u32[]{:S(2)}) collective-permute-start(bf16[2,384,384]{2,1,0:T(8,128)(2,1)S(1)} %get-tuple-element.328.refs_0_), channel_id=1, source_target_pairs={{0,16},{1,17},{2,18},{3,19},{4,20},{5,21},{6,22},{7,23},{8,24},{9,... | collective-permute-start | bytes 1769480 | tf_op jit(solution)/shard_map/ppermute | solution.py:763
  82.7 15.7 %collective-permute-start.29 = (bf16[2,384,384]{2,1,0:T(8,128)(2,1)S(1)}, bf16[2,384,384]{2,1,0:T(8,128)(2,1)S(1)}, u32[]{:S(2)}, u32[]{:S(2)}) collective-permute-start(bf16[2,384,384]{2,1,0:T(8,128)(2,1)S(1)} %get-tuple-element.329.refs_1_), channel_id=1, source_target_pairs={{0,8},{1,9},{2,10},{3,11},{4,12},{5,13},{6,14},{7,15},{8,0},{9,1},... | collective-permute-start | bytes 1769480 | tf_op jit(solution)/shard_map/ppermute | solution.py:763
  83.7 14.6 %collective-permute-start.30 = (bf16[2,384,384]{2,1,0:T(8,128)(2,1)S(1)}, bf16[2,384,384]{2,1,0:T(8,128)(2,1)S(1)}, u32[]{:S(2)}, u32[]{:S(2)}) collective-permute-start(bf16[2,384,384]{2,1,0:T(8,128)(2,1)S(1)} %get-tuple-element.328.refs_0_), channel_id=1, source_target_pairs={{0,4},{1,5},{2,6},{3,7},{4,0},{5,1},{6,2},{7,3},{8,12},{9,13},{10,... | collective-permute-start | bytes 1769480 | tf_op jit(solution)/shard_map/ppermute | solution.py:763
  84.6 13.8 %collective-permute-start.31 = (bf16[2,384,384]{2,1,0:T(8,128)(2,1)S(1)}, bf16[2,384,384]{2,1,0:T(8,128)(2,1)S(1)}, u32[]{:S(2)}, u32[]{:S(2)}) collective-permute-start(bf16[2,384,384]{2,1,0:T(8,128)(2,1)S(1)} %get-tuple-element.329.refs_1_), channel_id=1, source_target_pairs={{0,4},{1,5},{2,6},{3,7},{4,0},{5,1},{6,2},{7,3},{8,12},{9,13},{10,... | collective-permute-start | bytes 1769480 | tf_op jit(solution)/shard_map/ppermute | solution.py:763
  99.0 18.5 %collective-permute-start.26 = (bf16[2,384,384]{2,1,0:T(8,128)(2,1)S(1)}, bf16[2,384,384]{2,1,0:T(8,128)(2,1)S(1)}, u32[]{:S(2)}, u32[]{:S(2)}) collective-permute-start(bf16[2,384,384]{2,1,0:T(8,128)(2,1)S(1)} %get-tuple-element.324), channel_id=1, source_target_pairs={{0,16},{1,17},{2,18},{3,19},{4,20},{5,21},{6,22},{7,23},{8,24},{9,... | collective-permute-start | bytes 1769480 | tf_op jit(solution)/shard_map/ppermute | solution.py:763
  100.5 17.0 %collective-permute-start.27 = (bf16[2,384,384]{2,1,0:T(8,128)(2,1)S(1)}, bf16[2,384,384]{2,1,0:T(8,128)(2,1)S(1)}, u32[]{:S(2)}, u32[]{:S(2)}) collective-permute-start(bf16[2,384,384]{2,1,0:T(8,128)(2,1)S(1)} %get-tuple-element.325), channel_id=1, source_target_pairs={{0,8},{1,9},{2,10},{3,11},{4,12},{5,13},{6,14},{7,15},{8,0},{9,1},... | collective-permute-start | bytes 1769480 | tf_op jit(solution)/shard_map/ppermute | solution.py:763
  117.5 6.7 %collective-permute-start.34 = (bf16[384,3072]{1,0:T(8,128)(2,1)S(1)}, bf16[384,3072]{1,0:T(8,128)(2,1)S(1)}, u32[]{:S(2)}, u32[]{:S(2)}) collective-permute-start(bf16[384,3072]{1,0:T(8,128)(2,1)S(1)} %get-tuple-element.350.du_ref.refs_1_), channel_id=1, source_target_pairs={{0,4},{1,5},{2,6},{3,7},{4,0},{5,1},{6,2},{7,3},{8,12},{9,13},{10,... | collective-permute-start | bytes 7077896 | tf_op jit(solution)/shard_map/ppermute | solution.py:763
  124.2 12.5 %collective-permute-start.35 = (bf16[384,2304]{1,0:T(8,128)(2,1)S(1)}, bf16[384,2304]{1,0:T(8,128)(2,1)S(1)}, u32[]{:S(2)}, u32[]{:S(2)}) collective-permute-start(bf16[384,2304]{1,0:T(8,128)(2,1)S(1)} %unattend.1.dqkv_ref.refs_1_), channel_id=1, source_target_pairs={{0,4},{1,5},{2,6},{3,7},{4,0},{5,1},{6,2},{7,3},{8,12},{9,13},{10,... | collective-permute-start | bytes 5308424 | tf_op jit(solution)/shard_map/ppermute | solution.py:763
  124.7 8.3 %collective-permute-start.36 = (bf16[384,768]{1,0:T(8,128)(2,1)S(1)}, bf16[384,768]{1,0:T(8,128)(2,1)S(1)}, u32[]{:S(2)}, u32[]{:S(2)}) collective-permute-start(bf16[384,768]{1,0:T(8,128)(2,1)S(1)} %get-tuple-element.352.da_ref.refs_5_), channel_id=1, source_target_pairs={{0,4},{1,5},{2,6},{3,7},{4,0},{5,1},{6,2},{7,3},{8,12},{9,13},{10,... | collective-permute-start | bytes 1769480 | tf_op jit(solution)/shard_map/ppermute | solution.py:763
  127.8 15.7 %collective-permute-start.42 = (bf16[2,96,1536]{2,1,0:T(8,128)(2,1)S(1)}, bf16[2,96,1536]{2,1,0:T(8,128)(2,1)S(1)}, u32[]{:S(2)}, u32[]{:S(2)}) collective-permute-start(bf16[2,96,1536]{2,1,0:T(8,128)(2,1)S(1)} %get-tuple-element.391), channel_id=1, source_target_pairs={{0,16},{1,17},{2,18},{3,19},{4,20},{5,21},{6,22},{7,23},{8,24},{9,... | collective-permute-start | bytes 1769480 | tf_op jit(solution)/shard_map/ppermute | solution.py:763
  128.7 16.1 %collective-permute-start.43 = (bf16[2,96,1536]{2,1,0:T(8,128)(2,1)S(1)}, bf16[2,96,1536]{2,1,0:T(8,128)(2,1)S(1)}, u32[]{:S(2)}, u32[]{:S(2)}) collective-permute-start(bf16[2,96,1536]{2,1,0:T(8,128)(2,1)S(1)} %get-tuple-element.392), channel_id=1, source_target_pairs={{0,8},{1,9},{2,10},{3,11},{4,12},{5,13},{6,14},{7,15},{8,0},{9,1},... | collective-permute-start | bytes 1769480 | tf_op jit(solution)/shard_map/ppermute | solution.py:763
  129.7 15.1 %collective-permute-start.44 = (bf16[2,4,96,384]{3,2,1,0:T(8,128)(2,1)S(1)}, bf16[2,4,96,384]{3,2,1,0:T(8,128)(2,1)S(1)}, u32[]{:S(2)}, u32[]{:S(2)}) collective-permute-start(bf16[2,4,96,384]{3,2,1,0:T(8,128)(2,1)S(1)} %get-tuple-element.393), channel_id=1, source_target_pairs={{0,1},{1,0},{2,3},{3,2},{4,5},{5,4},{6,7},{7,6},{8,9},{9,8},{10,11... | collective-permute-start | bytes 1769480 | tf_op jit(solution)/shard_map/ppermute | solution.py:763
  139.9 17.6 %collective-permute-start.41 = (bf16[2,96,1664]{2,1,0:T(8,128)(2,1)S(1)}, bf16[2,96,1664]{2,1,0:T(8,128)(2,1)S(1)}, u32[]{:S(2)}, u32[]{:S(2)}) collective-permute-start(bf16[2,96,1664]{2,1,0:T(8,128)(2,1)S(1)} %get-tuple-element.388), channel_id=1, source_target_pairs={{0,8},{1,9},{2,10},{3,11},{4,12},{5,13},{6,14},{7,15},{8,0},{9,1},... | collective-permute-start | bytes 1916936 | tf_op jit(solution)/shard_map/ppermute | solution.py:763
  141.0 15.2 %collective-permute-start.40 = (bf16[2,96,1536]{2,1,0:T(8,128)(2,1)S(1)}, bf16[2,96,1536]{2,1,0:T(8,128)(2,1)S(1)}, u32[]{:S(2)}, u32[]{:S(2)}) collective-permute-start(bf16[2,96,1536]{2,1,0:T(8,128)(2,1)S(1)} %get-tuple-element.387), channel_id=1, source_target_pairs={{0,16},{1,17},{2,18},{3,19},{4,20},{5,21},{6,22},{7,23},{8,24},{9,... | collective-permute-start | bytes 1769480 | tf_op jit(solution)/shard_map/ppermute | solution.py:763
  145.3 20.2 %collective-permute-start.47 = (bf16[2,4,24,1536]{3,2,1,0:T(8,128)(2,1)S(1)}, bf16[2,4,24,1536]{3,2,1,0:T(8,128)(2,1)S(1)}, u32[]{:S(2)}, u32[]{:S(2)}) collective-permute-start(bf16[2,4,24,1536]{3,2,1,0:T(8,128)(2,1)S(1)} %get-tuple-element.418), channel_id=1, source_target_pairs={{0,1},{1,0},{2,3},{3,2},{4,5},{5,4},{6,7},{7,6},{8,9},{9,8},{10,11... | collective-permute-start | bytes 1769480 | tf_op jit(solution)/shard_map/ppermute | solution.py:763
  146.9 17.9 %collective-permute-start.48 = (bf16[4,96,384]{2,1,0:T(8,128)(2,1)S(1)}, bf16[4,96,384]{2,1,0:T(8,128)(2,1)S(1)}, u32[]{:S(2)}, u32[]{:S(2)}) collective-permute-start(bf16[4,96,384]{2,1,0:T(8,128)(2,1)S(1)} %get-tuple-element.419), channel_id=1, source_target_pairs={{0,2},{1,3},{2,0},{3,1},{4,6},{5,7},{6,4},{7,5},{8,10},{9,11},{10,... | collective-permute-start | bytes 884744 | tf_op jit(solution)/shard_map/ppermute | solution.py:763
  157.8 13.2 %collective-permute-start.46 = (bf16[96,1664]{1,0:T(8,128)(2,1)S(1)}, bf16[96,1664]{1,0:T(8,128)(2,1)S(1)}, u32[]{:S(2)}, u32[]{:S(2)}) collective-permute-start(bf16[96,1664]{1,0:T(8,128)(2,1)S(1)} %get-tuple-element.416), channel_id=1, source_target_pairs={{0,16},{1,17},{2,18},{3,19},{4,20},{5,21},{6,22},{7,23},{8,24},{9,... | collective-permute-start | bytes 958472 | tf_op jit(solution)/shard_map/ppermute | solution.py:763
  159.3 11.7 %collective-permute-start.45 = (bf16[96,1536]{1,0:T(8,128)(2,1)S(1)}, bf16[96,1536]{1,0:T(8,128)(2,1)S(1)}, u32[]{:S(2)}, u32[]{:S(2)}) collective-permute-start(bf16[96,1536]{1,0:T(8,128)(2,1)S(1)} %get-tuple-element.415), channel_id=1, source_target_pairs={{0,8},{1,9},{2,10},{3,11},{4,12},{5,13},{6,14},{7,15},{8,0},{9,1},... | collective-permute-start | bytes 884744 | tf_op jit(solution)/shard_map/ppermute | solution.py:763
  165.8 4.6 %collective-permute-start.49 = (bf16[96,384]{1,0:T(8,128)(2,1)S(1)}, bf16[96,384]{1,0:T(8,128)(2,1)S(1)}, u32[]{:S(2)}, u32[]{:S(2)}) collective-permute-start(bf16[96,384]{1,0:T(8,128)(2,1)S(1)} %get-tuple-element.428), channel_id=1, source_target_pairs={{0,8},{1,9},{2,10},{3,11},{4,12},{5,13},{6,14},{7,15},{8,0},{9,1},... | collective-permute-start | bytes 221192 | tf_op jit(solution)/shard_map/ppermute | solution.py:763
  168.5 14.0 %collective-permute-start.52 = (bf16[4,24,1536]{2,1,0:T(8,128)(2,1)S(1)}, bf16[4,24,1536]{2,1,0:T(8,128)(2,1)S(1)}, u32[]{:S(2)}, u32[]{:S(2)}) collective-permute-start(bf16[4,24,1536]{2,1,0:T(8,128)(2,1)S(1)} %get-tuple-element.437), channel_id=1, source_target_pairs={{0,2},{1,3},{2,0},{3,1},{4,6},{5,7},{6,4},{7,5},{8,10},{9,11},{10,... | collective-permute-start | bytes 884744 | tf_op jit(solution)/shard_map/ppermute | solution.py:763
  171.2 11.7 %collective-permute-start.51 = (bf16[2,24,3200]{2,1,0:T(8,128)(2,1)S(1)}, bf16[2,24,3200]{2,1,0:T(8,128)(2,1)S(1)}, u32[]{:S(2)}, u32[]{:S(2)}) collective-permute-start(bf16[2,24,3200]{2,1,0:T(8,128)(2,1)S(1)} %get-tuple-element.436), channel_id=1, source_target_pairs={{0,1},{1,0},{2,3},{3,2},{4,5},{5,4},{6,7},{7,6},{8,9},{9,8},{10,11... | collective-permute-start | bytes 921608 | tf_op jit(solution)/shard_map/ppermute | solution.py:763
  183.2 7.5 %collective-permute-start.53 = (bf16[24,3200]{1,0:T(8,128)(2,1)S(1)}, bf16[24,3200]{1,0:T(8,128)(2,1)S(1)}, u32[]{:S(2)}, u32[]{:S(2)}) collective-permute-start(bf16[24,3200]{1,0:T(8,128)(2,1)S(1)} %get-tuple-element.446), channel_id=1, source_target_pairs={{0,2},{1,3},{2,0},{3,1},{4,6},{5,7},{6,4},{7,5},{8,10},{9,11},{10,... | collective-permute-start | bytes 460808 | tf_op jit(solution)/shard_map/ppermute | solution.py:763
  (55 other events, 537.5 us)

commit v4 on v3

--- a/solution.py
+++ b/solution.py
@@ -682,20 +682,25 @@
     return kernel(body, "settle_halves", outs, (keep, other_l, other_r), "vvv")
 
 
-def settle_z(mine, other):
+def settle_z(mine, other, squares, devices):
     rows, width = mine.shape
 
-    def body(mine, other, grad, square, last, turned):
+    def body(mine, other, *refs):
+        more, (grad, square, last, turned) = refs[: len(squares)], refs[len(squares) :]
         value = mine[...] + other[...].astype(f32)
         grad[...] = value
-        square[...] = jnp.full(square.shape, jnp.sum(value * value))
+        total = jnp.sum(value * value)
+        for ref in more:
+            total = total + ref[0:1, :]
+        square[...] = jnp.broadcast_to(total, square.shape)
         turned[...] = jnp.zeros_like(turned)
         turned[:rows] = value[:, width - 128 :]
         last[...] = turned[...].T[:8]
 
-    outs = [(mine.shape, f32), ((8, 128), f32), ((8, 128), f32)]
+    outs = [(mine.shape, f32), ((devices, 128), f32), ((8, 128), f32)]
     scratch = [pltpu.VMEM((128, 128), f32)]
-    return kernel(body, "settle_z", outs, (mine, other), "vv", scratch)
+    args = (mine, other, *squares)
+    return kernel(body, "settle_z", outs, args, "v" * len(args), scratch)
 
 
 def update(squares, limit, grads, states, vec_grad, vec_states):
@@ -706,7 +711,7 @@
         state_refs, refs = refs[: 3 * count], refs[3 * count :]
         vec_ref, vec_m, vec_v, norm_ref, out_refs = *refs[:4], refs[4:]
         norm = jnp.sqrt(jnp.sum(square_ref[...], axis=0, keepdims=True)[:, 0:1])
-        norm_ref[...] = jnp.broadcast_to(norm, norm_ref.shape)
+        norm_ref[...] = norm
         factor = jnp.minimum(1.0, limit / (norm + 1e-06))
         for place in range(count):
             w, m, v = (ref[...] for ref in state_refs[3 * place : 3 * place + 3])
@@ -719,7 +724,7 @@
         out_refs[-1][...] = second
 
     flat = [array for state in states for array in state]
-    outs = [((8, 128), f32)] + [(array.shape, f32) for array in (*flat, *vec_states)]
+    outs = [((1, 1), f32)] + [(array.shape, f32) for array in (*flat, *vec_states)]
     args = (squares, *(grad.array for grad in grads), *flat, vec_grad, *vec_states)
     return kernel(body, "update", outs, args, "v" * len(args), (), 32)
 
@@ -805,7 +810,7 @@
     (other,) = yield [(send, 1)]
     mine, send = add_next(mine, other)
     (other,) = yield [(send, 2)]
-    return settle_z(mine, other)
+    return mine, other
 
 
 def scatter_pairs(z, send_l, send_r, keep_l, keep_r):
@@ -995,15 +1000,15 @@
     input_grad = stage([give_a, give_b], input_grad)
     input_grad = tick([give_a, give_b], input_grad)
     if paired:
-        give_a, give_b, give_c = give_a.result, give_b.result, give_c.result
-        vec_grad = give_a[2]
-        local_sq = give_a[1] + give_b[1] + give_c[1]
+        (grad_b, square_b), (grad_c, square_c) = give_b.result, give_c.result
+        grad_a, squares, vec_grad = settle_z(*give_a.result, (square_b, square_c), devices_all)
     else:
         rows = jnp.stack([dg1[0], dg2[0], dr[0]], axis=0)
         rows = lax.psum_scatter(rows, AXES, scatter_dimension=1, tiled=True)
         vec_grad = jnp.pad(rows, ((0, 5), (0, 128 - shard_width)))
-        local_sq = give_a[1] + give_b[1] + give_c[1] + jnp.sum(rows * rows)
-    squares = jnp.broadcast_to(local_sq[:1], (devices_all, 128))
+        (grad_a, square_a), (grad_b, square_b), (grad_c, square_c) = give_a, give_b, give_c
+        local_sq = square_a + square_b + square_c + jnp.sum(rows * rows)
+        squares = jnp.broadcast_to(local_sq[:1], (devices_all, 128))
     squares = lax.all_to_all(squares, AXES, 0, 0, tiled=True)
     params_all = 4 * model_width * model_width + 2 * model_width * ff_width + 3 * model_width
     selected_all = seq_count * top_count * devices_all
@@ -1012,10 +1017,10 @@
         squares,
         clip_limit,
         [
-            View(give_a[0], qkv_width),
-            View(give_a[0], model_width, qkv_width),
-            View(give_b[0]),
-            View(give_c[0]),
+            View(grad_a, qkv_width),
+            View(grad_a, model_width, qkv_width),
+            View(grad_b),
+            View(grad_c),
         ],
         [
             (w_qkv, m_qkv, v_qkv),

time: 208 us -> 207 us (level)
  no operation moved by 1% of the time
where the time goes in v4:
time: 207 us; the launch traced here: 205 us
  waiting for transfers between devices  62.6 us (30%)
  starting transfers between devices  55.1 us (27%)
  Pallas kernels  52.9 us (26%)
  blocking collectives  11.1 us (5%)
  matrix products  10.5 us (5%)
  local copies, waits for them, and re-layouts  7.38 us (4%)
  other arithmetic  3.37 us (2%)
    ppermute x56, waiting for transfers between devices, swap(): return lax.ppermute(array, AXES, [(i, i ^ bit) for i in range(count)])  62.6 us
    ppermute x56, starting transfers between devices, swap(): return lax.ppermute(array, AXES, [(i, i ^ bit) for i in range(count)])  55.1 us
    pallas_call x28, Pallas kernels, kernel(): pl.pallas_call(body, out_shape=[jax.ShapeDtypeStruct(*out) if place < hel...  52.9 us
    all_to_all x1, blocking collectives, per_device(): squares = lax.all_to_all(squares, AXES, 0, 0, tiled=True)  11.1 us
    dot_general x2, matrix products, place(): jnp.einsum('skl,skd->sld', hot_low, rows, preferred_element_type=f32)  6.11 us
    unnamed x94, local copies, waits for them, and re-layouts  6.02 us
    dot_general x2, matrix products, pick(): jnp.einsum('skl,sld->skd', hot_low, blocks, preferred_element_type=f32)  4.37 us
  transfers between devices with their start and end apart: 56, of which 27 were waited for; matrix products, arithmetic and copies ran while one was open for 7% of the time, Pallas kernels for 24%

profile of v4, /device:TPU:0, one launch (start us, length us, event | category | flops | bytes accessed | tf_op | source)
XLA Modules:
  0.0 204.7 jit_solution(6717015848318843645)
XLA Ops:
  1.8 3.0 %collective-permute-start = (bf16[24,3200]{1,0:T(8,128)(2,1)S(1)}, bf16[24,3200]{1,0:T(8,128)(2,1)S(1)}, u32[]{:S(2)}, u32[]{:S(2)}) collective-permute-start(bf16[24,3200]{1,0:T(8,128)(2,1)S(1)} %gather_input.1.refs_0_), channel_id=1, source_target_pairs={{0,1},{1,0},{2,3},{3,2},{4,5},{5,4},{6,7},{7,6},{8,9},{9,8},{10,11... | collective-permute-start | bytes 460808 | tf_op jit(solution)/shard_map/ppermute | solution.py:768
  4.8 2.6 %collective-permute-start.1 = (bf16[24,3200]{1,0:T(8,128)(2,1)S(1)}, bf16[24,3200]{1,0:T(8,128)(2,1)S(1)}, u32[]{:S(2)}, u32[]{:S(2)}) collective-permute-start(bf16[24,3200]{1,0:T(8,128)(2,1)S(1)} %gather_input.1.refs_0_), channel_id=1, source_target_pairs={{0,2},{1,3},{2,0},{3,1},{4,6},{5,7},{6,4},{7,5},{8,10},{9,11},{10,... | collective-permute-start | bytes 460808 | tf_op jit(solution)/shard_map/ppermute | solution.py:768
  7.4 3.4 %fusion.3 = bf16[3,128,768]{2,1,0:T(8,128)(2,1)S(1)} fusion(bf16[3,1024,768]{2,1,0:T(8,128)(2,1)} %bitcast.74, s32[3,128]{1,0:T(4,128)} %param.22), kind=kOutput, calls=%fused_computation.7 | convolution fusion | flops 604667904 | bytes 5309952 | tf_op jit(solution)/shard_map/skl,sld->skd/dot_general | solution.py:900
  13.0 6.2 %collective-permute-done.1.refs_2_ = bf16[24,3200]{1,0:T(8,128)(2,1)S(1)} collective-permute-done((bf16[24,3200]{1,0:T(8,128)(2,1)S(1)}, bf16[24,3200]{1,0:T(8,128)(2,1)S(1)}, u32[]{:S(2)}, u32[]{:S(2)}) %collective-permute-start.1) | collective-permute-done | bytes 153632 | tf_op jit(solution)/shard_map/ppermute | solution.py:768
  19.4 1.6 collective-permute-start.4
  21.0 1.6 collective-permute-start.3
  22.5 3.4 %collective-permute-start.5 = (bf16[24,3072]{1,0:T(8,128)(2,1)S(1)}, bf16[24,3072]{1,0:T(8,128)(2,1)S(1)}, u32[]{:S(2)}, u32[]{:S(2)}) collective-permute-start(bf16[24,3072]{1,0:T(8,128)(2,1)S(1)} %convert_element_type.21.refs_0_), channel_id=1, source_target_pairs={{0,2},{1,3},{2,0},{3,1},{4,6},{5,7},{6,4},{7,5},{8,10},{9,11},{10,... | collective-permute-start | bytes 442376 | tf_op jit(solution)/shard_map/ppermute | solution.py:768
  27.1 3.3 %collective-permute-done.6.refs_1_ = bf16[96,384]{1,0:T(8,128)(2,1)S(1)} collective-permute-done((bf16[96,384]{1,0:T(8,128)(2,1)S(1)}, bf16[96,384]{1,0:T(8,128)(2,1)S(1)}, u32[]{:S(2)}, u32[]{:S(2)}) %collective-permute-start.6) | collective-permute-done | bytes 73760 | tf_op jit(solution)/shard_map/ppermute | solution.py:768
  33.5 1.7 collective-permute-start.12
  35.3 7.5 %collective-permute-done.12 = bf16[2,24,3072]{2,1,0:T(8,128)(2,1)S(1)} collective-permute-done((bf16[2,24,3072]{2,1,0:T(8,128)(2,1)S(1)}, bf16[2,24,3072]{2,1,0:T(8,128)(2,1)S(1)}, u32[]{:S(2)}, u32[]{:S(2)}) %collective-permute-start.12) | collective-permute-done | bytes 294944 | tf_op jit(solution)/shard_map/ppermute | solution.py:768
  42.8 2.8 %collective-permute-start.17 = (bf16[4,96,384]{2,1,0:T(8,128)(2,1)S(1)}, bf16[4,96,384]{2,1,0:T(8,128)(2,1)S(1)}, u32[]{:S(2)}, u32[]{:S(2)}) collective-permute-start(bf16[4,96,384]{2,1,0:T(8,128)(2,1)S(1)} %get-tuple-element.486), channel_id=1, source_target_pairs={{0,2},{1,3},{2,0},{3,1},{4,6},{5,7},{6,4},{7,5},{8,10},{9,11},{10,... | collective-permute-start | bytes 884744 | tf_op jit(solution)/shard_map/ppermute | solution.py:768
  45.6 2.9 %collective-permute-done.8.refs_2_ = bf16[2,96,1536]{2,1,0:T(8,128)(2,1)S(1)} collective-permute-done((bf16[2,96,1536]{2,1,0:T(8,128)(2,1)S(1)}, bf16[2,96,1536]{2,1,0:T(8,128)(2,1)S(1)}, u32[]{:S(2)}, u32[]{:S(2)}) %collective-permute-start.8) | collective-permute-done | bytes 589856 | tf_op jit(solution)/shard_map/ppermute | solution.py:768
  52.0 6.6 %collective-permute-done.17.refs_5_ = bf16[4,96,384]{2,1,0:T(8,128)(2,1)S(1)} collective-permute-done((bf16[4,96,384]{2,1,0:T(8,128)(2,1)S(1)}, bf16[4,96,384]{2,1,0:T(8,128)(2,1)S(1)}, u32[]{:S(2)}, u32[]{:S(2)}) %collective-permute-start.17) | collective-permute-done | bytes 294944 | tf_op jit(solution)/shard_map/ppermute | solution.py:768
  63.4 1.7 collective-permute-start.22
  65.3 8.0 %attend.1 = (bf16[2,384,384]{2,1,0:T(8,128)(2,1)S(1)}, bf16[6,384,384]{2,1,0:T(8,128)(2,1)S(1)}, bf16[384,768]{1,0:T(8,128)(2,1)S(1)}, f32[384,128]{1,0:T(8,128)...) custom-call(s32[1]{0:T(128)} %bitcast.24.me_ref, ...), custom_call_target="tpu_custom_call" | custom-call | flops 1 | bytes 1 | tf_op jit(solution)/shard_map/attend/pallas_call | solution.py:55
  73.8 3.6 %collective-permute-done.19.refs_3_ = bf16[2,96,1536]{2,1,0:T(8,128)(2,1)} collective-permute-done((bf16[2,96,1536]{2,1,0:T(8,128)(2,1)}, bf16[2,96,1536]{2,1,0:T(8,128)(2,1)}, u32[]{:S(2)}, u32[]{:S(2)}) %collective-permute-start.19) | collective-permute-done | bytes 589856 | tf_op jit(solution)/shard_map/ppermute | solution.py:768
  77.4 1.9 collective-permute-done.22
  81.1 1.6 collective-permute-start.28
  85.4 10.1 %climb.1 = (bf16[384,1536]{1,0:T(8,128)(2,1)S(1)}, bf16[384,1536]{1,0:T(8,128)(2,1)S(1)}, bf16[384,1536]{1,0:T(8,128)(2,1)S(1)}, bf16[2,384,384]{2,1,0:T(8,128)(...) custom-call(s32[1]{0:T(128)} %bitcast.24.me_ref, bf16[2,96,1536]{2,1,0:T(8,128)(2,1)} %copy-done.24, ...), custom_call_target="tpu_custom_call" | custom-call | flops 1 | bytes 1 | tf_op jit(solution)/shard_map/climb/pallas_call | solution.py:55
  95.7 2.6 %outer_c.1 = (bf16[2,384,384]{2,1,0:T(8,128)(2,1)S(1)}, bf16[2,384,384]{2,1,0:T(8,128)(2,1)S(1)}, f32[2,384,384]{2,1,0:T(8,128)S(1)}, f32[2,384,384]{2,1,0:T(8,128)S(1)}) custom-call(bf16[384,1536]{1,0:T(8,128)(2,1)S(1)} %get-tuple-element.318.refs_0_.own_ref, bf16[384,768]{1,0:T(8,128)(2,1)S(1)} %get-tuple-element.319.refs_1_.refs_9_, ...), custom_call_target="tpu_custom_call" | custom-call | flops 1 | bytes 1 | tf_op jit(solution)/shard_map/outer_c/pallas_call | solution.py:55
  99.0 1.5 collective-permute-start.26
  103.2 7.1 %descend.1 = (bf16[384,3072]{1,0:T(8,128)(2,1)S(1)}, bf16[3072,768]{1,0:T(8,128)(2,1)}) custom-call(s32[1]{0:T(128)} %bitcast.24.me_ref, bf16[2,384,384]{2,1,0:T(8,128)(2,1)} %copy-done.8, bf16[2,384,384]{2,1,0:T(8,128)(2,1)} %copy-done.9, bf16[2,384,384]{2,1,0:T(8,128)(2,1)} %copy-done.31, bf16[2,384,384]{2,1,0:T(8,128)(2,1)} %copy-done.33, ...), custom_call_target="tpu_custom_call" | custom-call | flops 1 | bytes 1 | tf_op jit(solution)/shard_map/descend/pallas_call | solution.py:55
  110.3 2.3 %copy-done = bf16[3072,768]{1,0:T(8,128)(2,1)S(1)} copy-done((bf16[3072,768]{1,0:T(8,128)(2,1)S(1)}, bf16[3072,768]{1,0:T(8,128)(2,1)}, u32[]{:S(2)}) %copy-start) | copy-done | bytes 4718616
  112.7 2.4 %finish_mlp.1 = (bf16[384,768]{1,0:T(8,128)(2,1)S(1)}, f32[384,128]{1,0:T(8,128)S(1)}, f32[8,768]{1,0:T(8,128)S(1)}) custom-call(bf16[3072,768]{1,0:T(8,128)(2,1)S(1)} %copy-done, bf16[384,1536]{1,0:T(8,128)(2,1)S(1)} %get-tuple-element.318.refs_0_.own_ref, bf16[384,1536]{1,0:T(8,128)(2,1)S(1)} %get-tuple-element.347.send_ref, ...), custom_call_target="tpu_custom_call" | custom-call | flops 1 | bytes 1 | tf_op jit(solution)/shard_map/finish_mlp/pallas_call | solution.py:55
  115.1 2.4 %unclimb.1 = (f32[384,768]{1,0:T(8,128)S(1)}, bf16[384,768]{1,0:T(8,128)(2,1)S(1)}, f32[8,768]{1,0:T(8,128)S(1)}) custom-call(bf16[768,3072]{1,0:T(8,128)(2,1)S(1)} %bitcast.60, bf16[384,3072]{1,0:T(8,128)(2,1)S(1)} %get-tuple-element.350.du_ref.refs_1_, bf16[384,768]{1,0:T(8,128)(2,1)S(1)} %bitcast.53, f32[384,768]{1,0:T(8,128)S(1)} %get-tuple-element.341.add_ref, ...), custom_call_target="tpu_custom_call" | custom-call | flops 1 | bytes 1 | tf_op jit(solution)/shard_map/unclimb/pallas_call | solution.py:55
  117.6 6.6 %unattend.1.dqkv_ref.refs_1_ = bf16[384,2304]{1,0:T(8,128)(2,1)S(1)} custom-call(bf16[768,768]{1,0:T(8,128)(2,1)S(1)} %copy-done.6, bf16[384,768]{1,0:T(8,128)(2,1)S(1)} %get-tuple-element.352.da_ref.refs_5_, bf16[384,2304]{1,0:T(8,128)(2,1)S(1)} %copy-done.3, f32[18,256,128]{2,1,0:T(8,128)S(1)} %copy-done.2), custom_call_target="tpu_custom_call" | custom-call | flops 1 | bytes 1 | tf_op jit(solution)/shard_map/unattend/pallas_call | solution.py:55
  125.2 2.6 %outer_b.1 = (bf16[2,96,1536]{2,1,0:T(8,128)(2,1)S(1)}, bf16[2,96,1536]{2,1,0:T(8,128)(2,1)S(1)}, f32[2,96,1536]{2,1,0:T(8,128)S(1)}, f32[2,96,1536]{2,1,0:T(8,128)S(1)}) custom-call(bf16[2,384,384]{2,1,0:T(8,128)(2,1)S(1)} %get-tuple-element.357.refs_0_.refs_2_, bf16[384,3072]{1,0:T(8,128)(2,1)S(1)} %get-tuple-element.350.du_ref.refs_1_, ...), custom_call_target="tpu_custom_call" | custom-call | flops 1 | bytes 1 | tf_op jit(solution)/shard_map/outer_b/pallas_call | solution.py:55
  129.7 1.3 collective-permute-start.44
  131.0 2.0 finish_rows.1
  137.1 2.8 %outer_a.1 = (bf16[2,96,1536]{2,1,0:T(8,128)(2,1)S(1)}, bf16[2,96,1664]{2,1,0:T(8,128)(2,1)S(1)}, f32[2,96,1536]{2,1,0:T(8,128)S(1)}, f32[2,96,1664]{2,1,0:T(8,128)S(1)}) custom-call(bf16[2,384,384]{2,1,0:T(8,128)(2,1)S(1)} %get-tuple-element.303.refs_0_.refs_4_, bf16[384,2304]{1,0:T(8,128)(2,1)S(1)} %unattend.1.dqkv_ref.refs_1_, ...), custom_call_target="tpu_custom_call" | custom-call | flops 1 | bytes 1 | tf_op jit(solution)/shard_map/outer_a/pallas_call | solution.py:55
  145.3 1.6 collective-permute-start.47
  146.9 1.3 collective-permute-start.48
  148.3 3.2 %convert_select_fusion.1 = bf16[3,1024,768]{2,1,0:T(8,128)(2,1)} fusion(bf16[3,1024,768]{2,1,0:T(8,128)(2,1)S(1)} %bitcast.77, pred[3,1024]{1,0:T(4,128)(4,1)S(1)} %fusion, bf16[3,128,768]{2,1,0:T(8,128)(2,1)S(1)} %bitcast.64, s32[3,128]{1,0:T(4,128)S(1)} %copy-done.25), kind=kOutput, calls=%fused_computation.1 | convolution fusion | flops 609091584 | bytes 10031616 | tf_op jit(solution)/shard_map/skl,skd->sld/dot_general | solution.py:905
  151.4 4.8 %collective-permute-done.40.other_l = bf16[2,96,1536]{2,1,0:T(8,128)(2,1)S(1)} collective-permute-done((bf16[2,96,1536]{2,1,0:T(8,128)(2,1)S(1)}, bf16[2,96,1536]{2,1,0:T(8,128)(2,1)S(1)}, u32[]{:S(2)}, u32[]{:S(2)}) %collective-permute-start.40) | collective-permute-done | bytes 589856 | tf_op jit(solution)/shard_map/ppermute | solution.py:768
  156.2 1.3 collective-permute-done.41.other_r
  157.8 1.6 collective-permute-start.46
  160.3 4.5 %collective-permute-done.48.other = bf16[4,96,384]{2,1,0:T(8,128)(2,1)S(1)} collective-permute-done((bf16[4,96,384]{2,1,0:T(8,128)(2,1)S(1)}, bf16[4,96,384]{2,1,0:T(8,128)(2,1)S(1)}, u32[]{:S(2)}, u32[]{:S(2)}) %collective-permute-start.48) | collective-permute-done | bytes 294944 | tf_op jit(solution)/shard_map/ppermute | solution.py:768
  166.6 1.8 collective-permute-start.50
  168.5 1.9 collective-permute-start.52
  171.2 2.8 %collective-permute-start.51 = (bf16[2,24,3200]{2,1,0:T(8,128)(2,1)S(1)}, bf16[2,24,3200]{2,1,0:T(8,128)(2,1)S(1)}, u32[]{:S(2)}, u32[]{:S(2)}) collective-permute-start(bf16[2,24,3200]{2,1,0:T(8,128)(2,1)S(1)} %get-tuple-element.436), channel_id=1, source_target_pairs={{0,1},{1,0},{2,3},{3,2},{4,5},{5,4},{6,7},{7,6},{8,9},{9,8},{10,11... | collective-permute-start | bytes 921608 | tf_op jit(solution)/shard_map/ppermute | solution.py:768
  174.0 3.0 %convert_select_fusion = bf16[3,1024,768]{2,1,0:T(8,128)(2,1)} fusion(bf16[3,1024,768]{2,1,0:T(8,128)(2,1)S(1)} %bitcast.81, pred[3,1024]{1,0:T(4,128)(4,1)S(1)} %fusion, bf16[3,128,768]{2,1,0:T(8,128)(2,1)S(1)} %bitcast.63, s32[3,128]{1,0:T(4,128)S(1)} %copy-done.25), kind=kOutput, calls=%fused_computation | convolution fusion | flops 609091584 | bytes 10031616 | tf_op jit(solution)/shard_map/skl,skd->sld/dot_general | solution.py:905
  177.0 5.5 %collective-permute-done.52.other = bf16[4,24,1536]{2,1,0:T(8,128)(2,1)S(1)} collective-permute-done((bf16[4,24,1536]{2,1,0:T(8,128)(2,1)S(1)}, bf16[4,24,1536]{2,1,0:T(8,128)(2,1)S(1)}, u32[]{:S(2)}, u32[]{:S(2)}) %collective-permute-start.52) | collective-permute-done | bytes 294944 | tf_op jit(solution)/shard_map/ppermute | solution.py:768
  183.2 1.5 collective-permute-start.53
  184.7 1.7 collective-permute-start.54
  187.1 2.0 collective-permute-done.54.other_l
  189.1 1.7 collective-permute-done.55.other_r
  191.2 11.1 %all_to_all.11 = f32[32,1,128]{2,1,0:T(1,128)S(1)} all-to-all(f32[32,1,128]{2,1,0:T(1,128)S(1)} %bitcast.73), channel_id=1, replica_groups=mesh['wide'=8,'narrow'=4] {'wide','narrow'}, dimensions={0} | all-to-all | bytes 32768 | tf_op jit(solution)/shard_map/all_to_all | solution.py:1012
  202.3 2.1 %update.1 = (f32[1,1]{1,0:T(1,128)}, f32[24,2304]{1,0:T(8,128)}, f32[24,2304]{1,0:T(8,128)}, f32[24,2304]{1,0:T(8,128)}, f32[24,768]{1,0:T(8,128)}, /*index=5*/f...) custom-call(f32[32,128]{1,0:T(8,128)S(1)} %bitcast.72, ...), custom_call_target="tpu_custom_call" | custom-call | flops 1 | bytes 1 | tf_op jit(solution)/shard_map/update/pallas_call | solution.py:55
  (213 shorter events, 42.7 us)
Async XLA Ops:
  1.8 11.3 %collective-permute-start = (bf16[24,3200]{1,0:T(8,128)(2,1)S(1)}, bf16[24,3200]{1,0:T(8,128)(2,1)S(1)}, u32[]{:S(2)}, u32[]{:S(2)}) collective-permute-start(bf16[24,3200]{1,0:T(8,128)(2,1)S(1)} %gather_input.1.refs_0_), channel_id=1, source_target_pairs={{0,1},{1,0},{2,3},{3,2},{4,5},{5,4},{6,7},{7,6},{8,9},{9,8},{10,11... | collective-permute-start | bytes 460808 | tf_op jit(solution)/shard_map/ppermute | solution.py:768
  4.8 14.4 %collective-permute-start.1 = (bf16[24,3200]{1,0:T(8,128)(2,1)S(1)}, bf16[24,3200]{1,0:T(8,128)(2,1)S(1)}, u32[]{:S(2)}, u32[]{:S(2)}) collective-permute-start(bf16[24,3200]{1,0:T(8,128)(2,1)S(1)} %gather_input.1.refs_0_), channel_id=1, source_target_pairs={{0,2},{1,3},{2,0},{3,1},{4,6},{5,7},{6,4},{7,5},{8,10},{9,11},{10,... | collective-permute-start | bytes 460808 | tf_op jit(solution)/shard_map/ppermute | solution.py:768
  7.4 11.8 %collective-permute-start.2 = (bf16[24,3200]{1,0:T(8,128)(2,1)S(1)}, bf16[24,3200]{1,0:T(8,128)(2,1)S(1)}, u32[]{:S(2)}, u32[]{:S(2)}) collective-permute-start(bf16[24,3200]{1,0:T(8,128)(2,1)S(1)} %gather_input.1.refs_0_), channel_id=1, source_target_pairs={{0,3},{1,2},{2,1},{3,0},{4,7},{5,6},{6,5},{7,4},{8,11},{9,10},{10,... | collective-permute-start | bytes 460808 | tf_op jit(solution)/shard_map/ppermute | solution.py:768
  19.4 12.1 %collective-permute-start.4 = (bf16[96,1664]{1,0:T(8,128)(2,1)S(1)}, bf16[96,1664]{1,0:T(8,128)(2,1)S(1)}, u32[]{:S(2)}, u32[]{:S(2)}) collective-permute-start(bf16[96,1664]{1,0:T(8,128)(2,1)S(1)} %get-tuple-element.254), channel_id=1, source_target_pairs={{0,16},{1,17},{2,18},{3,19},{4,20},{5,21},{6,22},{7,23},{8,24},{9,... | collective-permute-start | bytes 958472 | tf_op jit(solution)/shard_map/ppermute | solution.py:768
  21.0 10.5 %collective-permute-start.3 = (bf16[96,1536]{1,0:T(8,128)(2,1)S(1)}, bf16[96,1536]{1,0:T(8,128)(2,1)S(1)}, u32[]{:S(2)}, u32[]{:S(2)}) collective-permute-start(bf16[96,1536]{1,0:T(8,128)(2,1)S(1)} %get-tuple-element.253), channel_id=1, source_target_pairs={{0,8},{1,9},{2,10},{3,11},{4,12},{5,13},{6,14},{7,15},{8,0},{9,1},... | collective-permute-start | bytes 884744 | tf_op jit(solution)/shard_map/ppermute | solution.py:768
  22.5 8.9 %collective-permute-start.5 = (bf16[24,3072]{1,0:T(8,128)(2,1)S(1)}, bf16[24,3072]{1,0:T(8,128)(2,1)S(1)}, u32[]{:S(2)}, u32[]{:S(2)}) collective-permute-start(bf16[24,3072]{1,0:T(8,128)(2,1)S(1)} %convert_element_type.21.refs_0_), channel_id=1, source_target_pairs={{0,2},{1,3},{2,0},{3,1},{4,6},{5,7},{6,4},{7,5},{8,10},{9,11},{10,... | collective-permute-start | bytes 442376 | tf_op jit(solution)/shard_map/ppermute | solution.py:768
  26.0 4.4 %collective-permute-start.6 = (bf16[96,384]{1,0:T(8,128)(2,1)S(1)}, bf16[96,384]{1,0:T(8,128)(2,1)S(1)}, u32[]{:S(2)}, u32[]{:S(2)}) collective-permute-start(bf16[96,384]{1,0:T(8,128)(2,1)S(1)} %get-tuple-element.492.refs_0_), channel_id=1, source_target_pairs={{0,8},{1,9},{2,10},{3,11},{4,12},{5,13},{6,14},{7,15},{8,0},{9,1},... | collective-permute-start | bytes 221192 | tf_op jit(solution)/shard_map/ppermute | solution.py:768
  26.6 4.4 %collective-permute-start.7 = (bf16[96,384]{1,0:T(8,128)(2,1)S(1)}, bf16[96,384]{1,0:T(8,128)(2,1)S(1)}, u32[]{:S(2)}, u32[]{:S(2)}) collective-permute-start(bf16[96,384]{1,0:T(8,128)(2,1)S(1)} %get-tuple-element.491.refs_2_), channel_id=1, source_target_pairs={{0,16},{1,17},{2,18},{3,19},{4,20},{5,21},{6,22},{7,23},{8,24},{9,... | collective-permute-start | bytes 221192 | tf_op jit(solution)/shard_map/ppermute | solution.py:768
  31.6 16.9 %collective-permute-start.9 = (bf16[2,96,1664]{2,1,0:T(8,128)(2,1)S(1)}, bf16[2,96,1664]{2,1,0:T(8,128)(2,1)S(1)}, u32[]{:S(2)}, u32[]{:S(2)}) collective-permute-start(bf16[2,96,1664]{2,1,0:T(8,128)(2,1)S(1)} %pad_maximum_fusion.refs_1_), channel_id=1, source_target_pairs={{0,8},{1,9},{2,10},{3,11},{4,12},{5,13},{6,14},{7,15},{8,0},{9,1},... | collective-permute-start | bytes 1916936 | tf_op jit(solution)/shard_map/ppermute | solution.py:768
  32.6 15.9 %collective-permute-start.11 = (bf16[2,96,1664]{2,1,0:T(8,128)(2,1)S(1)}, bf16[2,96,1664]{2,1,0:T(8,128)(2,1)S(1)}, u32[]{:S(2)}, u32[]{:S(2)}) collective-permute-start(bf16[2,96,1664]{2,1,0:T(8,128)(2,1)S(1)} %pad_maximum_fusion.refs_1_), channel_id=1, source_target_pairs={{0,4},{1,5},{2,6},{3,7},{4,0},{5,1},{6,2},{7,3},{8,12},{9,13},{10,... | collective-permute-start | bytes 1916936 | tf_op jit(solution)/shard_map/ppermute | solution.py:768
  32.7 15.8 %collective-permute-start.8 = (bf16[2,96,1536]{2,1,0:T(8,128)(2,1)S(1)}, bf16[2,96,1536]{2,1,0:T(8,128)(2,1)S(1)}, u32[]{:S(2)}, u32[]{:S(2)}) collective-permute-start(bf16[2,96,1536]{2,1,0:T(8,128)(2,1)S(1)} %pad_maximum_fusion.1.refs_0_), channel_id=1, source_target_pairs={{0,16},{1,17},{2,18},{3,19},{4,20},{5,21},{6,22},{7,23},{8,24},{9,... | collective-permute-start | bytes 1769480 | tf_op jit(solution)/shard_map/ppermute | solution.py:768
  33.3 15.2 %collective-permute-start.10 = (bf16[2,96,1536]{2,1,0:T(8,128)(2,1)S(1)}, bf16[2,96,1536]{2,1,0:T(8,128)(2,1)S(1)}, u32[]{:S(2)}, u32[]{:S(2)}) collective-permute-start(bf16[2,96,1536]{2,1,0:T(8,128)(2,1)S(1)} %pad_maximum_fusion.1.refs_0_), channel_id=1, source_target_pairs={{0,4},{1,5},{2,6},{3,7},{4,0},{5,1},{6,2},{7,3},{8,12},{9,13},{10,... | collective-permute-start | bytes 1769480 | tf_op jit(solution)/shard_map/ppermute | solution.py:768
  33.5 9.3 %collective-permute-start.12 = (bf16[2,24,3072]{2,1,0:T(8,128)(2,1)S(1)}, bf16[2,24,3072]{2,1,0:T(8,128)(2,1)S(1)}, u32[]{:S(2)}, u32[]{:S(2)}) collective-permute-start(bf16[2,24,3072]{2,1,0:T(8,128)(2,1)S(1)} %pad_maximum_fusion.6), channel_id=1, source_target_pairs={{0,1},{1,0},{2,3},{3,2},{4,5},{5,4},{6,7},{7,6},{8,9},{9,8},{10,11... | collective-permute-start | bytes 884744 | tf_op jit(solution)/shard_map/ppermute | solution.py:768
  42.8 15.8 %collective-permute-start.17 = (bf16[4,96,384]{2,1,0:T(8,128)(2,1)S(1)}, bf16[4,96,384]{2,1,0:T(8,128)(2,1)S(1)}, u32[]{:S(2)}, u32[]{:S(2)}) collective-permute-start(bf16[4,96,384]{2,1,0:T(8,128)(2,1)S(1)} %get-tuple-element.486), channel_id=1, source_target_pairs={{0,2},{1,3},{2,0},{3,1},{4,6},{5,7},{6,4},{7,5},{8,10},{9,11},{10,... | collective-permute-start | bytes 884744 | tf_op jit(solution)/shard_map/ppermute | solution.py:768
  49.4 10.5 %collective-permute-start.13 = (bf16[2,96,1536]{2,1,0:T(8,128)(2,1)S(1)}, bf16[2,96,1536]{2,1,0:T(8,128)(2,1)S(1)}, u32[]{:S(2)}, u32[]{:S(2)}) collective-permute-start(bf16[2,96,1536]{2,1,0:T(8,128)(2,1)S(1)} %collective-permute-done.8.refs_2_), channel_id=1, source_target_pairs={{0,4},{1,5},{2,6},{3,7},{4,0},{5,1},{6,2},{7,3},{8,12},{9,13},{10,... | collective-permute-start | bytes 1769480 | tf_op jit(solution)/shard_map/ppermute | solution.py:768
  49.4 10.5 %collective-permute-start.14 = (bf16[2,96,1664]{2,1,0:T(8,128)(2,1)S(1)}, bf16[2,96,1664]{2,1,0:T(8,128)(2,1)S(1)}, u32[]{:S(2)}, u32[]{:S(2)}) collective-permute-start(bf16[2,96,1664]{2,1,0:T(8,128)(2,1)S(1)} %collective-permute-done.9.refs_3_), channel_id=1, source_target_pairs={{0,4},{1,5},{2,6},{3,7},{4,0},{5,1},{6,2},{7,3},{8,12},{9,13},{10,... | collective-permute-start | bytes 1916936 | tf_op jit(solution)/shard_map/ppermute | solution.py:768
  50.3 8.7 %collective-permute-start.15 = (bf16[96,1536]{1,0:T(8,128)(2,1)S(1)}, bf16[96,1536]{1,0:T(8,128)(2,1)S(1)}, u32[]{:S(2)}, u32[]{:S(2)}) collective-permute-start(bf16[96,1536]{1,0:T(8,128)(2,1)S(1)} %get-tuple-element.269), channel_id=1, source_target_pairs={{0,8},{1,9},{2,10},{3,11},{4,12},{5,13},{6,14},{7,15},{8,0},{9,1},... | collective-permute-start | bytes 884744 | tf_op jit(solution)/shard_map/ppermute | solution.py:768
  51.4 8.4 %collective-permute-start.16 = (bf16[96,1536]{1,0:T(8,128)(2,1)S(1)}, bf16[96,1536]{1,0:T(8,128)(2,1)S(1)}, u32[]{:S(2)}, u32[]{:S(2)}) collective-permute-start(bf16[96,1536]{1,0:T(8,128)(2,1)S(1)} %get-tuple-element.272), channel_id=1, source_target_pairs={{0,16},{1,17},{2,18},{3,19},{4,20},{5,21},{6,22},{7,23},{8,24},{9,... | collective-permute-start | bytes 884744 | tf_op jit(solution)/shard_map/ppermute | solution.py:768
  59.9 13.9 %collective-permute-start.18 = (bf16[2,96,1536]{2,1,0:T(8,128)(2,1)S(1)}, bf16[2,96,1536]{2,1,0:T(8,128)(2,1)}, u32[]{:S(2)}, u32[]{:S(2)}) collective-permute-start(bf16[2,96,1536]{2,1,0:T(8,128)(2,1)S(1)} %pad_maximum_fusion.2.refs_0_), channel_id=1, source_target_pairs={{0,16},{1,17},{2,18},{3,19},{4,20},{5,21},{6,22},{7,23},{8,24},{9,... | collective-permute-start | bytes 1769480 | tf_op jit(solution)/shard_map/ppermute | solution.py:768
  60.5 16.9 %collective-permute-start.20 = (bf16[2,96,1536]{2,1,0:T(8,128)(2,1)S(1)}, bf16[2,96,1536]{2,1,0:T(8,128)(2,1)}, u32[]{:S(2)}, u32[]{:S(2)}) collective-permute-start(bf16[2,96,1536]{2,1,0:T(8,128)(2,1)S(1)} %pad_maximum_fusion.2.refs_0_), channel_id=1, source_target_pairs={{0,4},{1,5},{2,6},{3,7},{4,0},{5,1},{6,2},{7,3},{8,12},{9,13},{10,... | collective-permute-start | bytes 1769480 | tf_op jit(solution)/shard_map/ppermute | solution.py:768
  61.3 16.1 %collective-permute-start.19 = (bf16[2,96,1536]{2,1,0:T(8,128)(2,1)}, bf16[2,96,1536]{2,1,0:T(8,128)(2,1)}, u32[]{:S(2)}, u32[]{:S(2)}) collective-permute-start(bf16[2,96,1536]{2,1,0:T(8,128)(2,1)} %pad_maximum_fusion.3.refs_1_), channel_id=1, source_target_pairs={{0,8},{1,9},{2,10},{3,11},{4,12},{5,13},{6,14},{7,15},{8,0},{9,1},... | collective-permute-start | bytes 1769480 | tf_op jit(solution)/shard_map/ppermute | solution.py:768
  62.3 15.1 %collective-permute-start.21 = (bf16[2,96,1536]{2,1,0:T(8,128)(2,1)}, bf16[2,96,1536]{2,1,0:T(8,128)(2,1)}, u32[]{:S(2)}, u32[]{:S(2)}) collective-permute-start(bf16[2,96,1536]{2,1,0:T(8,128)(2,1)} %pad_maximum_fusion.3.refs_1_), channel_id=1, source_target_pairs={{0,4},{1,5},{2,6},{3,7},{4,0},{5,1},{6,2},{7,3},{8,12},{9,13},{10,... | collective-permute-start | bytes 1769480 | tf_op jit(solution)/shard_map/ppermute | solution.py:768
  63.4 15.9 %collective-permute-start.22 = (bf16[2,4,96,384]{3,2,1,0:T(8,128)(2,1)}, bf16[2,4,96,384]{3,2,1,0:T(8,128)(2,1)}, u32[]{:S(2)}, u32[]{:S(2)}) collective-permute-start(bf16[2,4,96,384]{3,2,1,0:T(8,128)(2,1)} %pad_maximum_fusion.4), channel_id=1, source_target_pairs={{0,1},{1,0},{2,3},{3,2},{4,5},{5,4},{6,7},{7,6},{8,9},{9,8},{10,11... | collective-permute-start | bytes 1769480 | tf_op jit(solution)/shard_map/ppermute | solution.py:768
  79.3 5.6 %collective-permute-start.25 = (bf16[6,384,384]{2,1,0:T(8,128)(2,1)S(1)}, bf16[6,384,384]{2,1,0:T(8,128)(2,1)S(1)}, u32[]{:S(2)}, u32[]{:S(2)}) collective-permute-start(bf16[6,384,384]{2,1,0:T(8,128)(2,1)S(1)} %get-tuple-element.308), channel_id=1, source_target_pairs={{0,4},{1,5},{2,6},{3,7},{4,0},{5,1},{6,2},{7,3},{8,12},{9,13},{10,... | collective-permute-start | bytes 5308424 | tf_op jit(solution)/shard_map/ppermute | solution.py:768
  79.3 4.4 %collective-permute-start.23 = (bf16[2,96,1536]{2,1,0:T(8,128)(2,1)}, bf16[2,96,1536]{2,1,0:T(8,128)(2,1)S(1)}, u32[]{:S(2)}, u32[]{:S(2)}) collective-permute-start(bf16[2,96,1536]{2,1,0:T(8,128)(2,1)} %collective-permute-done.18.refs_2_), channel_id=1, source_target_pairs={{0,4},{1,5},{2,6},{3,7},{4,0},{5,1},{6,2},{7,3},{8,12},{9,13},{10,... | collective-permute-start | bytes 1769480 | tf_op jit(solution)/shard_map/ppermute | solution.py:768
  79.9 4.7 %collective-permute-start.24 = (bf16[2,96,1536]{2,1,0:T(8,128)(2,1)}, bf16[2,96,1536]{2,1,0:T(8,128)(2,1)S(1)}, u32[]{:S(2)}, u32[]{:S(2)}) collective-permute-start(bf16[2,96,1536]{2,1,0:T(8,128)(2,1)} %collective-permute-done.19.refs_3_), channel_id=1, source_target_pairs={{0,4},{1,5},{2,6},{3,7},{4,0},{5,1},{6,2},{7,3},{8,12},{9,13},{10,... | collective-permute-start | bytes 1769480 | tf_op jit(solution)/shard_map/ppermute | solution.py:768
  81.1 17.2 %collective-permute-start.28 = (bf16[2,384,384]{2,1,0:T(8,128)(2,1)S(1)}, bf16[2,384,384]{2,1,0:T(8,128)(2,1)S(1)}, u32[]{:S(2)}, u32[]{:S(2)}) collective-permute-start(bf16[2,384,384]{2,1,0:T(8,128)(2,1)S(1)} %get-tuple-element.328.refs_0_), channel_id=1, source_target_pairs={{0,16},{1,17},{2,18},{3,19},{4,20},{5,21},{6,22},{7,23},{8,24},{9,... | collective-permute-start | bytes 1769480 | tf_op jit(solution)/shard_map/ppermute | solution.py:768
  82.7 15.7 %collective-permute-start.29 = (bf16[2,384,384]{2,1,0:T(8,128)(2,1)S(1)}, bf16[2,384,384]{2,1,0:T(8,128)(2,1)S(1)}, u32[]{:S(2)}, u32[]{:S(2)}) collective-permute-start(bf16[2,384,384]{2,1,0:T(8,128)(2,1)S(1)} %get-tuple-element.329.refs_1_), channel_id=1, source_target_pairs={{0,8},{1,9},{2,10},{3,11},{4,12},{5,13},{6,14},{7,15},{8,0},{9,1},... | collective-permute-start | bytes 1769480 | tf_op jit(solution)/shard_map/ppermute | solution.py:768
  83.7 14.6 %collective-permute-start.30 = (bf16[2,384,384]{2,1,0:T(8,128)(2,1)S(1)}, bf16[2,384,384]{2,1,0:T(8,128)(2,1)S(1)}, u32[]{:S(2)}, u32[]{:S(2)}) collective-permute-start(bf16[2,384,384]{2,1,0:T(8,128)(2,1)S(1)} %get-tuple-element.328.refs_0_), channel_id=1, source_target_pairs={{0,4},{1,5},{2,6},{3,7},{4,0},{5,1},{6,2},{7,3},{8,12},{9,13},{10,... | collective-permute-start | bytes 1769480 | tf_op jit(solution)/shard_map/ppermute | solution.py:768
  84.6 13.8 %collective-permute-start.31 = (bf16[2,384,384]{2,1,0:T(8,128)(2,1)S(1)}, bf16[2,384,384]{2,1,0:T(8,128)(2,1)S(1)}, u32[]{:S(2)}, u32[]{:S(2)}) collective-permute-start(bf16[2,384,384]{2,1,0:T(8,128)(2,1)S(1)} %get-tuple-element.329.refs_1_), channel_id=1, source_target_pairs={{0,4},{1,5},{2,6},{3,7},{4,0},{5,1},{6,2},{7,3},{8,12},{9,13},{10,... | collective-permute-start | bytes 1769480 | tf_op jit(solution)/shard_map/ppermute | solution.py:768
  99.0 18.5 %collective-permute-start.26 = (bf16[2,384,384]{2,1,0:T(8,128)(2,1)S(1)}, bf16[2,384,384]{2,1,0:T(8,128)(2,1)S(1)}, u32[]{:S(2)}, u32[]{:S(2)}) collective-permute-start(bf16[2,384,384]{2,1,0:T(8,128)(2,1)S(1)} %get-tuple-element.324), channel_id=1, source_target_pairs={{0,16},{1,17},{2,18},{3,19},{4,20},{5,21},{6,22},{7,23},{8,24},{9,... | collective-permute-start | bytes 1769480 | tf_op jit(solution)/shard_map/ppermute | solution.py:768
  100.5 17.0 %collective-permute-start.27 = (bf16[2,384,384]{2,1,0:T(8,128)(2,1)S(1)}, bf16[2,384,384]{2,1,0:T(8,128)(2,1)S(1)}, u32[]{:S(2)}, u32[]{:S(2)}) collective-permute-start(bf16[2,384,384]{2,1,0:T(8,128)(2,1)S(1)} %get-tuple-element.325), channel_id=1, source_target_pairs={{0,8},{1,9},{2,10},{3,11},{4,12},{5,13},{6,14},{7,15},{8,0},{9,1},... | collective-permute-start | bytes 1769480 | tf_op jit(solution)/shard_map/ppermute | solution.py:768
  117.5 6.7 %collective-permute-start.34 = (bf16[384,3072]{1,0:T(8,128)(2,1)S(1)}, bf16[384,3072]{1,0:T(8,128)(2,1)S(1)}, u32[]{:S(2)}, u32[]{:S(2)}) collective-permute-start(bf16[384,3072]{1,0:T(8,128)(2,1)S(1)} %get-tuple-element.350.du_ref.refs_1_), channel_id=1, source_target_pairs={{0,4},{1,5},{2,6},{3,7},{4,0},{5,1},{6,2},{7,3},{8,12},{9,13},{10,... | collective-permute-start | bytes 7077896 | tf_op jit(solution)/shard_map/ppermute | solution.py:768
  124.2 12.5 %collective-permute-start.35 = (bf16[384,2304]{1,0:T(8,128)(2,1)S(1)}, bf16[384,2304]{1,0:T(8,128)(2,1)S(1)}, u32[]{:S(2)}, u32[]{:S(2)}) collective-permute-start(bf16[384,2304]{1,0:T(8,128)(2,1)S(1)} %unattend.1.dqkv_ref.refs_1_), channel_id=1, source_target_pairs={{0,4},{1,5},{2,6},{3,7},{4,0},{5,1},{6,2},{7,3},{8,12},{9,13},{10,... | collective-permute-start | bytes 5308424 | tf_op jit(solution)/shard_map/ppermute | solution.py:768
  124.7 8.3 %collective-permute-start.36 = (bf16[384,768]{1,0:T(8,128)(2,1)S(1)}, bf16[384,768]{1,0:T(8,128)(2,1)S(1)}, u32[]{:S(2)}, u32[]{:S(2)}) collective-permute-start(bf16[384,768]{1,0:T(8,128)(2,1)S(1)} %get-tuple-element.352.da_ref.refs_5_), channel_id=1, source_target_pairs={{0,4},{1,5},{2,6},{3,7},{4,0},{5,1},{6,2},{7,3},{8,12},{9,13},{10,... | collective-permute-start | bytes 1769480 | tf_op jit(solution)/shard_map/ppermute | solution.py:768
  127.8 15.7 %collective-permute-start.42 = (bf16[2,96,1536]{2,1,0:T(8,128)(2,1)S(1)}, bf16[2,96,1536]{2,1,0:T(8,128)(2,1)S(1)}, u32[]{:S(2)}, u32[]{:S(2)}) collective-permute-start(bf16[2,96,1536]{2,1,0:T(8,128)(2,1)S(1)} %get-tuple-element.391), channel_id=1, source_target_pairs={{0,16},{1,17},{2,18},{3,19},{4,20},{5,21},{6,22},{7,23},{8,24},{9,... | collective-permute-start | bytes 1769480 | tf_op jit(solution)/shard_map/ppermute | solution.py:768
  128.7 16.1 %collective-permute-start.43 = (bf16[2,96,1536]{2,1,0:T(8,128)(2,1)S(1)}, bf16[2,96,1536]{2,1,0:T(8,128)(2,1)S(1)}, u32[]{:S(2)}, u32[]{:S(2)}) collective-permute-start(bf16[2,96,1536]{2,1,0:T(8,128)(2,1)S(1)} %get-tuple-element.392), channel_id=1, source_target_pairs={{0,8},{1,9},{2,10},{3,11},{4,12},{5,13},{6,14},{7,15},{8,0},{9,1},... | collective-permute-start | bytes 1769480 | tf_op jit(solution)/shard_map/ppermute | solution.py:768
  129.7 15.1 %collective-permute-start.44 = (bf16[2,4,96,384]{3,2,1,0:T(8,128)(2,1)S(1)}, bf16[2,4,96,384]{3,2,1,0:T(8,128)(2,1)S(1)}, u32[]{:S(2)}, u32[]{:S(2)}) collective-permute-start(bf16[2,4,96,384]{3,2,1,0:T(8,128)(2,1)S(1)} %get-tuple-element.393), channel_id=1, source_target_pairs={{0,1},{1,0},{2,3},{3,2},{4,5},{5,4},{6,7},{7,6},{8,9},{9,8},{10,11... | collective-permute-start | bytes 1769480 | tf_op jit(solution)/shard_map/ppermute | solution.py:768
  139.9 17.6 %collective-permute-start.41 = (bf16[2,96,1664]{2,1,0:T(8,128)(2,1)S(1)}, bf16[2,96,1664]{2,1,0:T(8,128)(2,1)S(1)}, u32[]{:S(2)}, u32[]{:S(2)}) collective-permute-start(bf16[2,96,1664]{2,1,0:T(8,128)(2,1)S(1)} %get-tuple-element.388), channel_id=1, source_target_pairs={{0,8},{1,9},{2,10},{3,11},{4,12},{5,13},{6,14},{7,15},{8,0},{9,1},... | collective-permute-start | bytes 1916936 | tf_op jit(solution)/shard_map/ppermute | solution.py:768
  141.0 15.2 %collective-permute-start.40 = (bf16[2,96,1536]{2,1,0:T(8,128)(2,1)S(1)}, bf16[2,96,1536]{2,1,0:T(8,128)(2,1)S(1)}, u32[]{:S(2)}, u32[]{:S(2)}) collective-permute-start(bf16[2,96,1536]{2,1,0:T(8,128)(2,1)S(1)} %get-tuple-element.387), channel_id=1, source_target_pairs={{0,16},{1,17},{2,18},{3,19},{4,20},{5,21},{6,22},{7,23},{8,24},{9,... | collective-permute-start | bytes 1769480 | tf_op jit(solution)/shard_map/ppermute | solution.py:768
  145.3 20.2 %collective-permute-start.47 = (bf16[2,4,24,1536]{3,2,1,0:T(8,128)(2,1)S(1)}, bf16[2,4,24,1536]{3,2,1,0:T(8,128)(2,1)S(1)}, u32[]{:S(2)}, u32[]{:S(2)}) collective-permute-start(bf16[2,4,24,1536]{3,2,1,0:T(8,128)(2,1)S(1)} %get-tuple-element.418), channel_id=1, source_target_pairs={{0,1},{1,0},{2,3},{3,2},{4,5},{5,4},{6,7},{7,6},{8,9},{9,8},{10,11... | collective-permute-start | bytes 1769480 | tf_op jit(solution)/shard_map/ppermute | solution.py:768
  146.9 17.9 %collective-permute-start.48 = (bf16[4,96,384]{2,1,0:T(8,128)(2,1)S(1)}, bf16[4,96,384]{2,1,0:T(8,128)(2,1)S(1)}, u32[]{:S(2)}, u32[]{:S(2)}) collective-permute-start(bf16[4,96,384]{2,1,0:T(8,128)(2,1)S(1)} %get-tuple-element.419), channel_id=1, source_target_pairs={{0,2},{1,3},{2,0},{3,1},{4,6},{5,7},{6,4},{7,5},{8,10},{9,11},{10,... | collective-permute-start | bytes 884744 | tf_op jit(solution)/shard_map/ppermute | solution.py:768
  157.8 13.2 %collective-permute-start.46 = (bf16[96,1664]{1,0:T(8,128)(2,1)S(1)}, bf16[96,1664]{1,0:T(8,128)(2,1)S(1)}, u32[]{:S(2)}, u32[]{:S(2)}) collective-permute-start(bf16[96,1664]{1,0:T(8,128)(2,1)S(1)} %get-tuple-element.416), channel_id=1, source_target_pairs={{0,16},{1,17},{2,18},{3,19},{4,20},{5,21},{6,22},{7,23},{8,24},{9,... | collective-permute-start | bytes 958472 | tf_op jit(solution)/shard_map/ppermute | solution.py:768
  159.3 11.7 %collective-permute-start.45 = (bf16[96,1536]{1,0:T(8,128)(2,1)S(1)}, bf16[96,1536]{1,0:T(8,128)(2,1)S(1)}, u32[]{:S(2)}, u32[]{:S(2)}) collective-permute-start(bf16[96,1536]{1,0:T(8,128)(2,1)S(1)} %get-tuple-element.415), channel_id=1, source_target_pairs={{0,8},{1,9},{2,10},{3,11},{4,12},{5,13},{6,14},{7,15},{8,0},{9,1},... | collective-permute-start | bytes 884744 | tf_op jit(solution)/shard_map/ppermute | solution.py:768
  165.8 4.6 %collective-permute-start.49 = (bf16[96,384]{1,0:T(8,128)(2,1)S(1)}, bf16[96,384]{1,0:T(8,128)(2,1)S(1)}, u32[]{:S(2)}, u32[]{:S(2)}) collective-permute-start(bf16[96,384]{1,0:T(8,128)(2,1)S(1)} %get-tuple-element.428), channel_id=1, source_target_pairs={{0,8},{1,9},{2,10},{3,11},{4,12},{5,13},{6,14},{7,15},{8,0},{9,1},... | collective-permute-start | bytes 221192 | tf_op jit(solution)/shard_map/ppermute | solution.py:768
  168.5 14.0 %collective-permute-start.52 = (bf16[4,24,1536]{2,1,0:T(8,128)(2,1)S(1)}, bf16[4,24,1536]{2,1,0:T(8,128)(2,1)S(1)}, u32[]{:S(2)}, u32[]{:S(2)}) collective-permute-start(bf16[4,24,1536]{2,1,0:T(8,128)(2,1)S(1)} %get-tuple-element.437), channel_id=1, source_target_pairs={{0,2},{1,3},{2,0},{3,1},{4,6},{5,7},{6,4},{7,5},{8,10},{9,11},{10,... | collective-permute-start | bytes 884744 | tf_op jit(solution)/shard_map/ppermute | solution.py:768
  171.2 11.7 %collective-permute-start.51 = (bf16[2,24,3200]{2,1,0:T(8,128)(2,1)S(1)}, bf16[2,24,3200]{2,1,0:T(8,128)(2,1)S(1)}, u32[]{:S(2)}, u32[]{:S(2)}) collective-permute-start(bf16[2,24,3200]{2,1,0:T(8,128)(2,1)S(1)} %get-tuple-element.436), channel_id=1, source_target_pairs={{0,1},{1,0},{2,3},{3,2},{4,5},{5,4},{6,7},{7,6},{8,9},{9,8},{10,11... | collective-permute-start | bytes 921608 | tf_op jit(solution)/shard_map/ppermute | solution.py:768
  183.2 7.5 %collective-permute-start.53 = (bf16[24,3200]{1,0:T(8,128)(2,1)S(1)}, bf16[24,3200]{1,0:T(8,128)(2,1)S(1)}, u32[]{:S(2)}, u32[]{:S(2)}) collective-permute-start(bf16[24,3200]{1,0:T(8,128)(2,1)S(1)} %get-tuple-element.446), channel_id=1, source_target_pairs={{0,2},{1,3},{2,0},{3,1},{4,6},{5,7},{6,4},{7,5},{8,10},{9,11},{10,... | collective-permute-start | bytes 460808 | tf_op jit(solution)/shard_map/ppermute | solution.py:768
  (55 other events, 536.9 us)
